TPU v7x, 32 devices: a whole 2x2x4 slice. The times are simulated.
32 devices in a mesh: seq: 8 (over z, x), tp: 4 (over y, core).
Axes of the slice: x: 2, y: 2, z: 4, core: 2. Of those that a mesh axis runs over, the one named last changes fastest.
Arguments:
- tokens: bfloat16 [4, 16, 5120], P(None, None, 'seq'), may hold values from -32 to 32
- attn_gain: bfloat16 [5120], P('seq'), may hold values from 0.099609375 to 1.8984375
- w_query: bfloat16 [5120, 4096], P('seq', 'tp'), may hold values from -0.078125 to 0.078125
- w_key: bfloat16 [5120, 1024], P('seq', 'tp'), may hold values from -0.078125 to 0.078125
- w_value: bfloat16 [5120, 1024], P('seq', 'tp'), may hold values from -0.078125 to 0.078125
- w_out: bfloat16 [4096, 5120], P('tp', 'seq'), may hold values from -0.09375 to 0.09375
- ffn_gain: bfloat16 [5120], replicated, may hold values from 0.099609375 to 1.8984375
- w_gate: bfloat16 [5120, 32768], P(None, ('seq', 'tp')), may hold values from -0.078125 to 0.078125
- w_up: bfloat16 [5120, 32768], P(None, ('seq', 'tp')), may hold values from -0.078125 to 0.078125
- w_down: bfloat16 [32768, 5120], P(('seq', 'tp')), may hold values from -0.0625 to 0.0625
- key_cache: bfloat16 [16, 1024, 8, 128], P(None, 'seq', 'tp'), may hold values from -96 to 96
- value_cache: bfloat16 [16, 1024, 8, 128], P(None, 'seq', 'tp'), may hold values from -48 to 48
- lengths: int32 [16], replicated, may hold values from 1 to 1020, as said below
Outputs:
- hidden_out: bfloat16 [4, 16, 5120], P(None, None, 'seq')
- keys_out: bfloat16 [16, 1024, 8, 128], P(None, 'seq', 'tp')
- values_out: bfloat16 [16, 1024, 8, 128], P(None, 'seq', 'tp')
Inputs may be any that keep to these rules, and one draw needn't show every extreme that they name: `lengths`: some request's length is exactly 1020.
All inputs are finite; a program needn't handle non-finite values.
Results may differ from a plain program's by a relative error of at most 0.012.
The roundings to bfloat16 on the way count: a program that leaves them out, or rounds other values in their place, can miss the bound.
Values may be sent and summed in bfloat16 or wider, within the bound.
No kernel may reach another device: no remote copies, remote signals or barrier semaphores. Data moves between devices by JAX's collectives and lax.ppermute only.
A program may use at most 128 MiB of HBM per device.

v0:
```python
import math

import jax
import jax.numpy as jnp
from jax import lax
from jax.sharding import PartitionSpec as P

D = 5120
STEPS = 4


def rotate(vectors, position):
    half = vectors.shape[-1] // 2
    freqs = jnp.exp(
        jnp.arange(half, dtype=jnp.float32) * (-2.0 * math.log(100000000.0) / vectors.shape[-1])
    )
    angles = position.astype(jnp.float32)[:, None] * freqs[None, :]
    cosine = jnp.cos(angles)[:, None, :]
    sine = jnp.sin(angles)[:, None, :]
    first = vectors[..., :half]
    second = vectors[..., half:]
    return jnp.concatenate(
        [first * cosine - second * sine, second * cosine + first * sine], axis=-1
    )


def per_device(
    tokens,
    attn_gain,
    w_query,
    w_key,
    w_value,
    w_out,
    ffn_gain,
    w_gate,
    w_up,
    w_down,
    key_cache,
    value_cache,
    lengths,
):
    requests = lengths.shape[0]
    span = key_cache.shape[1]
    kv_local = key_cache.shape[2]
    head_dim = key_cache.shape[3]
    local_width = tokens.shape[2]
    heads_local = w_query.shape[1] // head_dim
    group = heads_local // kv_local
    seq_index = lax.axis_index("seq")
    first_slot = seq_index * span
    first_col = seq_index * local_width
    req_index = jnp.arange(requests)
    slot_pos = first_slot + jnp.arange(span)
    results = []
    for step in range(STEPS):
        residual = tokens[step].astype(jnp.float32)
        squares = jnp.sum(residual * residual, axis=1)
        normed = (residual * attn_gain.astype(jnp.float32)).astype(jnp.bfloat16)
        part_query = jnp.dot(normed, w_query, preferred_element_type=jnp.float32)
        part_key = jnp.dot(normed, w_key, preferred_element_type=jnp.float32)
        part_value = jnp.dot(normed, w_value, preferred_element_type=jnp.float32)
        total_in = lax.psum(squares, "seq")
        part_query, part_key, part_value = lax.psum((part_query, part_key, part_value), "seq")
        scale_in = lax.rsqrt(total_in / D + 1e-05)[:, None]
        position = lengths + step
        query = rotate(
            (part_query * scale_in).reshape(requests, heads_local, head_dim), position
        ).astype(jnp.bfloat16)
        key_new = rotate(
            (part_key * scale_in).reshape(requests, kv_local, head_dim), position
        ).astype(jnp.bfloat16)
        value_new = (
            (part_value * scale_in).reshape(requests, kv_local, head_dim).astype(jnp.bfloat16)
        )
        local_slot = position - first_slot
        owned = (local_slot >= 0) & (local_slot < span)
        target = jnp.where(owned, local_slot, span)
        key_cache = key_cache.at[req_index, target].set(key_new, mode="drop")
        value_cache = value_cache.at[req_index, target].set(value_new, mode="drop")
        grouped = query.reshape(requests, kv_local, group, head_dim)
        scores = jnp.einsum(
            "rgjd,rpgd->rgjp", grouped, key_cache, preferred_element_type=jnp.float32
        ) * head_dim ** (-0.5)
        live = (slot_pos[None, :] <= position[:, None])[:, None, None, :]
        masked = jnp.where(live, scores, -1e30)
        local_top = jnp.max(masked, axis=3)
        expo = jnp.where(live, jnp.exp(masked - local_top[..., None]), 0.0)
        local_total = jnp.sum(expo, axis=3)
        local_out = jnp.einsum(
            "rgjp,rpgd->rgjd",
            expo.astype(jnp.bfloat16),
            value_cache,
            preferred_element_type=jnp.float32,
        )
        global_top = lax.pmax(local_top, "seq")
        factor = jnp.exp(local_top - global_top)
        denom, summed = lax.psum((local_total * factor, local_out * factor[..., None]), "seq")
        attended = (
            (summed / denom[..., None])
            .astype(jnp.bfloat16)
            .reshape(requests, heads_local * head_dim)
        )
        projected = jnp.dot(attended, w_out, preferred_element_type=jnp.float32)
        mixed = residual + lax.psum(projected, "tp")
        own_gain = lax.dynamic_slice_in_dim(ffn_gain, first_col, local_width, 0).astype(jnp.float32)
        ffn_in = (mixed * own_gain).astype(jnp.bfloat16)
        total_mid = lax.psum(jnp.sum(mixed * mixed, axis=1), "seq")
        piece = lax.all_gather(ffn_in, "seq", axis=1, tiled=True)
        gate_raw = jnp.dot(piece, w_gate, preferred_element_type=jnp.float32)
        up_raw = jnp.dot(piece, w_up, preferred_element_type=jnp.float32)
        scale_mid = lax.rsqrt(total_mid / D + 1e-05)[:, None]
        hidden = (jax.nn.silu(gate_raw * scale_mid) * (up_raw * scale_mid)).astype(jnp.bfloat16)
        whole = lax.psum(jnp.dot(hidden, w_down, preferred_element_type=jnp.float32), ("seq", "tp"))
        ffn_part = lax.dynamic_slice_in_dim(whole, first_col, local_width, 1)
        results.append((mixed + ffn_part).astype(jnp.bfloat16))
    return (jnp.stack(results), key_cache, value_cache)


def solution(mesh):
    placed = (
        P(None, None, "seq"),
        P("seq"),
        P("seq", "tp"),
        P("seq", "tp"),
        P("seq", "tp"),
        P("tp", "seq"),
        P(),
        P(None, ("seq", "tp")),
        P(None, ("seq", "tp")),
        P(("seq", "tp"), None),
        P(None, "seq", "tp", None),
        P(None, "seq", "tp", None),
        P(),
    )
    return jax.shard_map(
        per_device,
        mesh=mesh,
        in_specs=placed,
        out_specs=(P(None, None, "seq"), P(None, "seq", "tp", None), P(None, "seq", "tp", None)),
        check_vma=False,
    )
```

profile of v0, /device:TPU:0, one launch (start us, length us, event | category | flops | bytes accessed | tf_op | source)
XLA Modules:
  0.0 813.6 jit_solution(5473151882080552711)
XLA Ops:
  7.3 3.1 copy.85
  30.3 38.8 %all-reduce.5 = (f32[16]{0:T(128)S(1)}, f32[16,256]{1,0:T(8,128)S(1)}) all-reduce(f32[16]{0:T(128)S(1)} %fusion.53, f32[16,256]{1,0:T(8,128)S(1)} %fusion.120), channel_id=1, replica_groups=mesh['seq'=8,'tp'=4] {'seq'}, use_global_device_ids=true, to_apply=%region_2.0 | all-reduce | flops 4112 | bytes 32896 | tf_op jit(solution)/shard_map/psum | solution.py:62
  73.1 14.1 %all-reduce.16.cloned.1.call-done = f32[16,1024]{1,0:T(8,128)} async-done(((f32[16,1024]{1,0:T(8,128)}), f32[16,1024]{1,0:T(8,128)}) %all-reduce.16.cloned.1.call-update) | async-done | bytes 65552 | tf_op jit(solution)/shard_map/psum | solution.py:63
  90.2 36.1 %pmax.28 = f32[16,2,4]{2,1,0:T(2,128)S(1)} all-reduce(f32[16,2,4]{2,1,0:T(2,128)S(1)} %get-tuple-element.108), channel_id=1, replica_groups=mesh['seq'=8,'tp'=4] {'seq'}, use_global_device_ids=true, to_apply=%region_8.9 | all-reduce | flops 128 | bytes 1024 | tf_op jit(solution)/shard_map/pmax | solution.py:95
  126.6 33.1 %all-reduce.4 = (f32[16,256]{1,0:T(8,128)S(1)}, f32[16,2,4]{2,1,0:T(2,128)S(1)}) all-reduce(f32[16,256]{1,0:T(8,128)S(1)} %fusion.118, f32[16,2,4]{2,1,0:T(2,128)S(1)} %bitcast.198), channel_id=1, replica_groups=mesh['seq'=8,'tp'=4] {'seq'}, use_global_device_ids=true, to_apply=%region_6.7 | all-reduce | flops 4224 | bytes 33792 | tf_op jit(solution)/shard_map/psum | solution.py:63
  165.7 67.8 %all-reduce.22.cloned.1.call-done = (f32[16,2,4,128]{3,2,1,0:T(4,128)}, f32[16,1024]{1,0:T(8,128)}, f32[16,1024]{1,0:T(8,128)}, f32[16,1024]{1,0:T(8,128)}) async-done(((f32[16,2,4,128]{3,2,1,0:T(4,128)}, f32[16,1024]{1,0:T(8,128)}, f32[16,1024]{1,0:T(8,128)}, f32[16,1024]{1,0:T(8,128)}), (f32[16,2,4,128]{3,2,1,0:T(4,128)}, f32[16,1024]{1,0:T(8,128)}, f32[16,1024]{1,0:T(8,128)}, ...) | async-done | bytes 262160 | tf_op jit(solution)/shard_map/psum | solution.py:97
  234.8 10.5 %psum.258 = f32[16,640]{1,0:T(8,128)S(1)} all-reduce(f32[16,640]{1,0:T(8,128)S(1)} %fusion.172), channel_id=1, replica_groups=mesh['seq'=8,'tp'=4] {'tp'}, use_global_device_ids=true, to_apply=%region_12.13 | all-reduce | flops 10240 | bytes 81920 | tf_op jit(solution)/shard_map/psum | solution.py:104
  246.0 36.2 %all-reduce.3 = (f32[16]{0:T(128)S(1)}, f32[16]{0:T(128)S(1)}, f32[16]{0:T(128)S(1)}, f32[16,256]{1,0:T(8,128)S(1)}, f32[16,256]{1,0:T(8,128)S(1)}, /*index=5*/f32[16,256]{1,0:T(8,128)S(1)}) all-reduce(f32[16]{0:T(128)S(1)} %get-tuple-element.4, f32[16]{0:T(128)S(1)} %get-tuple-element.5, ...), channel_id=1, replica_groups=mesh['seq'=8,'tp'=4] {'seq'}, use_global_device_ids=true, to_apply=%region_18.19 | all-reduce | flops 12336 | bytes 98688 | tf_op jit(solution)/shard_map/psum | solution.py:62
  302.0 33.4 %all-reduce.8 = (f32[16,2,4]{2,1,0:T(2,128)S(1)}, f32[16,2,4]{2,1,0:T(2,128)S(1)}, f32[16,2,4]{2,1,0:T(2,128)S(1)}) all-reduce(f32[16,2,4]{2,1,0:T(2,128)S(1)} %get-tuple-element.110, f32[16,2,4]{2,1,0:T(2,128)S(1)} %get-tuple-element.112, f32[16,2,4]{2,1,0:T(2,128)S(1)} %get-tuple-element.114), channel_id=1, replica_groups=mesh['seq'=8,'tp'=4] {'seq'}, use_global_device_ids=true, to_apply=%region_56.57 | all-reduce | flops 384 | bytes 3072 | tf_op jit(solution)/shard_map/pmax | solution.py:95
  335.8 35.9 %all-reduce.2 = (f32[16,256]{1,0:T(8,128)S(1)}, f32[16,256]{1,0:T(8,128)S(1)}, f32[16,256]{1,0:T(8,128)S(1)}, f32[16,2,4]{2,1,0:T(2,128)S(1)}, f32[16,2,4]{2,1,0:T(2,128)S(1)}, /*index=5*/f32[16,2,4]{2,1,0:T(2,128)S(1)}) all-reduce(f32[16,256]{1,0:T(8,128)S(1)} %fusion.112, ...), channel_id=1, replica_groups=mesh['seq'=8,'tp'=4] {'seq'}, use_global_device_ids=true, to_apply=%region_22.23 | all-reduce | flops 12672 | bytes 101376 | tf_op jit(solution)/shard_map/psum | solution.py:63
  387.1 68.3 %all-reduce.20.cloned.1.call-done = (f32[16,2,4,128]{3,2,1,0:T(4,128)}, f32[16,2,4,128]{3,2,1,0:T(4,128)}, f32[16,2,4,128]{3,2,1,0:T(4,128)}) async-done(((f32[16,2,4,128]{3,2,1,0:T(4,128)}, f32[16,2,4,128]{3,2,1,0:T(4,128)}, f32[16,2,4,128]{3,2,1,0:T(4,128)}), (f32[16,2,4,128]{3,2,1,0:T(4,128)}, f32[16,2,4,128]{3,2,1,0:T(4,128)}, f32[16,2,4,128]{3,2,1,0:T(4,128)})) %all-reduce.20.cloned.1.call-update) | async-done | bytes 196624 | tf_op jit(solution)/shard_map/psum | solution.py:97
  463.2 32.6 %all_gather.12 = bf16[16,5120]{1,0:T(8,128)(2,1)} all-gather(bf16[16,640]{1,0:T(8,128)(2,1)S(1)} %get-tuple-element.55), channel_id=1, replica_groups=mesh['seq'=8,'tp'=4] {'seq'}, dimensions={1}, use_global_device_ids=true | all-gather | bytes 184320 | tf_op jit(solution)/shard_map/all_gather | solution.py:108
  497.9 20.2 %all-reduce.1 = (f32[16]{0:T(128)}, f32[16]{0:T(128)}, f32[16]{0:T(128)}, f32[16]{0:T(128)}) all-reduce(f32[16]{0:T(128)} %get-tuple-element.9, f32[16]{0:T(128)} %get-tuple-element.8, f32[16]{0:T(128)} %get-tuple-element.7, f32[16]{0:T(128)} %get-tuple-element.3), channel_id=1, replica_groups=mesh['seq'=8,'tp'=4] {'seq'}, use_global_device_ids=true, to_apply=%region_62.63 | all-reduce | flops 64 | bytes 512 | tf_op jit(solution)/shard_map/psum | solution.py:107
  521.3 30.8 %all_gather.13 = bf16[16,5120]{1,0:T(8,128)(2,1)S(1)} all-gather(bf16[16,640]{1,0:T(8,128)(2,1)} %get-tuple-element.56), channel_id=1, replica_groups=mesh['seq'=8,'tp'=4] {'seq'}, dimensions={1}, use_global_device_ids=true | all-gather | bytes 184320 | tf_op jit(solution)/shard_map/all_gather | solution.py:108
  552.1 31.0 %all_gather.14 = bf16[16,5120]{1,0:T(8,128)(2,1)S(1)} all-gather(bf16[16,640]{1,0:T(8,128)(2,1)} %get-tuple-element.57), channel_id=1, replica_groups=mesh['seq'=8,'tp'=4] {'seq'}, dimensions={1}, use_global_device_ids=true | all-gather | bytes 184320 | tf_op jit(solution)/shard_map/all_gather | solution.py:108
  583.1 6.2 convolution_multiply_fusion.9
  591.7 10.6 %fusion.22 = f32[16,5120]{1,0:T(8,128)} fusion(bf16[1024,5120]{1,0:T(8,128)(2,1)} %param.22, bf16[16,5120]{1,0:T(8,128)(2,1)} %copy-done.7, bf16[5120,1024]{1,0:T(8,128)(2,1)} %param.21, f32[16,1024]{1,0:T(8,128)} %convolution_multiply_fusion.9, f32[16]{0:T(128)} %copy-done.19), kind=kOutput, calls=%fused_computation.46 | convolution fusion | flops 335659008 | bytes 21528640 | tf_op jit(solution)/shard_map/dot_general | solution.py:113
  602.4 10.5 %fusion.21 = f32[16,5120]{1,0:T(8,128)} fusion(bf16[1024,5120]{1,0:T(8,128)(2,1)} %param.22, bf16[16,5120]{1,0:T(8,128)(2,1)S(1)} %copy-done.6, bf16[5120,1024]{1,0:T(8,128)(2,1)} %param.21, f32[16,1024]{1,0:T(8,128)S(1)} %copy-done.8, f32[16]{0:T(128)S(1)} %copy-done.18), kind=kOutput, calls=%fused_computation.45 | convolution fusion | flops 335659008 | bytes 21528640 | tf_op jit(solution)/shard_map/dot_general | solution.py:113
  612.9 30.8 %all_gather.15 = bf16[16,5120]{1,0:T(8,128)(2,1)S(1)} all-gather(bf16[16,640]{1,0:T(8,128)(2,1)S(1)} %get-tuple-element.58), channel_id=1, replica_groups=mesh['seq'=8,'tp'=4] {'seq'}, dimensions={1}, use_global_device_ids=true | all-gather | bytes 184320 | tf_op jit(solution)/shard_map/all_gather | solution.py:108
  643.8 5.4 convolution_multiply_fusion.1
  649.2 10.6 %fusion.20 = f32[16,5120]{1,0:T(8,128)} fusion(bf16[1024,5120]{1,0:T(8,128)(2,1)} %param.22, bf16[16,5120]{1,0:T(8,128)(2,1)S(1)} %all_gather.15, bf16[5120,1024]{1,0:T(8,128)(2,1)} %param.21, f32[16,1024]{1,0:T(8,128)S(1)} %convolution_multiply_fusion.1, f32[16]{0:T(128)S(1)} %add_rsqrt_fusion), kind=kOutput, calls=%fused_computation.44 | convolution fusion | flops 335659008 | bytes 21528640 | tf_op jit(solution)/shard_map/dot_general | solution.py:113
  659.8 5.4 convolution_multiply_fusion.13
  665.2 10.5 %fusion.23 = f32[16,5120]{1,0:T(8,128)} fusion(bf16[1024,5120]{1,0:T(8,128)(2,1)} %param.22, bf16[16,5120]{1,0:T(8,128)(2,1)S(1)} %copy-done.4, bf16[5120,1024]{1,0:T(8,128)(2,1)} %param.21, f32[16,1024]{1,0:T(8,128)S(1)} %convolution_multiply_fusion.13, f32[16]{0:T(128)S(1)} %copy-done.16), kind=kOutput, calls=%fused_computation.47 | convolution fusion | flops 335659008 | bytes 21528640 | tf_op jit(solution)/shard_map/dot_general | solution.py:113
  675.8 129.3 %all-reduce.18.cloned.1.call-done = (f32[16,5120]{1,0:T(8,128)}, f32[16,5120]{1,0:T(8,128)}, f32[16,5120]{1,0:T(8,128)}, f32[16,5120]{1,0:T(8,128)}) async-done(((f32[16,5120]{1,0:T(8,128)}, f32[16,5120]{1,0:T(8,128)}, f32[16,5120]{1,0:T(8,128)}, f32[16,5120]{1,0:T(8,128)}), (f32[16,5120]{1,0:T(8,128)}, f32[16,5120]{1,0:T(8,128)}, f32[16,5120]{1,0:T(8,128)}, ...) | async-done | bytes 1310736 | tf_op jit(solution)/shard_map/psum | solution.py:113
  (163 shorter events, 87.4 us)
Async XLA Ops:
  7.2 22.2 %copy-start.3 = (bf16[4,16,640]{2,1,0:T(8,128)(2,1)S(1)}, bf16[4,16,640]{2,1,0:T(8,128)(2,1)}, u32[]{:S(2)}) copy-start(bf16[4,16,640]{2,1,0:T(8,128)(2,1)} %param.13) | copy-start | bytes 245764
  7.2 158.4 %copy-start.2 = (bf16[640,256]{1,0:T(8,128)(2,1)S(1)}, bf16[640,256]{1,0:T(8,128)(2,1)}, u32[]{:S(2)}) copy-start(bf16[640,256]{1,0:T(8,128)(2,1)} %param.17) | copy-start | bytes 983044
  7.2 227.3 %copy-start.1 = (bf16[1024,640]{1,0:T(8,128)(2,1)S(1)}, bf16[1024,640]{1,0:T(8,128)(2,1)}, u32[]{:S(2)}) copy-start(bf16[1024,640]{1,0:T(8,128)(2,1)} %param.18) | copy-start | bytes 3932164
  7.2 62.3 %copy-start.15 = (s32[16]{0:T(128)S(1)}, s32[16]{0:T(128)}, u32[]{:S(2)}) copy-start(s32[16]{0:T(128)} %param.25) | copy-start | bytes 196
  7.2 80.0 %all-reduce.16.cloned.1.call-start = ((), (), s32[]{:S(2)}) async-start(), calls=%async_computation | async-start | bytes 131072 | tf_op jit(solution)/shard_map/psum | solution.py:63
  15.7 217.8 %all-reduce.22.cloned.1.call-start = ((), (), s32[]{:S(2)}) async-start(), calls=%async_computation.3 | async-start | bytes 524288 | tf_op jit(solution)/shard_map/psum | solution.py:97
  159.6 175.9 %copy-start.12 = (pred[16,128]{1,0:T(8,128)(4,1)S(1)}, pred[16,128]{1,0:T(8,128)(4,1)}, u32[]{:S(2)}) copy-start(pred[16,128]{1,0:T(8,128)(4,1)} %get-tuple-element.89) | copy-start | bytes 6148
  159.6 215.0 %copy-start.14 = (pred[16,128]{1,0:T(8,128)(4,1)S(1)}, pred[16,128]{1,0:T(8,128)(4,1)}, u32[]{:S(2)}) copy-start(pred[16,128]{1,0:T(8,128)(4,1)} %get-tuple-element.88) | copy-start | bytes 6148
  159.6 220.0 %copy-start.13 = (pred[16,128]{1,0:T(8,128)(4,1)S(1)}, pred[16,128]{1,0:T(8,128)(4,1)}, u32[]{:S(2)}) copy-start(pred[16,128]{1,0:T(8,128)(4,1)} %get-tuple-element.87) | copy-start | bytes 6148
  164.8 290.6 %all-reduce.20.cloned.1.call-start = ((), (), s32[]{:S(2)}) async-start(), calls=%async_computation.2 | async-start | bytes 393216 | tf_op jit(solution)/shard_map/psum | solution.py:97
  387.0 108.8 %all-reduce.24.cloned.1.call-start = ((), (), s32[]{:S(2)}) async-start(), calls=%async_computation.4 | async-start | bytes 245760 | tf_op jit(solution)/shard_map/psum | solution.py:104
  460.7 128.6 %slice-start = ((s8[10485760]{0:T(1024)(128)(4,1)}), s8[2097152]{0:T(1024)(128)(4,1)S(1)}, s32[]{:S(2)}) async-start(s8[10485760]{0:T(1024)(128)(4,1)} %bitcast.184), calls=%async_computation.5 | async-start | bytes 4194304
  463.1 342.0 %all-reduce.18.cloned.1.call-start = ((), (), s32[]{:S(2)}) async-start(), calls=%async_computation.1 | async-start | bytes 2621440 | tf_op jit(solution)/shard_map/psum | solution.py:113
  519.4 70.0 %copy-start.17 = (f32[16]{0:T(128)}, f32[16]{0:T(128)S(1)}, u32[]{:S(2)}) copy-start(f32[16]{0:T(128)S(1)} %add_rsqrt_fusion.2) | copy-start | bytes 196
  520.1 69.3 %copy-start.19 = (f32[16]{0:T(128)}, f32[16]{0:T(128)S(1)}, u32[]{:S(2)}) copy-start(f32[16]{0:T(128)S(1)} %add_rsqrt_fusion.4) | copy-start | bytes 196
  552.1 37.3 %copy-start.7 = (bf16[16,5120]{1,0:T(8,128)(2,1)}, bf16[16,5120]{1,0:T(8,128)(2,1)S(1)}, u32[]{:S(2)}) copy-start(bf16[16,5120]{1,0:T(8,128)(2,1)S(1)} %all_gather.13) | copy-start | bytes 491524
  591.7 10.6 %copy-start.6 = (bf16[16,5120]{1,0:T(8,128)(2,1)S(1)}, bf16[16,5120]{1,0:T(8,128)(2,1)}, u32[]{:S(2)}) copy-start(bf16[16,5120]{1,0:T(8,128)(2,1)} %copy-done.5) | copy-start | bytes 491524
  591.7 10.6 %copy-start.8 = (f32[16,1024]{1,0:T(8,128)S(1)}, f32[16,1024]{1,0:T(8,128)}, u32[]{:S(2)}) copy-start(f32[16,1024]{1,0:T(8,128)} %convolution_multiply_fusion.5) | copy-start | bytes 196612
  591.7 10.6 %copy-start.18 = (f32[16]{0:T(128)S(1)}, f32[16]{0:T(128)}, u32[]{:S(2)}) copy-start(f32[16]{0:T(128)} %copy-done.17) | copy-start | bytes 196
  649.2 10.6 %copy-start.4 = (bf16[16,5120]{1,0:T(8,128)(2,1)S(1)}, bf16[16,5120]{1,0:T(8,128)(2,1)}, u32[]{:S(2)}) copy-start(bf16[16,5120]{1,0:T(8,128)(2,1)} %all_gather.12) | copy-start | bytes 491524
  649.2 10.6 %copy-start.16 = (f32[16]{0:T(128)S(1)}, f32[16]{0:T(128)}, u32[]{:S(2)}) copy-start(f32[16]{0:T(128)} %add_rsqrt_fusion.6) | copy-start | bytes 196
  665.2 139.9 %copy-start.9 = (f32[16,640]{1,0:T(8,128)S(1)}, f32[16,640]{1,0:T(8,128)}, u32[]{:S(2)}) copy-start(f32[16,640]{1,0:T(8,128)} %get-tuple-element.44) | copy-start | bytes 122884
  665.2 139.9 %copy-start.10 = (f32[16,640]{1,0:T(8,128)S(1)}, f32[16,640]{1,0:T(8,128)}, u32[]{:S(2)}) copy-start(f32[16,640]{1,0:T(8,128)} %get-tuple-element.45) | copy-start | bytes 122884
  665.2 139.9 %copy-start.11 = (f32[16,640]{1,0:T(8,128)S(1)}, f32[16,640]{1,0:T(8,128)}, u32[]{:S(2)}) copy-start(f32[16,640]{1,0:T(8,128)} %get-tuple-element.46) | copy-start | bytes 122884
  (4 other events, 25.9 us)
Sparse Core Ops, SparseCore 0:
  15.8 71.3 all-reduce.15
  164.9 68.5 all-reduce.21
  387.1 68.2 all-reduce.19
  463.3 29.9 all-reduce.23
  675.9 129.1 all-reduce.17
where the time goes:
time: 820 us; the launch traced here: 814 us
  blocking collectives  369 us (45%)
  waiting for transfers between devices  280 us (34%)
  matrix products  97.2 us (12%)
  local copies, waits for them, and re-layouts  29.2 us (4%)
  other arithmetic  23.3 us (3%)
  between operations  14.7 us (2%)
    psum x2, waiting for transfers between devices, per_device(): lax.psum((local_total * factor, local_out * factor[..., None]), 'seq')  136 us
    psum x1, waiting for transfers between devices, per_device(): lax.psum(jnp.dot(hidden, w_down, preferred_element_type=jnp.float32), ('s...  129 us
    all_gather x4, blocking collectives, per_device(): piece = lax.all_gather(ffn_in, 'seq', axis=1, tiled=True)  125 us
    psum x2, blocking collectives, per_device(): total_in = lax.psum(squares, 'seq')  75 us
    pmax x2, blocking collectives, per_device(): global_top = lax.pmax(local_top, 'seq')  69.6 us
    psum x2, blocking collectives, per_device(): lax.psum((part_query, part_key, part_value), 'seq')  68.9 us
    dot_general x4, matrix products, per_device(): jnp.dot(hidden, w_down, preferred_element_type=jnp.float32)  42.3 us
    psum x1, blocking collectives, per_device(): total_mid = lax.psum(jnp.sum(mixed * mixed, axis=1), 'seq')  20.2 us
  transfers between devices with their start and end apart: 5, of which 4 were waited for; matrix products, arithmetic and copies ran while one was open for 2% of the time, Pallas kernels for 0%

commit v1 on v0

v1 whole, which is shorter than its diff:
```python
import functools
import math

import jax
import jax.numpy as jnp
from jax import lax
from jax.experimental import pallas as pl
from jax.experimental.pallas import tpu as pltpu
from jax.sharding import PartitionSpec as P

F32 = jnp.float32
BF16 = jnp.bfloat16
LANES = 128
VMEM = pl.BlockSpec(memory_space=pltpu.VMEM)
SMEM = pl.BlockSpec(memory_space=pltpu.SMEM)


def call(body, outs, ins, scratch=(), limit=16):
    return pl.pallas_call(
        body,
        out_shape=outs,
        in_specs=ins,
        out_specs=[VMEM] * len(outs),
        scratch_shapes=list(scratch),
        compiler_params=pltpu.CompilerParams(vmem_limit_bytes=limit << 20),
    )


def sds(shape, dtype):
    return jax.ShapeDtypeStruct(shape, dtype)


def lane_ids(rows):
    return lax.broadcasted_iota(jnp.int32, (rows, LANES), 1)


def split3(value):
    high = value.astype(BF16)
    rest = value - high.astype(F32)
    mid = rest.astype(BF16)
    low = (rest - mid.astype(F32)).astype(BF16)
    return high, mid, low


def pack_stats(stats):
    high, mid, low = (part.astype(F32) for part in split3(stats))
    return (high + pltpu.roll(mid, 8, 1) + pltpu.roll(low, 16, 1)).astype(BF16)


def unpack_stats(packed):
    packed = packed.astype(F32)
    return (packed + pltpu.roll(packed, LANES - 8, 1)) + pltpu.roll(packed, LANES - 16, 1)


def project_kernel(x_ref, gain_ref, wq_ref, wk_ref, wv_ref, acc_ref, msg_ref):
    x = x_ref[...].astype(F32)
    normed = (x * gain_ref[...].astype(F32)).astype(BF16)
    squares = jnp.sum(x * x, axis=1, keepdims=True)
    at = 0
    for w_ref in (wq_ref, wk_ref, wv_ref):
        width = w_ref.shape[1]
        part = jnp.dot(normed, w_ref[...], preferred_element_type=F32)
        acc_ref[:, at : at + width] = part
        msg_ref[:, at : at + width] = part.astype(BF16)
        at += width
    stats = jnp.where(lane_ids(x.shape[0]) == 0, squares, 0.0)
    acc_ref[:, at:] = stats
    msg_ref[:, at:] = pack_stats(stats)


def add_kernel(acc_ref, recv_ref, out_ref, msg_ref):
    at = acc_ref.shape[1] - LANES
    total = acc_ref[:, :at] + recv_ref[:, :at].astype(F32)
    out_ref[:, :at] = total
    msg_ref[:, :at] = total.astype(BF16)
    stats = acc_ref[:, at:] + unpack_stats(recv_ref[:, at:])
    stats = jnp.where(lane_ids(stats.shape[0]) == 0, stats, 0.0)
    out_ref[:, at:] = stats
    msg_ref[:, at:] = pack_stats(stats)


def attend_kernel(
    heads,
    kv,
    steps,
    features,
    slot_ref,
    len_ref,
    acc_ref,
    recv_ref,
    cos_ref,
    sin_ref,
    k_ref,
    v_ref,
    k_out,
    v_out,
    o_ref,
    st_ref,
    msg_ref,
    q_buf,
    kn_buf,
    vn_buf,
    o_buf,
    m_buf,
    l_buf,
):
    requests, rows_kv, hd = k_ref.shape
    rows = requests * steps
    group = heads // kv
    block = steps * heads
    fresh = steps * kv
    at = (heads + 2 * kv) * hd
    squares = acc_ref[:, at:] + unpack_stats(recv_ref[:, at:])
    scale = lax.rsqrt(squares[:, 0:1] / features + 1e-05)

    def vector(index):
        cols = slice(index * hd, (index + 1) * hd)
        return (acc_ref[:, cols] + recv_ref[:, cols].astype(F32)) * scale

    def rotated(value):
        return value * cos_ref[...] + pltpu.roll(value, hd // 2, 1) * sin_ref[...]

    def spread(buf, value, index, per_step):
        for t in range(steps):
            buf[pl.ds(t * per_step + index, requests, stride=steps * per_step), :] = value[
                t * requests : (t + 1) * requests
            ]

    for h in range(heads):
        spread(q_buf, rotated(vector(h)), h, heads)
    for g in range(kv):
        spread(kn_buf, rotated(vector(heads + g)), g, kv)
        spread(vn_buf, vector(heads + kv + g), g, kv)

    row = lax.broadcasted_iota(jnp.int32, (block, rows_kv), 0)
    col = lax.broadcasted_iota(jnp.int32, (block, rows_kv), 1)
    same = (row % heads) // group == col % kv
    need = jnp.where(same, col // kv - row // heads, 1 << 29)
    place = lax.broadcasted_iota(jnp.int32, (rows_kv, fresh), 0) - lax.broadcasted_iota(
        jnp.int32, (rows_kv, fresh), 1
    )
    line = lax.broadcasted_iota(jnp.int32, (rows_kv, hd), 0)
    first = slot_ref[0]
    for r in range(requests):
        start = len_ref[r] - first
        base = start * kv
        pick = jnp.where(place == base, 1.0, 0.0).astype(BF16)
        new = (line >= base) & (line < base + fresh)

        def renewed(cache_ref, buf):
            news = buf[r * fresh : (r + 1) * fresh, :].astype(BF16)
            put = jnp.dot(pick, news, preferred_element_type=F32)
            return jnp.where(new, put, cache_ref[r].astype(F32)).astype(BF16)

        keys = renewed(k_ref, kn_buf)
        values = renewed(v_ref, vn_buf)
        k_out[r] = keys
        v_out[r] = values
        query = q_buf[r * block : (r + 1) * block, :].astype(BF16)
        scores = lax.dot_general(
            query, keys, (((1,), (1,)), ((), ())), preferred_element_type=F32
        ) * hd ** (-0.5)
        live = need <= start
        masked = jnp.where(live, scores, -1e30)
        top = jnp.max(masked, axis=1, keepdims=True)
        expo = jnp.where(live, jnp.exp(masked - top), 0.0)
        total = jnp.sum(expo, axis=1, keepdims=True)
        o_buf[r * block : (r + 1) * block, :] = jnp.dot(
            expo.astype(BF16), values, preferred_element_type=F32
        )
        m_buf[r * block : (r + 1) * block, :] = jnp.broadcast_to(top, (block, hd))
        l_buf[r * block : (r + 1) * block, :] = jnp.broadcast_to(total, (block, hd))

    lane = lane_ids(requests)
    for t in range(steps):
        mine = slice(t * requests, (t + 1) * requests)
        stats = jnp.zeros((requests, LANES), F32)
        for h in range(heads):
            take = pl.ds(t * heads + h, requests, stride=block)
            value = o_buf[take, :]
            o_ref[mine, h * hd : (h + 1) * hd] = value
            msg_ref[mine, h * hd : (h + 1) * hd] = value.astype(BF16)
            stats = jnp.where(lane == h, m_buf[take, :], stats)
            stats = jnp.where(lane == 24 + h, l_buf[take, :], stats)
        st_ref[mine, :] = stats
        msg_ref[mine, heads * hd :] = pack_stats(stats)


def merged(heads, o_ref, st_ref, recv_ref):
    hd = o_ref.shape[1] // heads
    mine = st_ref[...]
    theirs = unpack_stats(recv_ref[:, heads * hd :])
    top = jnp.maximum(mine, theirs)
    keep, take = jnp.exp(mine - top), jnp.exp(theirs - top)
    total = mine * pltpu.roll(keep, 24, 1) + theirs * pltpu.roll(take, 24, 1)
    lane = lane_ids(mine.shape[0])
    stats = jnp.where(lane < heads, top, jnp.where((lane >= 24) & (lane < 24 + heads), total, 0.0))

    def head(h):
        cols = slice(h * hd, (h + 1) * hd)
        return o_ref[:, cols] * keep[:, h : h + 1] + recv_ref[:, cols].astype(F32) * take[:, h : h + 1]

    return stats, head


def merge_kernel(heads, o_ref, st_ref, recv_ref, o_out, st_out, msg_out):
    stats, head = merged(heads, o_ref, st_ref, recv_ref)
    hd = o_ref.shape[1] // heads
    for h in range(heads):
        value = head(h)
        o_out[:, h * hd : (h + 1) * hd] = value
        msg_out[:, h * hd : (h + 1) * hd] = value.astype(BF16)
    st_out[...] = stats
    msg_out[:, heads * hd :] = pack_stats(stats)


def finish_kernel(heads, core_ref, o_ref, st_ref, recv_ref, w_ref, mine_ref, other_ref, att_buf):
    stats, head = merged(heads, o_ref, st_ref, recv_ref)
    hd = o_ref.shape[1] // heads
    for h in range(heads):
        att_buf[:, h * hd : (h + 1) * hd] = (head(h) / stats[:, 24 + h : 25 + h]).astype(BF16)
    part = jnp.dot(att_buf[...], w_ref[...], preferred_element_type=F32)
    half = part.shape[0] // 2
    low = core_ref[0] == 0
    mine_ref[...] = jnp.where(low, part[:half], part[half:])
    other_ref[...] = jnp.where(low, part[half:], part[:half])


def hidden_kernel(masks, features, seq_ref, own_ref, far_ref, wg_ref, wu_ref, h_ref):
    count, half, width = own_ref.shape
    width -= LANES
    seq = seq_ref[0]
    squares = []
    for ref in (own_ref, far_ref):
        total = jnp.zeros((half, LANES), F32)
        for j in range(count):
            total += unpack_stats(ref[j, :, :LANES])
        squares.append(total)
    scale = lax.rsqrt(jnp.concatenate(squares, axis=0)[:, 0:1] / features + 1e-05)
    gate = jnp.zeros((2 * half, wg_ref.shape[1]), F32)
    up = jnp.zeros((2 * half, wu_ref.shape[1]), F32)
    for j, mask in enumerate(masks):
        rows = pl.ds(pl.multiple_of((seq ^ mask) * width, 16), width)
        x = jnp.concatenate([own_ref[j, :, LANES:], far_ref[j, :, LANES:]], axis=0)
        gate += jnp.dot(x, wg_ref[rows, :], preferred_element_type=F32)
        up += jnp.dot(x, wu_ref[rows, :], preferred_element_type=F32)
    gate = gate * scale
    up = up * scale
    h_ref[...] = (gate / (1.0 + jnp.exp(-gate)) * up).astype(BF16)


def down_kernel(masks, width, seq_ref, h_ref, w_ref, own_ref, far_ref):
    seq = seq_ref[0]
    half = h_ref.shape[0] // 2
    hidden = h_ref[...]
    for j, mask in enumerate(masks):
        cols = pl.ds(pl.multiple_of((seq ^ mask) * width, LANES), width)
        part = jnp.dot(hidden, w_ref[:, cols], preferred_element_type=F32)
        own_ref[j] = part[:half]
        far_ref[j] = part[half:].astype(BF16)


def per_device(
    n_seq,
    n_tp,
    tokens,
    attn_gain,
    w_query,
    w_key,
    w_value,
    w_out,
    ffn_gain,
    w_gate,
    w_up,
    w_down,
    key_cache,
    value_cache,
    lengths,
):
    steps, requests, width = tokens.shape
    span, kv, hd = key_cache.shape[1:]
    heads = w_query.shape[1] // hd
    rows = steps * requests
    half = rows // 2
    features = width * n_seq
    wide = w_query.shape[1] + w_key.shape[1] + w_value.shape[1] + LANES
    seq = lax.axis_index("seq")
    tp = lax.axis_index("tp")
    seq_bits = [1 << b for b in range(n_seq.bit_length() - 1)]
    masks = [0]
    for bit in reversed(seq_bits):
        masks = masks + [m ^ bit for m in masks]

    def hop(value, axis, bit):
        size = n_seq if axis == "seq" else n_tp
        return lax.ppermute(value, axis, [(i, i ^ bit) for i in range(size)])

    x = tokens.reshape(rows, width)
    core = (tp & 1).astype(jnp.int32)
    seq_arr = seq.astype(jnp.int32).reshape(1)
    core_arr = core.reshape(1)

    positions = (lengths[None, :] + jnp.arange(steps, dtype=jnp.int32)[:, None]).reshape(rows)
    freqs = jnp.exp(jnp.arange(hd // 2, dtype=F32) * (-2.0 * math.log(100000000.0) / hd))
    angles = positions.astype(F32)[:, None] * freqs[None, :]
    cosine, sine = jnp.cos(angles), jnp.sin(angles)
    cosine = jnp.concatenate([cosine, cosine], axis=1)
    sine = jnp.concatenate([-sine, sine], axis=1)

    with jax.named_scope("project"):
        acc, msg = call(
            project_kernel, [sds((rows, wide), F32), sds((rows, wide), BF16)], [VMEM] * 5
        )(x, attn_gain.reshape(1, width), w_query, w_key, w_value)
        for bit in seq_bits[:-1]:
            acc, msg = call(
                add_kernel, [sds((rows, wide), F32), sds((rows, wide), BF16)], [VMEM] * 2
            )(acc, hop(msg, "seq", bit))
        recv = hop(msg, "seq", seq_bits[-1])

    with jax.named_scope("attend"):
        rows_kv = span * kv
        flat = (requests, rows_kv, hd)
        block = steps * heads
        joint = [
            sds((rows, heads * hd), F32),
            sds((rows, LANES), F32),
            sds((rows, heads * hd + LANES), BF16),
        ]
        keys, values, o, st, msg = call(
            functools.partial(attend_kernel, heads, kv, steps, features),
            [sds(flat, BF16), sds(flat, BF16)] + joint,
            [SMEM, SMEM] + [VMEM] * 6,
            [
                pltpu.VMEM((requests * block, hd), F32),
                pltpu.VMEM((requests * steps * kv, hd), F32),
                pltpu.VMEM((requests * steps * kv, hd), F32),
                pltpu.VMEM((requests * block, hd), F32),
                pltpu.VMEM((requests * block, hd), F32),
                pltpu.VMEM((requests * block, hd), F32),
            ],
        )(
            seq_arr * span,
            lengths,
            acc,
            recv,
            cosine,
            sine,
            key_cache.reshape(flat),
            value_cache.reshape(flat),
        )
        for bit in seq_bits[:-1]:
            o, st, msg = call(functools.partial(merge_kernel, heads), joint, [VMEM] * 3)(
                o, st, hop(msg, "seq", bit)
            )
        recv = hop(msg, "seq", seq_bits[-1])

    with jax.named_scope("mix"):
        mine, other = call(
            functools.partial(finish_kernel, heads),
            [sds((half, width), F32)] * 2,
            [SMEM] + [VMEM] * 4,
            [pltpu.VMEM((rows, heads * hd), BF16)],
        )(core_arr, o, st, recv, w_out)
        part = mine + hop(other, "tp", 1)
        for bit in [1 << b for b in range(1, n_tp.bit_length() - 1)]:
            sent = lax.reduce_precision(part, 8, 7)
            part = sent + hop(sent.astype(BF16), "tp", bit).astype(F32)
        own_x = lax.dynamic_slice_in_dim(x, core * half, half, 0).astype(F32)
        mixed = own_x + part
        gain = lax.dynamic_slice_in_dim(ffn_gain, seq * width, width, 0).astype(F32)
        ffn_in = (mixed * gain).astype(BF16)
        squares = jnp.sum(mixed * mixed, axis=1, keepdims=True)
        high = lax.reduce_precision(squares, 8, 7)
        mid = lax.reduce_precision(squares - high, 8, 7)
        low = squares - high - mid
        lane = lane_ids(half)
        stats = jnp.where(lane == 0, high, jnp.where(lane == 8, mid, jnp.where(lane == 16, low, 0.0)))
        pieces = jnp.concatenate([stats.astype(BF16), ffn_in], axis=1)[None]
        for bit in reversed(seq_bits):
            pieces = jnp.concatenate([pieces, hop(pieces, "seq", bit)], axis=0)
        far = hop(pieces, "tp", 1)

    with jax.named_scope("ffn"):
        (hidden,) = call(
            functools.partial(hidden_kernel, masks, features),
            [sds((rows, w_gate.shape[1]), BF16)],
            [SMEM] + [VMEM] * 4,
        )(seq_arr, pieces, far, w_gate, w_up)
        shape = (n_seq, half, width)
        if width % LANES == 0:
            own, far = call(
                functools.partial(down_kernel, masks, width),
                [sds(shape, F32), sds(shape, BF16)],
                [SMEM] + [VMEM] * 2,
            )(seq_arr, hidden, w_down)
        else:
            whole = jnp.dot(hidden, w_down, preferred_element_type=F32)
            whole = whole.reshape(rows, n_seq, width).transpose(1, 0, 2)
            whole = jnp.take(whole, seq ^ jnp.array(masks, jnp.int32), axis=0)
            own, far = whole[:, :half], whole[:, half:].astype(BF16)
        total = own + hop(far, "tp", 1).astype(F32)
        for bit in seq_bits:
            count = total.shape[0] // 2
            total = total[:count] + hop(total[count:].astype(BF16), "seq", bit).astype(F32)
        part = total[0]
        for bit in [1 << b for b in range(1, n_tp.bit_length() - 1)]:
            sent = lax.reduce_precision(part, 8, 7)
            part = sent + hop(sent.astype(BF16), "tp", bit).astype(F32)
        own = (mixed + part).astype(BF16)
        far = hop(own, "tp", 1)
        first, second = jnp.where(core == 0, own, far), jnp.where(core == 0, far, own)
        result = jnp.concatenate([first, second], axis=0).reshape(steps, requests, width)
    return result, keys.reshape(key_cache.shape), values.reshape(value_cache.shape)


def solution(mesh):
    placed = (
        P(None, None, "seq"),
        P("seq"),
        P("seq", "tp"),
        P("seq", "tp"),
        P("seq", "tp"),
        P("tp", "seq"),
        P(),
        P(None, ("seq", "tp")),
        P(None, ("seq", "tp")),
        P(("seq", "tp"), None),
        P(None, "seq", "tp", None),
        P(None, "seq", "tp", None),
        P(),
    )
    return jax.shard_map(
        functools.partial(per_device, mesh.shape["seq"], mesh.shape["tp"]),
        mesh=mesh,
        in_specs=placed,
        out_specs=(P(None, None, "seq"), P(None, "seq", "tp", None), P(None, "seq", "tp", None)),
        check_vma=False,
    )
```

time: 820 us -> 123 us (0.15)
  blocking collectives: 369 us -> 0 us
  waiting for transfers between devices: 280 us -> 69.1 us
  matrix products: 97.2 us -> 0 us
  other arithmetic: 23.3 us -> 3.63 us
  starting transfers between devices: 0.21 us -> 18.5 us
  between operations: 14.7 us -> 0.82 us
  Pallas kernels: 0 us -> 13.3 us
  local copies, waits for them, and re-layouts: 29.2 us -> 17.5 us
    psum x5 -> x0, waiting for transfers between devices: 280 us -> none  [the longest x2 136 us: per_device(): lax.psum((local_total * factor, local_out * factor[..., None]), 'seq')]
    psum x6 -> x0, blocking collectives: 175 us -> none  [the longest x2 75 us: per_device(): total_in = lax.psum(squares, 'seq')]
    all_gather x4 -> x0, blocking collectives: 125 us -> none  [per_device(): piece = lax.all_gather(ffn_in, 'seq', axis=1, tiled=True)]
    dot_general x32 -> x0, matrix products: 97.2 us -> none  [the longest x4 42.3 us: per_device(): jnp.dot(hidden, w_down, preferred_element_type=jnp.float32)]
    pmax x2 -> x0, blocking collectives: 69.6 us -> none  [per_device(): global_top = lax.pmax(local_top, 'seq')]
    ppermute x0 -> x18, waiting for transfers between devices: none -> 69.1 us  [hop(): return lax.ppermute(value, axis, [(i, i ^ bit) for i in range(size)])]
    scatter x8 -> x0, local copies, waits for them, and re-layouts: 21.9 us -> none  [the longest x4 11 us: per_device(): key_cache = key_cache.at[req_index, target].set(key_new, mode='drop')]
    ppermute x0 -> x18, starting transfers between devices: none -> 18.5 us  [hop(): return lax.ppermute(value, axis, [(i, i ^ bit) for i in range(size)])]
  transfers between devices with their start and end apart: 5 -> 18, of which waited for: 4 -> 18; matrix products, arithmetic and copies ran while one was open for 2% -> 1% of each run, Pallas kernels for 0% -> 0%
where the time goes in v1:
time: 123 us
  waiting for transfers between devices  69.1 us (56%)
  starting transfers between devices  18.5 us (15%)
  local copies, waits for them, and re-layouts  17.5 us (14%)
  Pallas kernels  13.3 us (11%)
  other arithmetic  3.63 us (3%)
    ppermute x18, waiting for transfers between devices, hop(): return lax.ppermute(value, axis, [(i, i ^ bit) for i in range(size)])  69.1 us
    ppermute x18, starting transfers between devices, hop(): return lax.ppermute(value, axis, [(i, i ^ bit) for i in range(size)])  18.5 us
    unnamed x22, local copies, waits for them, and re-layouts  16.7 us
    pallas_call x1, Pallas kernels, per_device(): call(functools.partial(attend_kernel, heads, kv, steps, features), [sds(f...  5.06 us
    pallas_call x1, Pallas kernels, per_device(): call(functools.partial(hidden_kernel, masks, features), [sds((rows, w_gat...  3.81 us
  transfers between devices with their start and end apart: 18, of which 18 were waited for; matrix products, arithmetic and copies ran while one was open for 1% of the time, Pallas kernels for 0%

profile of v1, /device:TPU:0, one launch (start us, length us, event | category | flops | bytes accessed | tf_op | source)
XLA Modules:
  0.0 122.8 jit_solution(7231747070233969949)
XLA Ops:
  5.9 3.0 %collective-permute-start = (bf16[64,1664]{1,0:T(8,128)(2,1)S(1)}, bf16[64,1664]{1,0:T(8,128)(2,1)S(1)}, u32[]{:S(2)}, u32[]{:S(2)}) collective-permute-start(bf16[64,1664]{1,0:T(8,128)(2,1)S(1)} %get-tuple-element.25), channel_id=1, source_target_pairs={{0,4},{4,0},{8,12},{12,8},{16,20},{20,16},{24,28},{28,24},{1,5},{5... | collective-permute-start | bytes 638984 | tf_op jit(solution)/shard_map/project/ppermute | solution.py:296
  8.9 5.2 %collective-permute-done.recv_ref = bf16[64,1664]{1,0:T(8,128)(2,1)S(1)} collective-permute-done((bf16[64,1664]{1,0:T(8,128)(2,1)S(1)}, bf16[64,1664]{1,0:T(8,128)(2,1)S(1)}, u32[]{:S(2)}, u32[]{:S(2)}) %collective-permute-start) | collective-permute-done | bytes 213024 | tf_op jit(solution)/shard_map/project/ppermute | solution.py:296
  14.4 1.9 %collective-permute-start.1 = (bf16[64,1664]{1,0:T(8,128)(2,1)S(1)}, bf16[64,1664]{1,0:T(8,128)(2,1)S(1)}, u32[]{:S(2)}, u32[]{:S(2)}) collective-permute-start(bf16[64,1664]{1,0:T(8,128)(2,1)S(1)} %get-tuple-element.27), channel_id=1, source_target_pairs={{0,8},{4,12},{8,0},{12,4},{16,24},{20,28},{24,16},{28,20},{1,9},{5... | collective-permute-start | bytes 638984 | tf_op jit(solution)/shard_map/project/ppermute | solution.py:296
  17.0 3.8 %collective-permute-done.1.recv_ref = bf16[64,1664]{1,0:T(8,128)(2,1)S(1)} collective-permute-done((bf16[64,1664]{1,0:T(8,128)(2,1)S(1)}, bf16[64,1664]{1,0:T(8,128)(2,1)S(1)}, u32[]{:S(2)}, u32[]{:S(2)}) %collective-permute-start.1) | collective-permute-done | bytes 213024 | tf_op jit(solution)/shard_map/project/ppermute | solution.py:296
  21.1 2.6 %collective-permute-start.2 = (bf16[64,1664]{1,0:T(8,128)(2,1)S(1)}, bf16[64,1664]{1,0:T(8,128)(2,1)S(1)}, u32[]{:S(2)}, u32[]{:S(2)}) collective-permute-start(bf16[64,1664]{1,0:T(8,128)(2,1)S(1)} %get-tuple-element.29), channel_id=1, source_target_pairs={{0,16},{4,20},{8,24},{12,28},{16,0},{20,4},{24,8},{28,12},{1,17},{... | collective-permute-start | bytes 638984 | tf_op jit(solution)/shard_map/project/ppermute | solution.py:296
  24.0 8.1 %collective-permute-done.2.recv_ref = bf16[64,1664]{1,0:T(8,128)(2,1)S(1)} collective-permute-done((bf16[64,1664]{1,0:T(8,128)(2,1)S(1)}, bf16[64,1664]{1,0:T(8,128)(2,1)S(1)}, u32[]{:S(2)}, u32[]{:S(2)}) %collective-permute-start.2) | collective-permute-done | bytes 213024 | tf_op jit(solution)/shard_map/project/ppermute | solution.py:296
  35.2 5.1 %attend.3 = (bf16[16,256,128]{2,1,0:T(8,128)(2,1)}, bf16[16,256,128]{2,1,0:T(8,128)(2,1)}, f32[64,1024]{1,0:T(8,128)S(1)}, f32[64,128]{1,0:T(8,128)S(1)}, bf16[64,1152]{1,0:T(8,128)(2,1)S(1)}) custom-call(s32[1]{0:T(128)S(6)} %mul.44.slot_ref, s32[16]{0:T(128)S(1)} %copy-done.10, f32[64,1664]{1,0:T(8,128)S(1)} %get-tuple-element.28.acc_ref, ...), custom_call_target="tpu_custom_call" | custom-call | tf_op jit(solution)/shard_map/attend/pallas_call | solution.py:329
  41.4 4.0 %collective-permute-done.3.recv_ref = bf16[64,1152]{1,0:T(8,128)(2,1)S(1)} collective-permute-done((bf16[64,1152]{1,0:T(8,128)(2,1)S(1)}, bf16[64,1152]{1,0:T(8,128)(2,1)S(1)}, u32[]{:S(2)}, u32[]{:S(2)}) %collective-permute-start.3) | collective-permute-done | bytes 147488 | tf_op jit(solution)/shard_map/attend/ppermute | solution.py:296
  46.1 4.8 %collective-permute-done.4.recv_ref = bf16[64,1152]{1,0:T(8,128)(2,1)S(1)} collective-permute-done((bf16[64,1152]{1,0:T(8,128)(2,1)S(1)}, bf16[64,1152]{1,0:T(8,128)(2,1)S(1)}, u32[]{:S(2)}, u32[]{:S(2)}) %collective-permute-start.4) | collective-permute-done | bytes 147488 | tf_op jit(solution)/shard_map/attend/ppermute | solution.py:296
  51.3 1.7 %collective-permute-start.5 = (bf16[64,1152]{1,0:T(8,128)(2,1)S(1)}, bf16[64,1152]{1,0:T(8,128)(2,1)S(1)}, u32[]{:S(2)}, u32[]{:S(2)}) collective-permute-start(bf16[64,1152]{1,0:T(8,128)(2,1)S(1)} %get-tuple-element.38), channel_id=1, source_target_pairs={{0,16},{4,20},{8,24},{12,28},{16,0},{20,4},{24,8},{28,12},{1,17},{... | collective-permute-start | bytes 442376 | tf_op jit(solution)/shard_map/attend/ppermute | solution.py:296
  53.8 5.2 %collective-permute-done.5.recv_ref = bf16[64,1152]{1,0:T(8,128)(2,1)S(1)} collective-permute-done((bf16[64,1152]{1,0:T(8,128)(2,1)S(1)}, bf16[64,1152]{1,0:T(8,128)(2,1)S(1)}, u32[]{:S(2)}, u32[]{:S(2)}) %collective-permute-start.5) | collective-permute-done | bytes 147488 | tf_op jit(solution)/shard_map/attend/ppermute | solution.py:296
  63.5 2.8 %collective-permute-done.7 = bf16[32,640]{1,0:T(8,128)(2,1)S(1)} collective-permute-done((bf16[32,640]{1,0:T(8,128)(2,1)S(1)}, bf16[32,640]{1,0:T(8,128)(2,1)S(1)}, u32[]{:S(2)}, u32[]{:S(2)}) %collective-permute-start.7) | collective-permute-done | bytes 40992 | tf_op jit(solution)/shard_map/mix/ppermute | solution.py:296
  67.7 5.0 %collective-permute-done.8 = bf16[1,32,768]{2,1,0:T(8,128)(2,1)S(1)} collective-permute-done((bf16[1,32,768]{2,1,0:T(8,128)(2,1)S(1)}, bf16[1,32,768]{2,1,0:T(8,128)(2,1)S(1)}, u32[]{:S(2)}, u32[]{:S(2)}) %collective-permute-start.8) | collective-permute-done | bytes 49184 | tf_op jit(solution)/shard_map/mix/ppermute | solution.py:296
  72.8 4.6 %collective-permute-done.9 = bf16[2,32,768]{2,1,0:T(8,128)(2,1)S(1)} collective-permute-done((bf16[2,32,768]{2,1,0:T(8,128)(2,1)S(1)}, bf16[2,32,768]{2,1,0:T(8,128)(2,1)S(1)}, u32[]{:S(2)}, u32[]{:S(2)}) %collective-permute-start.9) | collective-permute-done | bytes 98336 | tf_op jit(solution)/shard_map/mix/ppermute | solution.py:296
  78.9 4.2 %collective-permute-done.10 = bf16[4,32,768]{2,1,0:T(8,128)(2,1)S(1)} collective-permute-done((bf16[4,32,768]{2,1,0:T(8,128)(2,1)S(1)}, bf16[4,32,768]{2,1,0:T(8,128)(2,1)S(1)}, u32[]{:S(2)}, u32[]{:S(2)}) %collective-permute-start.10) | collective-permute-done | bytes 196640 | tf_op jit(solution)/shard_map/mix/ppermute | solution.py:296
  83.2 1.7 %collective-permute-done.11.far_ref = bf16[8,32,768]{2,1,0:T(8,128)(2,1)S(1)} collective-permute-done((bf16[8,32,768]{2,1,0:T(8,128)(2,1)S(1)}, bf16[8,32,768]{2,1,0:T(8,128)(2,1)S(1)}, u32[]{:S(2)}, u32[]{:S(2)}) %collective-permute-start.11) | collective-permute-done | bytes 393248 | tf_op jit(solution)/shard_map/mix/ppermute | solution.py:296
  84.9 4.0 %copy-done = bf16[5120,1024]{1,0:T(8,128)(2,1)S(1)} copy-done((bf16[5120,1024]{1,0:T(8,128)(2,1)S(1)}, bf16[5120,1024]{1,0:T(8,128)(2,1)}, u32[]{:S(2)}) %copy-start) | copy-done | bytes 10485784
  88.9 4.0 %copy-done.1 = bf16[5120,1024]{1,0:T(8,128)(2,1)S(1)} copy-done((bf16[5120,1024]{1,0:T(8,128)(2,1)S(1)}, bf16[5120,1024]{1,0:T(8,128)(2,1)}, u32[]{:S(2)}) %copy-start.1) | copy-done | bytes 10485784
  92.9 3.8 %ffn.2.h_ref = bf16[64,1024]{1,0:T(8,128)(2,1)S(1)} custom-call(s32[1]{0:T(128)} %bitcast.2.seq_ref, bf16[8,32,768]{2,1,0:T(8,128)(2,1)S(1)} %pad_maximum_fusion.own_ref, bf16[8,32,768]{2,1,0:T(8,128)(2,1)S(1)} %collective-permute-done.11.far_ref, bf16[5120,1024]{1,0:T(8,128)(2,1)S(1)} %copy-done, bf16[5120,1024]{1,0:T(8,128)(2,1)S(1)} %copy-done.1), custom_call_target="tpu_custom_call" | custom-call | tf_op jit(solution)/shard_map/ffn/pallas_call | solution.py:384
  96.9 2.2 %ffn.3 = (f32[8,32,640]{2,1,0:T(8,128)S(1)}, bf16[8,32,640]{2,1,0:T(8,128)(2,1)S(1)}) custom-call(s32[1]{0:T(128)} %bitcast.2.seq_ref, bf16[64,1024]{1,0:T(8,128)(2,1)S(1)} %ffn.2.h_ref, bf16[1024,5120]{1,0:T(8,128)(2,1)S(1)} %copy-done.2), custom_call_target="tpu_custom_call" | custom-call | tf_op jit(solution)/shard_map/ffn/pallas_call | solution.py:391
  102.4 4.8 %collective-permute-done.13 = bf16[4,32,640]{2,1,0:T(8,128)(2,1)S(1)} collective-permute-done((bf16[4,32,640]{2,1,0:T(8,128)(2,1)S(1)}, bf16[4,32,640]{2,1,0:T(8,128)(2,1)S(1)}, u32[]{:S(2)}, u32[]{:S(2)}) %collective-permute-start.13) | collective-permute-done | bytes 163872 | tf_op jit(solution)/shard_map/ffn/ppermute | solution.py:296
  107.4 4.4 %collective-permute-done.14 = bf16[2,32,640]{2,1,0:T(8,128)(2,1)S(1)} collective-permute-done((bf16[2,32,640]{2,1,0:T(8,128)(2,1)S(1)}, bf16[2,32,640]{2,1,0:T(8,128)(2,1)S(1)}, u32[]{:S(2)}, u32[]{:S(2)}) %collective-permute-start.14) | collective-permute-done | bytes 81952 | tf_op jit(solution)/shard_map/ffn/ppermute | solution.py:296
  112.8 3.9 %collective-permute-done.15 = bf16[1,32,640]{2,1,0:T(8,128)(2,1)S(1)} collective-permute-done((bf16[1,32,640]{2,1,0:T(8,128)(2,1)S(1)}, bf16[1,32,640]{2,1,0:T(8,128)(2,1)S(1)}, u32[]{:S(2)}, u32[]{:S(2)}) %collective-permute-start.15) | collective-permute-done | bytes 40992 | tf_op jit(solution)/shard_map/ffn/ppermute | solution.py:296
  118.4 2.4 %collective-permute-done.16 = bf16[32,640]{1,0:T(8,128)(2,1)S(1)} collective-permute-done((bf16[32,640]{1,0:T(8,128)(2,1)S(1)}, bf16[32,640]{1,0:T(8,128)(2,1)S(1)}, u32[]{:S(2)}, u32[]{:S(2)}) %collective-permute-start.16) | collective-permute-done | bytes 40992 | tf_op jit(solution)/shard_map/ffn/ppermute | solution.py:296
  (71 shorter events, 28.6 us)
Async XLA Ops:
  1.3 1.3 %copy-start.4 = (bf16[640,1024]{1,0:T(8,128)(2,1)S(1)}, bf16[640,1024]{1,0:T(8,128)(2,1)}, u32[]{:S(2)}) copy-start(bf16[640,1024]{1,0:T(8,128)(2,1)} %wq_ref.1) | copy-start | bytes 3932164
  5.9 8.3 %collective-permute-start = (bf16[64,1664]{1,0:T(8,128)(2,1)S(1)}, bf16[64,1664]{1,0:T(8,128)(2,1)S(1)}, u32[]{:S(2)}, u32[]{:S(2)}) collective-permute-start(bf16[64,1664]{1,0:T(8,128)(2,1)S(1)} %get-tuple-element.25), channel_id=1, source_target_pairs={{0,4},{4,0},{8,12},{12,8},{16,20},{20,16},{24,28},{28,24},{1,5},{5... | collective-permute-start | bytes 638984 | tf_op jit(solution)/shard_map/project/ppermute | solution.py:296
  14.4 6.5 %collective-permute-start.1 = (bf16[64,1664]{1,0:T(8,128)(2,1)S(1)}, bf16[64,1664]{1,0:T(8,128)(2,1)S(1)}, u32[]{:S(2)}, u32[]{:S(2)}) collective-permute-start(bf16[64,1664]{1,0:T(8,128)(2,1)S(1)} %get-tuple-element.27), channel_id=1, source_target_pairs={{0,8},{4,12},{8,0},{12,4},{16,24},{20,28},{24,16},{28,20},{1,9},{5... | collective-permute-start | bytes 638984 | tf_op jit(solution)/shard_map/project/ppermute | solution.py:296
  21.1 11.0 %collective-permute-start.2 = (bf16[64,1664]{1,0:T(8,128)(2,1)S(1)}, bf16[64,1664]{1,0:T(8,128)(2,1)S(1)}, u32[]{:S(2)}, u32[]{:S(2)}) collective-permute-start(bf16[64,1664]{1,0:T(8,128)(2,1)S(1)} %get-tuple-element.29), channel_id=1, source_target_pairs={{0,16},{4,20},{8,24},{12,28},{16,0},{20,4},{24,8},{28,12},{1,17},{... | collective-permute-start | bytes 638984 | tf_op jit(solution)/shard_map/project/ppermute | solution.py:296
  32.1 1.2 copy-start.5
  40.3 5.1 %collective-permute-start.3 = (bf16[64,1152]{1,0:T(8,128)(2,1)S(1)}, bf16[64,1152]{1,0:T(8,128)(2,1)S(1)}, u32[]{:S(2)}, u32[]{:S(2)}) collective-permute-start(bf16[64,1152]{1,0:T(8,128)(2,1)S(1)} %get-tuple-element.32), channel_id=1, source_target_pairs={{0,4},{4,0},{8,12},{12,8},{16,20},{20,16},{24,28},{28,24},{1,5},{5... | collective-permute-start | bytes 442376 | tf_op jit(solution)/shard_map/attend/ppermute | solution.py:296
  45.8 5.2 %collective-permute-start.4 = (bf16[64,1152]{1,0:T(8,128)(2,1)S(1)}, bf16[64,1152]{1,0:T(8,128)(2,1)S(1)}, u32[]{:S(2)}, u32[]{:S(2)}) collective-permute-start(bf16[64,1152]{1,0:T(8,128)(2,1)S(1)} %get-tuple-element.35), channel_id=1, source_target_pairs={{0,8},{4,12},{8,0},{12,4},{16,24},{20,28},{24,16},{28,20},{1,9},{5... | collective-permute-start | bytes 442376 | tf_op jit(solution)/shard_map/attend/ppermute | solution.py:296
  51.3 7.7 %collective-permute-start.5 = (bf16[64,1152]{1,0:T(8,128)(2,1)S(1)}, bf16[64,1152]{1,0:T(8,128)(2,1)S(1)}, u32[]{:S(2)}, u32[]{:S(2)}) collective-permute-start(bf16[64,1152]{1,0:T(8,128)(2,1)S(1)} %get-tuple-element.38), channel_id=1, source_target_pairs={{0,16},{4,20},{8,24},{12,28},{16,0},{20,4},{24,8},{28,12},{1,17},{... | collective-permute-start | bytes 442376 | tf_op jit(solution)/shard_map/attend/ppermute | solution.py:296
  59.0 1.3 %copy-start.3 = (bf16[1024,640]{1,0:T(8,128)(2,1)S(1)}, bf16[1024,640]{1,0:T(8,128)(2,1)}, u32[]{:S(2)}) copy-start(bf16[1024,640]{1,0:T(8,128)(2,1)} %w_ref.2) | copy-start | bytes 3932164
  61.0 1.3 %collective-permute-start.6 = (f32[32,640]{1,0:T(8,128)S(1)}, f32[32,640]{1,0:T(8,128)S(1)}, u32[]{:S(2)}, u32[]{:S(2)}) collective-permute-start(f32[32,640]{1,0:T(8,128)S(1)} %get-tuple-element.40), channel_id=1, source_target_pairs={{0,1},{1,0},{2,3},{3,2},{4,5},{5,4},{6,7},{7,6},{8,9},{9,8},{10,11... | collective-permute-start | bytes 245768 | tf_op jit(solution)/shard_map/mix/ppermute | solution.py:296
  62.3 4.1 %collective-permute-start.7 = (bf16[32,640]{1,0:T(8,128)(2,1)S(1)}, bf16[32,640]{1,0:T(8,128)(2,1)S(1)}, u32[]{:S(2)}, u32[]{:S(2)}) collective-permute-start(bf16[32,640]{1,0:T(8,128)(2,1)S(1)} %fusion.3), channel_id=1, source_target_pairs={{0,2},{1,3},{2,0},{3,1},{4,6},{5,7},{6,4},{7,5},{8,10},{9,11},{10,... | collective-permute-start | bytes 122888 | tf_op jit(solution)/shard_map/mix/ppermute | solution.py:296
  67.4 5.2 %collective-permute-start.8 = (bf16[1,32,768]{2,1,0:T(8,128)(2,1)S(1)}, bf16[1,32,768]{2,1,0:T(8,128)(2,1)S(1)}, u32[]{:S(2)}, u32[]{:S(2)}) collective-permute-start(bf16[1,32,768]{2,1,0:T(8,128)(2,1)S(1)} %maximum_bitcast_fusion), channel_id=1, source_target_pairs={{0,16},{4,20},{8,24},{12,28},{16,0},{20,4},{24,8},{28,12},{1,17},{... | collective-permute-start | bytes 147464 | tf_op jit(solution)/shard_map/mix/ppermute | solution.py:296
  72.7 4.7 %collective-permute-start.9 = (bf16[2,32,768]{2,1,0:T(8,128)(2,1)S(1)}, bf16[2,32,768]{2,1,0:T(8,128)(2,1)S(1)}, u32[]{:S(2)}, u32[]{:S(2)}) collective-permute-start(bf16[2,32,768]{2,1,0:T(8,128)(2,1)S(1)} %pad_maximum_fusion.2), channel_id=1, source_target_pairs={{0,8},{4,12},{8,0},{12,4},{16,24},{20,28},{24,16},{28,20},{1,9},{5... | collective-permute-start | bytes 294920 | tf_op jit(solution)/shard_map/mix/ppermute | solution.py:296
  77.4 5.7 %collective-permute-start.10 = (bf16[4,32,768]{2,1,0:T(8,128)(2,1)S(1)}, bf16[4,32,768]{2,1,0:T(8,128)(2,1)S(1)}, u32[]{:S(2)}, u32[]{:S(2)}) collective-permute-start(bf16[4,32,768]{2,1,0:T(8,128)(2,1)S(1)} %pad_maximum_fusion.1), channel_id=1, source_target_pairs={{0,4},{4,0},{8,12},{12,8},{16,20},{20,16},{24,28},{28,24},{1,5},{5... | collective-permute-start | bytes 589832 | tf_op jit(solution)/shard_map/mix/ppermute | solution.py:296
  83.1 1.8 %collective-permute-start.11 = (bf16[8,32,768]{2,1,0:T(8,128)(2,1)S(1)}, bf16[8,32,768]{2,1,0:T(8,128)(2,1)S(1)}, u32[]{:S(2)}, u32[]{:S(2)}) collective-permute-start(bf16[8,32,768]{2,1,0:T(8,128)(2,1)S(1)} %pad_maximum_fusion.own_ref), channel_id=1, source_target_pairs={{0,1},{1,0},{2,3},{3,2},{4,5},{5,4},{6,7},{7,6},{8,9},{9,8},{10,11... | collective-permute-start | bytes 1179656 | tf_op jit(solution)/shard_map/mix/ppermute | solution.py:296
  84.9 4.0 %copy-start = (bf16[5120,1024]{1,0:T(8,128)(2,1)S(1)}, bf16[5120,1024]{1,0:T(8,128)(2,1)}, u32[]{:S(2)}) copy-start(bf16[5120,1024]{1,0:T(8,128)(2,1)} %wg_ref.1) | copy-start | bytes 31457284
  88.9 4.0 %copy-start.1 = (bf16[5120,1024]{1,0:T(8,128)(2,1)S(1)}, bf16[5120,1024]{1,0:T(8,128)(2,1)}, u32[]{:S(2)}) copy-start(bf16[5120,1024]{1,0:T(8,128)(2,1)} %wu_ref.1) | copy-start | bytes 31457284
  92.9 4.0 %copy-start.2 = (bf16[1024,5120]{1,0:T(8,128)(2,1)S(1)}, bf16[1024,5120]{1,0:T(8,128)(2,1)}, u32[]{:S(2)}) copy-start(bf16[1024,5120]{1,0:T(8,128)(2,1)} %w_ref.3) | copy-start | bytes 31457284
  99.1 1.7 %collective-permute-start.12 = (bf16[8,32,640]{2,1,0:T(8,128)(2,1)S(1)}, bf16[8,32,640]{2,1,0:T(8,128)(2,1)S(1)}, u32[]{:S(2)}, u32[]{:S(2)}) collective-permute-start(bf16[8,32,640]{2,1,0:T(8,128)(2,1)S(1)} %get-tuple-element.42), channel_id=1, source_target_pairs={{0,1},{1,0},{2,3},{3,2},{4,5},{5,4},{6,7},{7,6},{8,9},{9,8},{10,11... | collective-permute-start | bytes 983048 | tf_op jit(solution)/shard_map/ffn/ppermute | solution.py:296
  100.9 6.3 %collective-permute-start.13 = (bf16[4,32,640]{2,1,0:T(8,128)(2,1)S(1)}, bf16[4,32,640]{2,1,0:T(8,128)(2,1)S(1)}, u32[]{:S(2)}, u32[]{:S(2)}) collective-permute-start(bf16[4,32,640]{2,1,0:T(8,128)(2,1)S(1)} %slice.47), channel_id=1, source_target_pairs={{0,4},{4,0},{8,12},{12,8},{16,20},{20,16},{24,28},{28,24},{1,5},{5... | collective-permute-start | bytes 491528 | tf_op jit(solution)/shard_map/ffn/ppermute | solution.py:296
  107.3 4.5 %collective-permute-start.14 = (bf16[2,32,640]{2,1,0:T(8,128)(2,1)S(1)}, bf16[2,32,640]{2,1,0:T(8,128)(2,1)S(1)}, u32[]{:S(2)}, u32[]{:S(2)}) collective-permute-start(bf16[2,32,640]{2,1,0:T(8,128)(2,1)S(1)} %slice.48), channel_id=1, source_target_pairs={{0,8},{4,12},{8,0},{12,4},{16,24},{20,28},{24,16},{28,20},{1,9},{5... | collective-permute-start | bytes 245768 | tf_op jit(solution)/shard_map/ffn/ppermute | solution.py:296
  111.8 5.0 %collective-permute-start.15 = (bf16[1,32,640]{2,1,0:T(8,128)(2,1)S(1)}, bf16[1,32,640]{2,1,0:T(8,128)(2,1)S(1)}, u32[]{:S(2)}, u32[]{:S(2)}) collective-permute-start(bf16[1,32,640]{2,1,0:T(8,128)(2,1)S(1)} %slice.49), channel_id=1, source_target_pairs={{0,16},{4,20},{8,24},{12,28},{16,0},{20,4},{24,8},{28,12},{1,17},{... | collective-permute-start | bytes 122888 | tf_op jit(solution)/shard_map/ffn/ppermute | solution.py:296
  116.8 4.1 %collective-permute-start.16 = (bf16[32,640]{1,0:T(8,128)(2,1)S(1)}, bf16[32,640]{1,0:T(8,128)(2,1)S(1)}, u32[]{:S(2)}, u32[]{:S(2)}) collective-permute-start(bf16[32,640]{1,0:T(8,128)(2,1)S(1)} %fusion.2), channel_id=1, source_target_pairs={{0,2},{1,3},{2,0},{3,1},{4,6},{5,7},{6,4},{7,5},{8,10},{9,11},{10,... | collective-permute-start | bytes 122888 | tf_op jit(solution)/shard_map/ffn/ppermute | solution.py:296
  120.9 1.3 %collective-permute-start.17 = (bf16[32,640]{1,0:T(8,128)(2,1)S(1)}, bf16[32,640]{1,0:T(8,128)(2,1)S(1)}, u32[]{:S(2)}, u32[]{:S(2)}) collective-permute-start(bf16[32,640]{1,0:T(8,128)(2,1)S(1)} %add_convert_fusion), channel_id=1, source_target_pairs={{0,1},{1,0},{2,3},{3,2},{4,5},{5,4},{6,7},{7,6},{8,9},{9,8},{10,11... | collective-permute-start | bytes 122888 | tf_op jit(solution)/shard_map/ffn/ppermute | solution.py:296
  (5 other events, 4.7 us)

commit v2 on v1

v2 whole, which is shorter than its diff:
```python
import functools
import math

import jax
import jax.numpy as jnp
from jax import lax
from jax.experimental import pallas as pl
from jax.experimental.pallas import tpu as pltpu
from jax.sharding import PartitionSpec as P

F32 = jnp.float32
BF16 = jnp.bfloat16
LANES = 128
VMEM = pl.BlockSpec(memory_space=pltpu.VMEM)
SMEM = pl.BlockSpec(memory_space=pltpu.SMEM)
HBM = pl.BlockSpec(memory_space=pltpu.HBM)
ANY = pl.BlockSpec(memory_space=pl.ANY)


def call(body, outs, ins, scratch=(), cost=3, limit=8):
    return pl.pallas_call(
        body,
        out_shape=outs,
        in_specs=ins,
        out_specs=[VMEM] * len(outs),
        scratch_shapes=list(scratch),
        cost_estimate=pl.CostEstimate(flops=int(cost * 1.15e9), bytes_accessed=1 << 20, transcendentals=0),
        compiler_params=pltpu.CompilerParams(vmem_limit_bytes=limit << 20),
    )


def sds(shape, dtype):
    return jax.ShapeDtypeStruct(shape, dtype)


def lane_ids(rows):
    return lax.broadcasted_iota(jnp.int32, (rows, LANES), 1)


def split3(value):
    high = value.astype(BF16)
    rest = value - high.astype(F32)
    mid = rest.astype(BF16)
    low = (rest - mid.astype(F32)).astype(BF16)
    return high, mid, low


def pack_stats(stats):
    high, mid, low = (part.astype(F32) for part in split3(stats))
    return (high + pltpu.roll(mid, 8, 1) + pltpu.roll(low, 16, 1)).astype(BF16)


def unpack_stats(packed):
    packed = packed.astype(F32)
    return (packed + pltpu.roll(packed, LANES - 8, 1)) + pltpu.roll(packed, LANES - 16, 1)


def halves(x):
    steps, requests, _ = x.shape
    cut = requests // 2
    low = jnp.concatenate([x[t, :cut] for t in range(steps)], axis=0)
    high = jnp.concatenate([x[t, cut:] for t in range(steps)], axis=0)
    return low, high


def project_kernel(
    pair_ref,
    x_hbm,
    gain_hbm,
    wq_hbm,
    wk_hbm,
    wv_hbm,
    k_hbm,
    v_hbm,
    acc_ref,
    msg_ref,
    lent_ref,
    x_ref,
    gain_ref,
    wq_ref,
    wk_ref,
    wv_ref,
    sems,
):
    cut = lent_ref.shape[1]
    lent = pl.ds((1 - pair_ref[0]) * cut, cut)
    copies = [
        pltpu.make_async_copy(source, target, sems.at[i])
        for i, (source, target) in enumerate(
            (
                (x_hbm, x_ref),
                (gain_hbm, gain_ref),
                (wq_hbm, wq_ref),
                (wk_hbm, wk_ref),
                (wv_hbm, wv_ref),
                (k_hbm.at[lent], lent_ref.at[0]),
                (v_hbm.at[lent], lent_ref.at[1]),
            )
        )
    ]
    for copy in copies:
        copy.start()
    copies[0].wait()
    copies[1].wait()
    low, high = halves(x_ref[...].astype(F32))
    first = pair_ref[0] == 0
    x = jnp.concatenate([jnp.where(first, low, high), jnp.where(first, high, low)], axis=0)
    normed = (x * gain_ref[...].astype(F32)).astype(BF16)
    squares = jnp.sum(x * x, axis=1, keepdims=True)
    at = 0
    for copy, w_ref in zip(copies[2:], (wq_ref, wk_ref, wv_ref)):
        copy.wait()
        width = w_ref.shape[1]
        part = jnp.dot(normed, w_ref[...], preferred_element_type=F32)
        acc_ref[:, at : at + width] = part
        msg_ref[:, at : at + width] = part.astype(BF16)
        at += width
    stats = jnp.where(lane_ids(x.shape[0]) == 0, squares, 0.0)
    acc_ref[:, at:] = stats
    msg_ref[:, at:] = pack_stats(stats)
    copies[5].wait()
    copies[6].wait()


def added(acc_ref, recv_ref):
    at = acc_ref.shape[1] - LANES
    total = acc_ref[:, :at] + recv_ref[:, :at].astype(F32)
    stats = acc_ref[:, at:] + unpack_stats(recv_ref[:, at:])
    return total, jnp.where(lane_ids(stats.shape[0]) == 0, stats, 0.0)


def add_kernel(acc_ref, recv_ref, out_ref, msg_ref):
    at = acc_ref.shape[1] - LANES
    total, stats = added(acc_ref, recv_ref)
    out_ref[:, :at] = total
    msg_ref[:, :at] = total.astype(BF16)
    out_ref[:, at:] = stats
    msg_ref[:, at:] = pack_stats(stats)


def part_kernel(acc_ref, recv_ref, out_ref, msg_ref):
    at = acc_ref.shape[1] - LANES
    total, stats = added(acc_ref, recv_ref)
    half = total.shape[0] // 2
    out_ref[:, :at] = total[:half]
    msg_ref[:, :at] = total[half:].astype(BF16)
    out_ref[:, at:] = stats[:half]
    msg_ref[:, at:] = pack_stats(stats[half:])


def attend_kernel(
    heads,
    kv,
    steps,
    features,
    span,
    seq_ref,
    len_ref,
    acc_ref,
    recv_ref,
    cos_ref,
    sin_ref,
    k_ref,
    v_ref,
    far_ref,
    o_ref,
    st_ref,
    msg_ref,
    new_ref,
    q_buf,
    kn_buf,
    vn_buf,
    o_buf,
    m_buf,
    l_buf,
):
    requests, rows_kv, hd = far_ref.shape[1:]
    group = heads // kv
    block = steps * heads
    fresh = steps * kv
    at = (heads + 2 * kv) * hd
    squares = acc_ref[:, at:] + unpack_stats(recv_ref[:, at:])
    scale = lax.rsqrt(squares[:, 0:1] / features + 1e-05)

    def vector(index):
        cols = slice(index * hd, (index + 1) * hd)
        return (acc_ref[:, cols] + recv_ref[:, cols].astype(F32)) * scale

    def rotated(value):
        return value * cos_ref[...] + pltpu.roll(value, hd // 2, 1) * sin_ref[...]

    def spread(buf, value, index, per_step):
        for t in range(steps):
            buf[pl.ds(t * per_step + index, requests, stride=steps * per_step), :] = value[
                t * requests : (t + 1) * requests
            ]

    for g in range(kv):
        for i, (buf, value) in enumerate(
            ((kn_buf, rotated(vector(heads + g))), (vn_buf, vector(heads + kv + g)))
        ):
            spread(buf, value, g, kv)
            new_ref[:, (i * kv + g) * hd : (i * kv + g + 1) * hd] = value.astype(BF16)
    for h in range(heads):
        spread(q_buf, rotated(vector(h)), h, heads)

    seq = seq_ref[0]
    pair = seq & 1
    own_first = seq * span
    far_first = (seq ^ 1) * span
    low = (seq - pair) * span
    shrink = hd ** (-0.5)

    k_new = kn_buf[...].astype(BF16)
    v_new = vn_buf[...].astype(BF16)
    queries = q_buf[...].astype(BF16)
    shape = (requests * block, requests * fresh)
    row = lax.broadcasted_iota(jnp.int32, shape, 0)
    col = lax.broadcasted_iota(jnp.int32, shape, 1)
    col_row = lax.broadcasted_iota(jnp.int32, (1, shape[1]), 1)
    at_position = (col_row % fresh) // kv
    for r in range(requests):
        at_position += jnp.where(col_row // fresh == r, len_ref[pair * requests + r], 0)
    held = (at_position >= low) & (at_position < low + 2 * span)
    new_live = (
        (row // block == col // fresh)
        & ((row % heads) // group == col % kv)
        & ((row % block) // heads >= (col % fresh) // kv)
        & held
    )
    new_scores = (
        lax.dot_general(queries, k_new, (((1,), (1,)), ((), ())), preferred_element_type=F32) * shrink
    )
    new_scores = jnp.where(new_live, new_scores, -1e30)
    new_top = jnp.max(new_scores, axis=1, keepdims=True)

    row = lax.broadcasted_iota(jnp.int32, (block, rows_kv), 0)
    col = lax.broadcasted_iota(jnp.int32, (block, rows_kv), 1)
    need = jnp.where((row % heads) // group == col % kv, col // kv, 1 << 29)
    for r in range(requests):
        mine = slice(r * block, (r + 1) * block)
        query = queries[mine]
        length = len_ref[pair * requests + r]
        top = new_top[mine]
        parts = []
        for keys, first in ((k_ref[pair * requests + r], own_first), (far_ref[0, r], far_first)):
            scores = lax.dot_general(query, keys, (((1,), (1,)), ((), ())), preferred_element_type=F32) * shrink
            live = need < length - first
            masked = jnp.where(live, scores, -1e30)
            top = jnp.maximum(top, jnp.max(masked, axis=1, keepdims=True))
            parts.append((live, masked))
        total = jnp.zeros((block, 1), F32)
        summed = jnp.zeros((block, hd), F32)
        for (live, masked), values in zip(parts, (v_ref[pair * requests + r], far_ref[1, r])):
            expo = jnp.where(live, jnp.exp(masked - top), 0.0)
            total += jnp.sum(expo, axis=1, keepdims=True)
            summed += jnp.dot(expo.astype(BF16), values, preferred_element_type=F32)
        o_buf[mine, :] = summed
        m_buf[mine, :] = jnp.broadcast_to(top, (block, hd))
        l_buf[mine, :] = jnp.broadcast_to(total, (block, hd))
    expo = jnp.where(new_live, jnp.exp(new_scores - m_buf[:, 0:1]), 0.0)
    l_buf[...] += jnp.sum(expo, axis=1, keepdims=True)
    o_buf[...] += jnp.dot(expo.astype(BF16), v_new, preferred_element_type=F32)

    lane = lane_ids(requests)
    for t in range(steps):
        mine = slice(t * requests, (t + 1) * requests)
        stats = jnp.zeros((requests, LANES), F32)
        for h in range(heads):
            take = pl.ds(t * heads + h, requests, stride=block)
            o_ref[mine, h * hd : (h + 1) * hd] = o_buf[take, :]
            stats = jnp.where(lane == h, m_buf[take, :], stats)
            stats = jnp.where(lane == 24 + h, l_buf[take, :], stats)
        st_ref[mine, :] = stats
    msg_ref[:, : heads * hd] = o_ref[...].astype(BF16)
    msg_ref[:, heads * hd :] = pack_stats(st_ref[...])


def merged(heads, o_ref, st_ref, recv_ref):
    hd = o_ref.shape[1] // heads
    mine = st_ref[...]
    theirs = unpack_stats(recv_ref[:, heads * hd :])
    top = jnp.maximum(mine, theirs)
    keep, take = jnp.exp(mine - top), jnp.exp(theirs - top)
    total = mine * pltpu.roll(keep, 24, 1) + theirs * pltpu.roll(take, 24, 1)
    lane = lane_ids(mine.shape[0])
    stats = jnp.where(lane < heads, top, jnp.where((lane >= 24) & (lane < 24 + heads), total, 0.0))

    def head(h):
        cols = slice(h * hd, (h + 1) * hd)
        return o_ref[:, cols] * keep[:, h : h + 1] + recv_ref[:, cols].astype(F32) * take[:, h : h + 1]

    return stats, head


def merge_kernel(heads, o_ref, st_ref, recv_ref, o_out, st_out, msg_out):
    stats, head = merged(heads, o_ref, st_ref, recv_ref)
    hd = o_ref.shape[1] // heads
    for h in range(heads):
        value = head(h)
        o_out[:, h * hd : (h + 1) * hd] = value
        msg_out[:, h * hd : (h + 1) * hd] = value.astype(BF16)
    st_out[...] = stats
    msg_out[:, heads * hd :] = pack_stats(stats)


def finish_kernel(heads, o_ref, st_ref, recv_ref, new_ref, att_ref):
    stats, head = merged(heads, o_ref, st_ref, recv_ref)
    hd = o_ref.shape[1] // heads
    for h in range(heads):
        att_ref[:, h * hd : (h + 1) * hd] = (head(h) / stats[:, 24 + h : 25 + h]).astype(BF16)
    att_ref[:, heads * hd :] = new_ref[...]


def store_kernel(
    heads, steps, span, seq_ref, len_ref, own_ref, far_ref, k_ref, v_ref, after_ref, k_out, v_out, done_ref, buf
):
    done_ref[...] = after_ref[...]
    requests, rows_kv, hd = k_ref.shape
    kv = rows_kv // span
    cut = requests // 2
    fresh = steps * kv
    seq = seq_ref[0]
    low = (seq & 1) == 0
    place = lax.broadcasted_iota(jnp.int32, (rows_kv, fresh), 0) - lax.broadcasted_iota(
        jnp.int32, (rows_kv, fresh), 1
    )
    line = lax.broadcasted_iota(jnp.int32, (rows_kv, hd), 0)
    for i, (cache_ref, out_ref) in enumerate(((k_ref, k_out), (v_ref, v_out))):
        for g in range(kv):
            at = (heads + i * kv + g) * hd
            own, far = (ref[:, at : at + hd].astype(F32) for ref in (own_ref, far_ref))
            for n, value in enumerate((jnp.where(low, own, far), jnp.where(low, far, own))):
                for t in range(steps):
                    buf[pl.ds((i * 2 + n) * cut * fresh + t * kv + g, cut, stride=fresh), :] = value[
                        t * cut : (t + 1) * cut
                    ]
        out_ref[...] = cache_ref[...]
        for r in range(requests):
            base = (len_ref[r] - seq * span) * kv

            @pl.when((base > -fresh) & (base < rows_kv))
            def _():
                pick = jnp.where(place == base, 1.0, 0.0).astype(BF16)
                at = (i * requests + r) * fresh
                rows = buf[at : at + fresh, :].astype(BF16)
                put = jnp.dot(pick, rows, preferred_element_type=F32)
                new = (line >= base) & (line < base + fresh)
                out_ref[r] = jnp.where(new, put, cache_ref[r].astype(F32)).astype(BF16)


def mix_kernel(seq_ref, core_ref, own_ref, far_ref, w_ref, mine_ref, other_ref):
    depth = w_ref.shape[0]
    att = jnp.concatenate([own_ref[:, :depth], far_ref[:, :depth]], axis=0)
    part = jnp.dot(att, w_ref[...], preferred_element_type=F32)
    half = part.shape[0] // 2
    same = (seq_ref[0] & 1) == core_ref[0]
    mine_ref[...] = jnp.where(same, part[:half], part[half:])
    other_ref[...] = jnp.where(same, part[half:], part[:half])


def stack_kernel(ties, *refs):
    *in_refs, out_ref = refs[ties:]
    at = 0
    for ref in in_refs:
        out_ref[at : at + ref.shape[0]] = ref[...]
        at += ref.shape[0]


def round_kernel(mine_ref, recv_ref, msg_ref):
    msg_ref[...] = (mine_ref[...] + recv_ref[...]).astype(BF16)


def sum_kernel(mine_ref, recv_ref, msg_ref):
    msg_ref[...] = (mine_ref[...].astype(F32) + recv_ref[...].astype(F32)).astype(BF16)


def residual_kernel(core_ref, x_ref, gain_ref, mine_ref, recv_ref, mixed_ref, piece_ref):
    low, high = halves(x_ref[...].astype(F32))
    part = mine_ref[...].astype(F32) + recv_ref[...].astype(F32)
    mixed = jnp.where(core_ref[0] == 0, low, high) + part
    mixed_ref[...] = mixed
    squares = jnp.sum(mixed * mixed, axis=1, keepdims=True)
    stats = jnp.where(lane_ids(mixed.shape[0]) == 0, squares, 0.0)
    piece_ref[0, :, :LANES] = pack_stats(stats)
    piece_ref[0, :, LANES:] = (mixed * gain_ref[...].astype(F32)).astype(BF16)


def gather_products(masks, seq, own_ref, far_ref, wg_ref, wu_ref):
    count, width = own_ref.shape[0], own_ref.shape[2] - LANES
    squares = []
    for ref in (own_ref, far_ref):
        total = unpack_stats(ref[0, :, :LANES])
        for j in range(1, count):
            total += unpack_stats(ref[j, :, :LANES])
        squares.append(total)
    gate = up = 0.0
    for j in range(count):
        take = pl.ds(pl.multiple_of((seq ^ masks[j]) * width, 16), width)
        x = jnp.concatenate([own_ref[j, :, LANES:], far_ref[j, :, LANES:]], axis=0)
        gate += jnp.dot(x, wg_ref[take, :], preferred_element_type=F32)
        up += jnp.dot(x, wu_ref[take, :], preferred_element_type=F32)
    return jnp.concatenate(squares, axis=0), gate, up


def begin_kernel(masks, seq_ref, own_ref, far_ref, wg_ref, wu_ref, sq_ref, gate_ref, up_ref):
    squares, gate, up = gather_products(masks, seq_ref[0], own_ref, far_ref, wg_ref, wu_ref)
    sq_ref[...] = squares
    gate_ref[...] = gate
    up_ref[...] = up


def hidden_kernel(
    masks, features, seq_ref, own_ref, far_ref, wg_ref, wu_ref, sq_ref, gate_ref, up_ref, h_ref
):
    squares, gate, up = gather_products(masks, seq_ref[0], own_ref, far_ref, wg_ref, wu_ref)
    scale = lax.rsqrt((squares + sq_ref[...])[:, 0:1] / features + 1e-05)
    gate = (gate + gate_ref[...]) * scale
    up = (up + up_ref[...]) * scale
    h_ref[...] = (gate / (1.0 + jnp.exp(-gate)) * up).astype(BF16)


def down_kernel(masks, seq_ref, h_ref, w_ref, own_ref, far_ref):
    half, width = own_ref.shape[1:]
    hidden = h_ref[...]
    for j, mask in enumerate(masks):
        take = pl.ds(pl.multiple_of((seq_ref[0] ^ mask) * width, LANES), width)
        part = jnp.dot(hidden, w_ref[:, take], preferred_element_type=F32)
        own_ref[j] = part[:half]
        far_ref[j] = part[half:].astype(BF16)


def fold_kernel(acc_ref, *refs):
    *recv_refs, keep_ref, msg_ref = refs
    count = acc_ref.shape[0] // 2
    for j in range(2 * count):
        total = acc_ref[j]
        for ref in recv_refs:
            total += ref[j].astype(F32)
        if j < count:
            keep_ref[j] = total
        else:
            msg_ref[j - count] = total.astype(BF16)


def end_kernel(mixed_ref, mine_ref, recv_ref, out_ref):
    part = mine_ref[0].astype(F32) + recv_ref[0].astype(F32)
    out_ref[...] = (mixed_ref[...] + part).astype(BF16)


def join_kernel(core_ref, own_ref, far_ref, out_ref):
    steps, requests, _ = out_ref.shape
    cut = requests // 2
    low = core_ref[0] == 0
    own, far = own_ref[...].astype(F32), far_ref[...].astype(F32)
    first, second = jnp.where(low, own, far), jnp.where(low, far, own)
    for t in range(steps):
        rows = slice(t * cut, (t + 1) * cut)
        out_ref[t] = jnp.concatenate([first[rows], second[rows]], axis=0).astype(BF16)


def per_device(
    n_seq,
    n_tp,
    tokens,
    attn_gain,
    w_query,
    w_key,
    w_value,
    w_out,
    ffn_gain,
    w_gate,
    w_up,
    w_down,
    key_cache,
    value_cache,
    lengths,
):
    steps, requests, width = tokens.shape
    span, kv, hd = key_cache.shape[1:]
    heads = w_query.shape[1] // hd
    cut = requests // 2
    half = steps * cut
    features = width * n_seq
    hidden_width = w_gate.shape[1]
    wide = w_query.shape[1] + w_key.shape[1] + w_value.shape[1] + LANES
    seq = lax.axis_index("seq").astype(jnp.int32)
    pair = seq & 1
    core = lax.axis_index("tp").astype(jnp.int32) & 1
    seq_arr, core_arr, pair_arr = seq.reshape(1), core.reshape(1), pair.reshape(1)
    seq_bits = [1 << b for b in range(n_seq.bit_length() - 1)]
    tp_bits = [1 << b for b in range(n_tp.bit_length() - 1)]
    masks = [0]
    for bit in reversed(seq_bits):
        masks = masks + [m ^ bit for m in masks]
    near, away = masks[: n_seq // 2], masks[n_seq // 2 :]

    def hop(value, axis, bit):
        size = n_seq if axis == "seq" else n_tp
        return lax.ppermute(value, axis, [(i, i ^ bit) for i in range(size)])

    flat = (requests, span * kv, hd)
    k_flat, v_flat = key_cache.reshape(flat), value_cache.reshape(flat)
    with jax.named_scope("project"):
        rows = 2 * half
        acc, msg, lent = call(
            project_kernel,
            [sds((rows, wide), F32), sds((rows, wide), BF16), sds((2, cut) + flat[1:], BF16)],
            [SMEM] + [HBM] * 7,
            [
                pltpu.VMEM(tokens.shape, BF16),
                pltpu.VMEM(attn_gain.shape, BF16),
                pltpu.VMEM(w_query.shape, BF16),
                pltpu.VMEM(w_key.shape, BF16),
                pltpu.VMEM(w_value.shape, BF16),
                pltpu.SemaphoreType.DMA((7,)),
            ],
            limit=60,
        )(pair_arr, tokens, attn_gain, w_query, w_key, w_value, k_flat, v_flat)
        borrowed = hop(lent, "seq", 1)
        for bit in reversed(seq_bits[1:]):
            recv = hop(msg, "seq", bit)
            last = bit == seq_bits[1]
            count = half if last else rows
            acc, msg = call(
                part_kernel if last else add_kernel,
                [sds((count, wide), F32), sds((count, wide), BF16)],
                [VMEM] * 2,
            )(acc, recv)
        recv = hop(msg, "seq", 1)

    lent_lengths = lax.dynamic_slice_in_dim(lengths, pair * cut, cut, 0)
    positions = (lent_lengths[None, :] + jnp.arange(steps, dtype=jnp.int32)[:, None]).reshape(half)
    freqs = jnp.exp(jnp.arange(hd // 2, dtype=F32) * (-2.0 * math.log(100000000.0) / hd))
    angles = positions.astype(F32)[:, None] * freqs[None, :]
    cosine, sine = jnp.cos(angles), jnp.sin(angles)
    cosine = jnp.concatenate([cosine, cosine], axis=1)
    sine = jnp.concatenate([-sine, sine], axis=1)

    with jax.named_scope("attend"):
        block = steps * heads
        fresh = steps * kv
        joint = [
            sds((half, heads * hd), F32),
            sds((half, LANES), F32),
            sds((half, heads * hd + LANES), BF16),
        ]
        o, st, msg, news = call(
            functools.partial(attend_kernel, heads, kv, steps, features, span),
            joint + [sds((half, 2 * kv * hd), BF16)],
            [SMEM, SMEM] + [VMEM] * 7,
            [
                pltpu.VMEM((cut * block, hd), F32),
                pltpu.VMEM((cut * fresh, hd), F32),
                pltpu.VMEM((cut * fresh, hd), F32),
                pltpu.VMEM((cut * block, hd), F32),
                pltpu.VMEM((cut * block, hd), F32),
                pltpu.VMEM((cut * block, hd), F32),
            ],
        )(seq_arr, lengths, acc, recv, cosine, sine, k_flat, v_flat, borrowed)
        for bit in seq_bits[1:-1]:
            o, st, msg = call(functools.partial(merge_kernel, heads), joint, [VMEM] * 3)(
                o, st, hop(msg, "seq", bit)
            )
        (attended,) = call(
            functools.partial(finish_kernel, heads),
            [sds((half, (heads + 2 * kv) * hd), BF16)],
            [VMEM] * 4,
        )(o, st, hop(msg, "seq", seq_bits[-1]), news)
        others = hop(attended, "seq", 1)

    with jax.named_scope("mix"):
        mine, other = call(mix_kernel, [sds((half, width), F32)] * 2, [SMEM, SMEM] + [VMEM] * 3)(
            seq_arr, core_arr, attended, others, w_out
        )
        (part,) = call(round_kernel, [sds((half, width), BF16)], [VMEM] * 2)(mine, hop(other, "tp", 1))
        for bit in tp_bits[1:-1]:
            (part,) = call(sum_kernel, [sds((half, width), BF16)], [VMEM] * 2)(part, hop(part, "tp", bit))
        gain = lax.dynamic_slice_in_dim(ffn_gain, seq * width, width, 0).reshape(1, width)
        mixed, pieces = call(
            residual_kernel,
            [sds((half, width), F32), sds((1, half, LANES + width), BF16)],
            [SMEM] + [VMEM] * 4,
        )(core_arr, tokens, gain, part, hop(part, "tp", tp_bits[-1]))
        ties = []
        for bit in reversed(seq_bits[1:]):
            if bit == seq_bits[1]:
                keys, values, done = call(
                    functools.partial(store_kernel, heads, steps, span),
                    [sds(flat, BF16)] * 2 + [sds((half, LANES), F32)],
                    [SMEM, SMEM] + [VMEM] * 5,
                    [pltpu.VMEM((2 * requests * fresh, hd), F32)],
                )(seq_arr, lengths, attended, others, k_flat, v_flat, pieces[0, :, :LANES].astype(F32))
                ties = [done]
            more = hop(pieces, "seq", bit)
            (pieces,) = call(
                functools.partial(stack_kernel, len(ties)),
                [sds((2 * pieces.shape[0],) + pieces.shape[1:], BF16)],
                [VMEM] * (len(ties) + 2),
            )(*ties, pieces, more)

    with jax.named_scope("ffn"):
        more = hop(pieces, "seq", 1)
        partial_products = call(
            functools.partial(begin_kernel, near),
            [sds((rows, LANES), F32)] + [sds((rows, hidden_width), F32)] * 2,
            [SMEM] + [VMEM] * 4,
        )(seq_arr, pieces, hop(pieces, "tp", 1), w_gate, w_up)
        (hidden,) = call(
            functools.partial(hidden_kernel, away, features),
            [sds((rows, hidden_width), BF16)],
            [SMEM] + [VMEM] * 7,
        )(seq_arr, more, hop(more, "tp", 1), w_gate, w_up, *partial_products)

        def down(some):
            shape = (len(some), half, width)
            if width % LANES == 0:
                return call(
                    functools.partial(down_kernel, some),
                    [sds(shape, F32), sds(shape, BF16)],
                    [SMEM] + [VMEM] * 2,
                )(seq_arr, hidden, w_down)
            whole = jnp.dot(hidden, w_down, preferred_element_type=F32)
            whole = whole.reshape(rows, n_seq, width).transpose(1, 0, 2)
            whole = jnp.take(whole, seq ^ jnp.array(some, jnp.int32), axis=0)
            return whole[:, :half], whole[:, half:].astype(BF16)

        away_own, away_far = down(away)
        near_own, near_far = down(near)
        shape = (len(away), half, width)
        (msg,) = call(round_kernel, [sds(shape, BF16)], [VMEM] * 2)(
            away_own, hop(away_far, "tp", 1).astype(F32)
        )
        arrived = [hop(near_far, "tp", 1), hop(msg, "seq", 1)]
        keep = near_own
        for bit in seq_bits[1:]:
            shape = (keep.shape[0] // 2, half, width)
            keep, msg = call(fold_kernel, [sds(shape, F32), sds(shape, BF16)], [VMEM] * (1 + len(arrived)))(
                keep, *arrived
            )
            arrived = [hop(msg, "seq", bit)]
        shape = (1, half, width)
        (part,) = call(sum_kernel, [sds(shape, BF16)], [VMEM] * 2)(keep, arrived[0])
        for bit in tp_bits[1:-1]:
            (part,) = call(sum_kernel, [sds(shape, BF16)], [VMEM] * 2)(part, hop(part, "tp", bit))
        (own,) = call(end_kernel, [sds((half, width), BF16)], [VMEM] * 3)(
            mixed, part, hop(part, "tp", tp_bits[-1])
        )
        (result,) = call(join_kernel, [sds(tokens.shape, BF16)], [SMEM] + [VMEM] * 2)(
            core_arr, own, hop(own, "tp", 1)
        )
    return result, keys.reshape(key_cache.shape), values.reshape(value_cache.shape)


def solution(mesh):
    placed = (
        P(None, None, "seq"),
        P("seq"),
        P("seq", "tp"),
        P("seq", "tp"),
        P("seq", "tp"),
        P("tp", "seq"),
        P(),
        P(None, ("seq", "tp")),
        P(None, ("seq", "tp")),
        P(("seq", "tp"), None),
        P(None, "seq", "tp", None),
        P(None, "seq", "tp", None),
        P(),
    )
    return jax.shard_map(
        functools.partial(per_device, mesh.shape["seq"], mesh.shape["tp"]),
        mesh=mesh,
        in_specs=placed,
        out_specs=(P(None, None, "seq"), P(None, "seq", "tp", None), P(None, "seq", "tp", None)),
        check_vma=False,
    )
```

time: 123 us -> 108 us (0.88)
  local copies, waits for them, and re-layouts: 17.5 us -> 2.25 us
  Pallas kernels: 13.3 us -> 20.2 us
  waiting for transfers between devices: 69.1 us -> 62.6 us
  starting transfers between devices: 18.5 us -> 21.9 us
  other arithmetic: 3.63 us -> 0.26 us
    unnamed x22 -> x30, local copies, waits for them, and re-layouts: 16.7 us -> 1.32 us
    pallas_call x7 -> x21, Pallas kernels: 12.6 us -> 19.9 us  [the longest x1 4.03 us: per_device(): call(functools.partial(store_kernel, heads, steps, span), [sds(flat, BF16...]
    ppermute x18 -> x21, waiting for transfers between devices: 69.1 us -> 62.6 us  [hop(): return lax.ppermute(value, axis, [(i, i ^ bit) for i in range(size)])]
    ppermute x18 -> x21, starting transfers between devices: 18.5 us -> 21.9 us  [hop(): return lax.ppermute(value, axis, [(i, i ^ bit) for i in range(size)])]
  transfers between devices with their start and end apart: 18 -> 21, of which waited for: 18 -> 16; matrix products, arithmetic and copies ran while one was open for 1% -> 1% of each run, Pallas kernels for 0% -> 7%
where the time goes in v2:
time: 108 us
  waiting for transfers between devices  62.6 us (58%)
  starting transfers between devices  21.9 us (20%)
  Pallas kernels  20.2 us (19%)
  local copies, waits for them, and re-layouts  2.25 us (2%)
    ppermute x21, waiting for transfers between devices, hop(): return lax.ppermute(value, axis, [(i, i ^ bit) for i in range(size)])  62.6 us
    ppermute x21, starting transfers between devices, hop(): return lax.ppermute(value, axis, [(i, i ^ bit) for i in range(size)])  21.9 us
    pallas_call x1, Pallas kernels, per_device(): call(functools.partial(store_kernel, heads, steps, span), [sds(flat, BF16...  4.03 us
    pallas_call x1, Pallas kernels, per_device(): call(project_kernel, [sds((rows, wide), F32), sds((rows, wide), BF16), sd...  3.43 us
    pallas_call x1, Pallas kernels, per_device(): call(functools.partial(attend_kernel, heads, kv, steps, features, span),...  3.25 us
    pallas_call x2, Pallas kernels, down(): call(functools.partial(down_kernel, some), [sds(shape, F32), sds(shape, B...  2.35 us
  transfers between devices with their start and end apart: 21, of which 16 were waited for; matrix products, arithmetic and copies ran while one was open for 1% of the time, Pallas kernels for 7%

profile of v2, /device:TPU:0, one launch (start us, length us, event | category | flops | bytes accessed | tf_op | source)
XLA Modules:
  0.0 108.1 jit_solution(6942190156988324620)
XLA Ops:
  0.6 3.4 %project.3 = (f32[64,1664]{1,0:T(8,128)}, bf16[64,1664]{1,0:T(8,128)(2,1)}, bf16[2,8,256,128]{3,2,1,0:T(8,128)(2,1)}) custom-call(s32[1]{0:T(128)} %bitcast.2.pair_ref, bf16[4,16,640]{2,1,0:T(8,128)(2,1)} %x_ref.1, bf16[640]{0:T(1024)(128)(2,1)} %gain_hbm.1, bf16[640,1024]{1,0:T(8,128)(2,1)} %wq_hbm.1, bf16[640,256]{1,0:T(8,128)(2,1)} %wk_hbm.1, ...), custom_call_target="tpu_custom_call" | custom-call | flops 3449999872 | bytes 1048576 | tf_op jit(solution)/shard_map/project/pallas_call | solution.py:506
  4.1 4.1 %collective-permute-start = (bf16[64,1664]{1,0:T(8,128)(2,1)}, bf16[64,1664]{1,0:T(8,128)(2,1)S(1)}, u32[]{:S(2)}, u32[]{:S(2)}) collective-permute-start(bf16[64,1664]{1,0:T(8,128)(2,1)} %get-tuple-element.36), channel_id=1, source_target_pairs={{0,16},{4,20},{8,24},{12,28},{16,0},{20,4},{24,8},{28,12},{1,17},{... | collective-permute-start | bytes 638984 | tf_op jit(solution)/shard_map/project/ppermute | solution.py:500
  9.9 8.4 %collective-permute-done.recv_ref = bf16[64,1664]{1,0:T(8,128)(2,1)S(1)} collective-permute-done((bf16[64,1664]{1,0:T(8,128)(2,1)}, bf16[64,1664]{1,0:T(8,128)(2,1)S(1)}, u32[]{:S(2)}, u32[]{:S(2)}) %collective-permute-start) | collective-permute-done | bytes 213024 | tf_op jit(solution)/shard_map/project/ppermute | solution.py:500
  20.4 5.5 %collective-permute-done.1.recv_ref = bf16[64,1664]{1,0:T(8,128)(2,1)S(1)} collective-permute-done((bf16[64,1664]{1,0:T(8,128)(2,1)S(1)}, bf16[64,1664]{1,0:T(8,128)(2,1)S(1)}, u32[]{:S(2)}, u32[]{:S(2)}) %collective-permute-start.1) | collective-permute-done | bytes 213024 | tf_op jit(solution)/shard_map/project/ppermute | solution.py:500
  27.5 7.8 %collective-permute-done.2.recv_ref = bf16[32,1664]{1,0:T(8,128)(2,1)S(1)} collective-permute-done((bf16[32,1664]{1,0:T(8,128)(2,1)S(1)}, bf16[32,1664]{1,0:T(8,128)(2,1)S(1)}, u32[]{:S(2)}, u32[]{:S(2)}) %collective-permute-start.2) | collective-permute-done | bytes 106528 | tf_op jit(solution)/shard_map/project/ppermute | solution.py:500
  35.3 3.2 %attend.3 = (f32[32,1024]{1,0:T(8,128)S(1)}, f32[32,128]{1,0:T(8,128)S(1)}, bf16[32,1152]{1,0:T(8,128)(2,1)S(1)}, bf16[32,512]{1,0:T(8,128)(2,1)S(1)}) custom-call(s32[1]{0:T(128)} %bitcast.1.seq_ref, s32[16]{0:T(128)S(1)} %copy-done.4, f32[32,1664]{1,0:T(8,128)S(1)} %get-tuple-element.39.acc_ref, bf16[32,1664]{1,0:T(8,128)(2,1)S(1)} %collective-permute-done.2.recv_ref, ...), custom_call_target="tpu_custom_call" | custom-call | flops 3449999872 | bytes 1048576 | tf_op jit(solution)/shard_map/attend/pallas_call | solution.py:548
  38.6 1.6 %collective-permute-start.4 = (bf16[32,1152]{1,0:T(8,128)(2,1)S(1)}, bf16[32,1152]{1,0:T(8,128)(2,1)S(1)}, u32[]{:S(2)}, u32[]{:S(2)}) collective-permute-start(bf16[32,1152]{1,0:T(8,128)(2,1)S(1)} %get-tuple-element.44), channel_id=1, source_target_pairs={{0,8},{4,12},{8,0},{12,4},{16,24},{20,28},{24,16},{28,20},{1,9},{5... | collective-permute-start | bytes 221192 | tf_op jit(solution)/shard_map/attend/ppermute | solution.py:500
  40.2 2.8 %collective-permute-done.4.recv_ref = bf16[32,1152]{1,0:T(8,128)(2,1)S(1)} collective-permute-done((bf16[32,1152]{1,0:T(8,128)(2,1)S(1)}, bf16[32,1152]{1,0:T(8,128)(2,1)S(1)}, u32[]{:S(2)}, u32[]{:S(2)}) %collective-permute-start.4) | collective-permute-done | bytes 73760 | tf_op jit(solution)/shard_map/attend/ppermute | solution.py:500
  43.6 4.9 %collective-permute-done.5.recv_ref = bf16[32,1152]{1,0:T(8,128)(2,1)S(1)} collective-permute-done((bf16[32,1152]{1,0:T(8,128)(2,1)S(1)}, bf16[32,1152]{1,0:T(8,128)(2,1)S(1)}, u32[]{:S(2)}, u32[]{:S(2)}) %collective-permute-start.5) | collective-permute-done | bytes 73760 | tf_op jit(solution)/shard_map/attend/ppermute | solution.py:500
  48.8 1.5 %collective-permute-start.6 = (bf16[32,1536]{1,0:T(8,128)(2,1)S(1)}, bf16[32,1536]{1,0:T(8,128)(2,1)}, u32[]{:S(2)}, u32[]{:S(2)}) collective-permute-start(bf16[32,1536]{1,0:T(8,128)(2,1)S(1)} %attend.5.own_ref), channel_id=1, source_target_pairs={{0,4},{4,0},{8,12},{12,8},{16,20},{20,16},{24,28},{28,24},{1,5},{5... | collective-permute-start | bytes 294920 | tf_op jit(solution)/shard_map/attend/ppermute | solution.py:500
  50.3 3.2 %collective-permute-done.6.far_ref = bf16[32,1536]{1,0:T(8,128)(2,1)} collective-permute-done((bf16[32,1536]{1,0:T(8,128)(2,1)S(1)}, bf16[32,1536]{1,0:T(8,128)(2,1)}, u32[]{:S(2)}, u32[]{:S(2)}) %collective-permute-start.6) | collective-permute-done | bytes 98336 | tf_op jit(solution)/shard_map/attend/ppermute | solution.py:500
  56.2 1.6 %collective-permute-start.8 = (bf16[32,640]{1,0:T(8,128)(2,1)S(1)}, bf16[32,640]{1,0:T(8,128)(2,1)S(1)}, u32[]{:S(2)}, u32[]{:S(2)}) collective-permute-start(bf16[32,640]{1,0:T(8,128)(2,1)S(1)} %mix.7.mine_ref), channel_id=1, source_target_pairs={{0,2},{1,3},{2,0},{3,1},{4,6},{5,7},{6,4},{7,5},{8,10},{9,11},{10,... | collective-permute-start | bytes 122888 | tf_op jit(solution)/shard_map/mix/ppermute | solution.py:500
  58.5 1.7 %collective-permute-done.8.recv_ref = bf16[32,640]{1,0:T(8,128)(2,1)S(1)} collective-permute-done((bf16[32,640]{1,0:T(8,128)(2,1)S(1)}, bf16[32,640]{1,0:T(8,128)(2,1)S(1)}, u32[]{:S(2)}, u32[]{:S(2)}) %collective-permute-start.8) | collective-permute-done | bytes 40992 | tf_op jit(solution)/shard_map/mix/ppermute | solution.py:500
  60.9 4.7 %collective-permute-done.9.refs_1_ = bf16[1,32,768]{2,1,0:T(8,128)(2,1)S(1)} collective-permute-done((bf16[1,32,768]{2,1,0:T(8,128)(2,1)S(1)}, bf16[1,32,768]{2,1,0:T(8,128)(2,1)S(1)}, u32[]{:S(2)}, u32[]{:S(2)}) %collective-permute-start.9) | collective-permute-done | bytes 49184 | tf_op jit(solution)/shard_map/mix/ppermute | solution.py:500
  65.7 2.5 %collective-permute-start.10 = (bf16[2,32,768]{2,1,0:T(8,128)(2,1)S(1)}, bf16[2,32,768]{2,1,0:T(8,128)(2,1)S(1)}, u32[]{:S(2)}, u32[]{:S(2)}) collective-permute-start(bf16[2,32,768]{2,1,0:T(8,128)(2,1)S(1)} %mix.9.refs_1_), channel_id=1, source_target_pairs={{0,8},{4,12},{8,0},{12,4},{16,24},{20,28},{24,16},{28,20},{1,9},{5... | collective-permute-start | bytes 294920 | tf_op jit(solution)/shard_map/mix/ppermute | solution.py:500
  68.2 4.0 %mix.10 = (bf16[16,256,128]{2,1,0:T(8,128)(2,1)}, bf16[16,256,128]{2,1,0:T(8,128)(2,1)}, f32[32,128]{1,0:T(8,128)S(1)}) custom-call(s32[1]{0:T(128)} %bitcast.1.seq_ref, s32[16]{0:T(128)S(1)} %copy-done.4, bf16[32,1536]{1,0:T(8,128)(2,1)S(1)} %attend.5.own_ref, bf16[32,1536]{1,0:T(8,128)(2,1)} %collective-permute-done.6.far_ref, ...), custom_call_target="tpu_custom_call" | custom-call | flops 3449999872 | bytes 1048576 | tf_op jit(solution)/shard_map/mix/pallas_call | solution.py:588
  73.4 4.5 %collective-permute-done.11.own_ref = bf16[4,32,768]{2,1,0:T(8,128)(2,1)S(1)} collective-permute-done((bf16[4,32,768]{2,1,0:T(8,128)(2,1)S(1)}, bf16[4,32,768]{2,1,0:T(8,128)(2,1)S(1)}, u32[]{:S(2)}, u32[]{:S(2)}) %collective-permute-start.11) | collective-permute-done | bytes 196640 | tf_op jit(solution)/shard_map/ffn/ppermute | solution.py:500
  78.1 2.0 %ffn.10 = (f32[64,128]{1,0:T(8,128)S(1)}, f32[64,1024]{1,0:T(8,128)S(1)}, f32[64,1024]{1,0:T(8,128)S(1)}) custom-call(s32[1]{0:T(128)} %bitcast.1.seq_ref, bf16[4,32,768]{2,1,0:T(8,128)(2,1)S(1)} %mix.11.own_ref, bf16[4,32,768]{2,1,0:T(8,128)(2,1)S(1)} %collective-permute-done.13.far_ref, bf16[5120,1024]{1,0:T(8,128)(2,1)S(1)} %bitcast.13, ...), custom_call_target="tpu_custom_call" | custom-call | flops 3449999872 | bytes 1048576 | tf_op jit(solution)/shard_map/ffn/pallas_call | solution.py:604
  80.1 2.0 %ffn.11.h_ref = bf16[64,1024]{1,0:T(8,128)(2,1)S(1)} custom-call(s32[1]{0:T(128)} %bitcast.1.seq_ref, bf16[4,32,768]{2,1,0:T(8,128)(2,1)S(1)} %collective-permute-done.11.own_ref, bf16[4,32,768]{2,1,0:T(8,128)(2,1)S(1)} %collective-permute-done.12.far_ref, bf16[5120,1024]{1,0:T(8,128)(2,1)S(1)} %bitcast.13, bf16[5120,1024]{1,0:T(8,128)(2,1)S(1)} %bitcast.15, ...), custom_call_target="tpu_custom_call" | custom-call | flops 3449999872 | bytes 1048576 | tf_op jit(solution)/shard_map/ffn/pallas_call | solution.py:609
  86.7 5.4 %collective-permute-done.16.refs_1_ = bf16[4,32,640]{2,1,0:T(8,128)(2,1)S(1)} collective-permute-done((bf16[4,32,640]{2,1,0:T(8,128)(2,1)S(1)}, bf16[4,32,640]{2,1,0:T(8,128)(2,1)S(1)}, u32[]{:S(2)}, u32[]{:S(2)}) %collective-permute-start.16) | collective-permute-done | bytes 163872 | tf_op jit(solution)/shard_map/ffn/ppermute | solution.py:500
  92.8 3.8 %collective-permute-done.17.refs_0_ = bf16[2,32,640]{2,1,0:T(8,128)(2,1)S(1)} collective-permute-done((bf16[2,32,640]{2,1,0:T(8,128)(2,1)S(1)}, bf16[2,32,640]{2,1,0:T(8,128)(2,1)S(1)}, u32[]{:S(2)}, u32[]{:S(2)}) %collective-permute-start.17) | collective-permute-done | bytes 81952 | tf_op jit(solution)/shard_map/ffn/ppermute | solution.py:500
  97.0 5.1 %collective-permute-done.18.recv_ref = bf16[1,32,640]{2,1,0:T(8,128)(2,1)S(1)} collective-permute-done((bf16[1,32,640]{2,1,0:T(8,128)(2,1)S(1)}, bf16[1,32,640]{2,1,0:T(8,128)(2,1)S(1)}, u32[]{:S(2)}, u32[]{:S(2)}) %collective-permute-start.18) | collective-permute-done | bytes 40992 | tf_op jit(solution)/shard_map/ffn/ppermute | solution.py:500
  102.1 1.8 %collective-permute-start.19 = (bf16[1,32,640]{2,1,0:T(8,128)(2,1)S(1)}, bf16[1,32,640]{2,1,0:T(8,128)(2,1)S(1)}, u32[]{:S(2)}, u32[]{:S(2)}) collective-permute-start(bf16[1,32,640]{2,1,0:T(8,128)(2,1)S(1)} %ffn.17.mine_ref), channel_id=1, source_target_pairs={{0,2},{1,3},{2,0},{3,1},{4,6},{5,7},{6,4},{7,5},{8,10},{9,11},{10,... | collective-permute-start | bytes 122888 | tf_op jit(solution)/shard_map/ffn/ppermute | solution.py:500
  103.9 2.3 %collective-permute-done.19.recv_ref = bf16[1,32,640]{2,1,0:T(8,128)(2,1)S(1)} collective-permute-done((bf16[1,32,640]{2,1,0:T(8,128)(2,1)S(1)}, bf16[1,32,640]{2,1,0:T(8,128)(2,1)S(1)}, u32[]{:S(2)}, u32[]{:S(2)}) %collective-permute-start.19) | collective-permute-done | bytes 40992 | tf_op jit(solution)/shard_map/ffn/ppermute | solution.py:500
  (83 shorter events, 19.3 us)
Async XLA Ops:
  4.1 14.1 %collective-permute-start = (bf16[64,1664]{1,0:T(8,128)(2,1)}, bf16[64,1664]{1,0:T(8,128)(2,1)S(1)}, u32[]{:S(2)}, u32[]{:S(2)}) collective-permute-start(bf16[64,1664]{1,0:T(8,128)(2,1)} %get-tuple-element.36), channel_id=1, source_target_pairs={{0,16},{4,20},{8,24},{12,28},{16,0},{20,4},{24,8},{28,12},{1,17},{... | collective-permute-start | bytes 638984 | tf_op jit(solution)/shard_map/project/ppermute | solution.py:500
  8.2 27.1 %collective-permute-start.3 = (bf16[2,8,256,128]{3,2,1,0:T(8,128)(2,1)}, bf16[2,8,256,128]{3,2,1,0:T(8,128)(2,1)S(1)}, u32[]{:S(2)}, u32[]{:S(2)}) collective-permute-start(bf16[2,8,256,128]{3,2,1,0:T(8,128)(2,1)} %get-tuple-element.41), channel_id=1, source_target_pairs={{0,4},{4,0},{8,12},{12,8},{16,20},{20,16},{24,28},{28,24},{1,5},{5... | collective-permute-start | bytes 3145736 | tf_op jit(solution)/shard_map/project/ppermute | solution.py:500
  19.2 16.1 %copy-start.2 = (bf16[16,128,2,128]{3,2,1,0:T(2,128)(2,1)S(1)}, bf16[16,128,2,128]{3,2,1,0:T(2,128)(2,1)}, u32[]{:S(2)}) copy-start(bf16[16,128,2,128]{3,2,1,0:T(2,128)(2,1)} %param.24) | copy-start | bytes 3145732
  19.4 6.5 %collective-permute-start.1 = (bf16[64,1664]{1,0:T(8,128)(2,1)S(1)}, bf16[64,1664]{1,0:T(8,128)(2,1)S(1)}, u32[]{:S(2)}, u32[]{:S(2)}) collective-permute-start(bf16[64,1664]{1,0:T(8,128)(2,1)S(1)} %get-tuple-element.38), channel_id=1, source_target_pairs={{0,8},{4,12},{8,0},{12,4},{16,24},{20,28},{24,16},{28,20},{1,9},{5... | collective-permute-start | bytes 638984 | tf_op jit(solution)/shard_map/project/ppermute | solution.py:500
  26.1 9.2 %collective-permute-start.2 = (bf16[32,1664]{1,0:T(8,128)(2,1)S(1)}, bf16[32,1664]{1,0:T(8,128)(2,1)S(1)}, u32[]{:S(2)}, u32[]{:S(2)}) collective-permute-start(bf16[32,1664]{1,0:T(8,128)(2,1)S(1)} %get-tuple-element.40), channel_id=1, source_target_pairs={{0,4},{4,0},{8,12},{12,8},{16,20},{20,16},{24,28},{28,24},{1,5},{5... | collective-permute-start | bytes 319496 | tf_op jit(solution)/shard_map/project/ppermute | solution.py:500
  38.6 4.4 %collective-permute-start.4 = (bf16[32,1152]{1,0:T(8,128)(2,1)S(1)}, bf16[32,1152]{1,0:T(8,128)(2,1)S(1)}, u32[]{:S(2)}, u32[]{:S(2)}) collective-permute-start(bf16[32,1152]{1,0:T(8,128)(2,1)S(1)} %get-tuple-element.44), channel_id=1, source_target_pairs={{0,8},{4,12},{8,0},{12,4},{16,24},{20,28},{24,16},{28,20},{1,9},{5... | collective-permute-start | bytes 221192 | tf_op jit(solution)/shard_map/attend/ppermute | solution.py:500
  43.2 5.3 %collective-permute-start.5 = (bf16[32,1152]{1,0:T(8,128)(2,1)S(1)}, bf16[32,1152]{1,0:T(8,128)(2,1)S(1)}, u32[]{:S(2)}, u32[]{:S(2)}) collective-permute-start(bf16[32,1152]{1,0:T(8,128)(2,1)S(1)} %get-tuple-element.47), channel_id=1, source_target_pairs={{0,16},{4,20},{8,24},{12,28},{16,0},{20,4},{24,8},{28,12},{1,17},{... | collective-permute-start | bytes 221192 | tf_op jit(solution)/shard_map/attend/ppermute | solution.py:500
  48.8 4.8 %collective-permute-start.6 = (bf16[32,1536]{1,0:T(8,128)(2,1)S(1)}, bf16[32,1536]{1,0:T(8,128)(2,1)}, u32[]{:S(2)}, u32[]{:S(2)}) collective-permute-start(bf16[32,1536]{1,0:T(8,128)(2,1)S(1)} %attend.5.own_ref), channel_id=1, source_target_pairs={{0,4},{4,0},{8,12},{12,8},{16,20},{20,16},{24,28},{28,24},{1,5},{5... | collective-permute-start | bytes 294920 | tf_op jit(solution)/shard_map/attend/ppermute | solution.py:500
  54.8 1.3 %collective-permute-start.7 = (f32[32,640]{1,0:T(8,128)S(1)}, f32[32,640]{1,0:T(8,128)S(1)}, u32[]{:S(2)}, u32[]{:S(2)}) collective-permute-start(f32[32,640]{1,0:T(8,128)S(1)} %get-tuple-element.50), channel_id=1, source_target_pairs={{0,1},{1,0},{2,3},{3,2},{4,5},{5,4},{6,7},{7,6},{8,9},{9,8},{10,11... | collective-permute-start | bytes 245768 | tf_op jit(solution)/shard_map/mix/ppermute | solution.py:500
  56.2 4.1 %collective-permute-start.8 = (bf16[32,640]{1,0:T(8,128)(2,1)S(1)}, bf16[32,640]{1,0:T(8,128)(2,1)S(1)}, u32[]{:S(2)}, u32[]{:S(2)}) collective-permute-start(bf16[32,640]{1,0:T(8,128)(2,1)S(1)} %mix.7.mine_ref), channel_id=1, source_target_pairs={{0,2},{1,3},{2,0},{3,1},{4,6},{5,7},{6,4},{7,5},{8,10},{9,11},{10,... | collective-permute-start | bytes 122888 | tf_op jit(solution)/shard_map/mix/ppermute | solution.py:500
  60.3 17.7 %slice-start.3 = ((s8[10485760]{0:T(1024)(128)(4,1)}), s8[4194304]{0:T(1024)(128)(4,1)S(1)}, s32[]{:S(2)}) async-start(s8[10485760]{0:T(1024)(128)(4,1)} %bitcast.14), calls=%async_computation.3 | async-start | bytes 8388608
  60.5 17.5 %slice-start.4 = ((s8[10485760]{0:T(1024)(128)(4,1)}), s8[4194304]{0:T(1024)(128)(4,1)S(1)}, s32[]{:S(2)}) async-start(s8[10485760]{0:T(1024)(128)(4,1)} %bitcast.14), calls=%async_computation.4 | async-start | bytes 8388608
  60.5 5.2 %collective-permute-start.9 = (bf16[1,32,768]{2,1,0:T(8,128)(2,1)S(1)}, bf16[1,32,768]{2,1,0:T(8,128)(2,1)S(1)}, u32[]{:S(2)}, u32[]{:S(2)}) collective-permute-start(bf16[1,32,768]{2,1,0:T(8,128)(2,1)S(1)} %get-tuple-element.52.refs_0_), channel_id=1, source_target_pairs={{0,16},{4,20},{8,24},{12,28},{16,0},{20,4},{24,8},{28,12},{1,17},{... | collective-permute-start | bytes 147464 | tf_op jit(solution)/shard_map/mix/ppermute | solution.py:500
  65.7 6.5 %collective-permute-start.10 = (bf16[2,32,768]{2,1,0:T(8,128)(2,1)S(1)}, bf16[2,32,768]{2,1,0:T(8,128)(2,1)S(1)}, u32[]{:S(2)}, u32[]{:S(2)}) collective-permute-start(bf16[2,32,768]{2,1,0:T(8,128)(2,1)S(1)} %mix.9.refs_1_), channel_id=1, source_target_pairs={{0,8},{4,12},{8,0},{12,4},{16,24},{20,28},{24,16},{28,20},{1,9},{5... | collective-permute-start | bytes 294920 | tf_op jit(solution)/shard_map/mix/ppermute | solution.py:500
  72.2 5.7 %collective-permute-start.11 = (bf16[4,32,768]{2,1,0:T(8,128)(2,1)S(1)}, bf16[4,32,768]{2,1,0:T(8,128)(2,1)S(1)}, u32[]{:S(2)}, u32[]{:S(2)}) collective-permute-start(bf16[4,32,768]{2,1,0:T(8,128)(2,1)S(1)} %mix.11.own_ref), channel_id=1, source_target_pairs={{0,4},{4,0},{8,12},{12,8},{16,20},{20,16},{24,28},{28,24},{1,5},{5... | collective-permute-start | bytes 589832 | tf_op jit(solution)/shard_map/ffn/ppermute | solution.py:500
  73.4 4.5 %collective-permute-start.13 = (bf16[4,32,768]{2,1,0:T(8,128)(2,1)S(1)}, bf16[4,32,768]{2,1,0:T(8,128)(2,1)S(1)}, u32[]{:S(2)}, u32[]{:S(2)}) collective-permute-start(bf16[4,32,768]{2,1,0:T(8,128)(2,1)S(1)} %mix.11.own_ref), channel_id=1, source_target_pairs={{0,1},{1,0},{2,3},{3,2},{4,5},{5,4},{6,7},{7,6},{8,9},{9,8},{10,11... | collective-permute-start | bytes 589832 | tf_op jit(solution)/shard_map/ffn/ppermute | solution.py:500
  78.0 2.1 %collective-permute-start.12 = (bf16[4,32,768]{2,1,0:T(8,128)(2,1)S(1)}, bf16[4,32,768]{2,1,0:T(8,128)(2,1)S(1)}, u32[]{:S(2)}, u32[]{:S(2)}) collective-permute-start(bf16[4,32,768]{2,1,0:T(8,128)(2,1)S(1)} %collective-permute-done.11.own_ref), channel_id=1, source_target_pairs={{0,1},{1,0},{2,3},{3,2},{4,5},{5,4},{6,7},{7,6},{8,9},{9,8},{10,11... | collective-permute-start | bytes 589832 | tf_op jit(solution)/shard_map/ffn/ppermute | solution.py:500
  83.5 1.8 %collective-permute-start.15 = (bf16[4,32,640]{2,1,0:T(8,128)(2,1)S(1)}, bf16[4,32,640]{2,1,0:T(8,128)(2,1)S(1)}, u32[]{:S(2)}, u32[]{:S(2)}) collective-permute-start(bf16[4,32,640]{2,1,0:T(8,128)(2,1)S(1)} %get-tuple-element.60), channel_id=1, source_target_pairs={{0,1},{1,0},{2,3},{3,2},{4,5},{5,4},{6,7},{7,6},{8,9},{9,8},{10,11... | collective-permute-start | bytes 491528 | tf_op jit(solution)/shard_map/ffn/ppermute | solution.py:500
  85.2 1.5 %collective-permute-start.14 = (bf16[4,32,640]{2,1,0:T(8,128)(2,1)S(1)}, bf16[4,32,640]{2,1,0:T(8,128)(2,1)S(1)}, u32[]{:S(2)}, u32[]{:S(2)}) collective-permute-start(bf16[4,32,640]{2,1,0:T(8,128)(2,1)S(1)} %get-tuple-element.58), channel_id=1, source_target_pairs={{0,1},{1,0},{2,3},{3,2},{4,5},{5,4},{6,7},{7,6},{8,9},{9,8},{10,11... | collective-permute-start | bytes 491528 | tf_op jit(solution)/shard_map/ffn/ppermute | solution.py:500
  85.4 6.7 %collective-permute-start.16 = (bf16[4,32,640]{2,1,0:T(8,128)(2,1)S(1)}, bf16[4,32,640]{2,1,0:T(8,128)(2,1)S(1)}, u32[]{:S(2)}, u32[]{:S(2)}) collective-permute-start(bf16[4,32,640]{2,1,0:T(8,128)(2,1)S(1)} %ffn.14), channel_id=1, source_target_pairs={{0,4},{4,0},{8,12},{12,8},{16,20},{20,16},{24,28},{28,24},{1,5},{5... | collective-permute-start | bytes 491528 | tf_op jit(solution)/shard_map/ffn/ppermute | solution.py:500
  92.1 4.5 %collective-permute-start.17 = (bf16[2,32,640]{2,1,0:T(8,128)(2,1)S(1)}, bf16[2,32,640]{2,1,0:T(8,128)(2,1)S(1)}, u32[]{:S(2)}, u32[]{:S(2)}) collective-permute-start(bf16[2,32,640]{2,1,0:T(8,128)(2,1)S(1)} %get-tuple-element.62), channel_id=1, source_target_pairs={{0,8},{4,12},{8,0},{12,4},{16,24},{20,28},{24,16},{28,20},{1,9},{5... | collective-permute-start | bytes 245768 | tf_op jit(solution)/shard_map/ffn/ppermute | solution.py:500
  96.7 5.4 %collective-permute-start.18 = (bf16[1,32,640]{2,1,0:T(8,128)(2,1)S(1)}, bf16[1,32,640]{2,1,0:T(8,128)(2,1)S(1)}, u32[]{:S(2)}, u32[]{:S(2)}) collective-permute-start(bf16[1,32,640]{2,1,0:T(8,128)(2,1)S(1)} %get-tuple-element.64), channel_id=1, source_target_pairs={{0,16},{4,20},{8,24},{12,28},{16,0},{20,4},{24,8},{28,12},{1,17},{... | collective-permute-start | bytes 122888 | tf_op jit(solution)/shard_map/ffn/ppermute | solution.py:500
  102.1 4.1 %collective-permute-start.19 = (bf16[1,32,640]{2,1,0:T(8,128)(2,1)S(1)}, bf16[1,32,640]{2,1,0:T(8,128)(2,1)S(1)}, u32[]{:S(2)}, u32[]{:S(2)}) collective-permute-start(bf16[1,32,640]{2,1,0:T(8,128)(2,1)S(1)} %ffn.17.mine_ref), channel_id=1, source_target_pairs={{0,2},{1,3},{2,0},{3,1},{4,6},{5,7},{6,4},{7,5},{8,10},{9,11},{10,... | collective-permute-start | bytes 122888 | tf_op jit(solution)/shard_map/ffn/ppermute | solution.py:500
  106.2 1.3 %collective-permute-start.20 = (bf16[32,640]{1,0:T(8,128)(2,1)S(1)}, bf16[32,640]{1,0:T(8,128)(2,1)S(1)}, u32[]{:S(2)}, u32[]{:S(2)}) collective-permute-start(bf16[32,640]{1,0:T(8,128)(2,1)S(1)} %ffn.18.own_ref), channel_id=1, source_target_pairs={{0,1},{1,0},{2,3},{3,2},{4,5},{5,4},{6,7},{7,6},{8,9},{9,8},{10,11... | collective-permute-start | bytes 122888 | tf_op jit(solution)/shard_map/ffn/ppermute | solution.py:500
  (12 other events, 95.4 us)

commit v3 on v2

v3 whole, which is shorter than its diff:
```python
import functools
import math

import jax
import jax.numpy as jnp
from jax import lax
from jax.experimental import pallas as pl
from jax.experimental.pallas import tpu as pltpu
from jax.sharding import PartitionSpec as P

F32 = jnp.float32
BF16 = jnp.bfloat16
LANES = 128
VMEM = pl.BlockSpec(memory_space=pltpu.VMEM)
SMEM = pl.BlockSpec(memory_space=pltpu.SMEM)
HBM = pl.BlockSpec(memory_space=pltpu.HBM)


def call(body, outs, ins, scratch=(), places=None, cost=3, limit=8):
    return pl.pallas_call(
        body,
        out_shape=outs,
        in_specs=ins,
        out_specs=places or [VMEM] * len(outs),
        scratch_shapes=list(scratch),
        cost_estimate=pl.CostEstimate(flops=int(cost * 1.15e9), bytes_accessed=1 << 20, transcendentals=0),
        compiler_params=pltpu.CompilerParams(vmem_limit_bytes=limit << 20),
    )


def sds(shape, dtype):
    return jax.ShapeDtypeStruct(shape, dtype)


def lane_ids(rows):
    return lax.broadcasted_iota(jnp.int32, (rows, LANES), 1)


def split3(value):
    high = value.astype(BF16)
    rest = value - high.astype(F32)
    mid = rest.astype(BF16)
    low = (rest - mid.astype(F32)).astype(BF16)
    return high, mid, low


def pack_stats(stats):
    high, mid, low = (part.astype(F32) for part in split3(stats))
    return (high + pltpu.roll(mid, 8, 1) + pltpu.roll(low, 16, 1)).astype(BF16)


def unpack_stats(packed):
    packed = packed.astype(F32)
    return (packed + pltpu.roll(packed, LANES - 8, 1)) + pltpu.roll(packed, LANES - 16, 1)


def halves(x):
    steps, requests, _ = x.shape
    cut = requests // 2
    low = jnp.concatenate([x[t, :cut] for t in range(steps)], axis=0)
    high = jnp.concatenate([x[t, cut:] for t in range(steps)], axis=0)
    return low, high


def project_kernel(
    pair_ref, x_hbm, gain_hbm, wq_hbm, wk_hbm, wv_hbm, acc_ref, msg_ref, x_ref, gain_ref, wq_ref, wk_ref, wv_ref, sems
):
    copies = [
        pltpu.make_async_copy(source, target, sems.at[i])
        for i, (source, target) in enumerate(
            (
                (x_hbm, x_ref),
                (gain_hbm, gain_ref),
                (wq_hbm, wq_ref),
                (wk_hbm, wk_ref),
                (wv_hbm, wv_ref),
            )
        )
    ]
    for copy in copies:
        copy.start()
    copies[0].wait()
    copies[1].wait()
    low, high = halves(x_ref[...].astype(F32))
    first = pair_ref[0] == 0
    x = jnp.concatenate([jnp.where(first, low, high), jnp.where(first, high, low)], axis=0)
    half = x.shape[0] // 2
    normed = (x * gain_ref[...].astype(F32)).astype(BF16)
    squares = jnp.sum(x * x, axis=1, keepdims=True)
    at = 0
    for copy, w_ref in zip(copies[2:], (wq_ref, wk_ref, wv_ref)):
        copy.wait()
        width = w_ref.shape[1]
        part = jnp.dot(normed, w_ref[...], preferred_element_type=F32)
        acc_ref[:, at : at + width] = part[:half]
        msg_ref[:, at : at + width] = part[half:].astype(BF16)
        at += width
    stats = jnp.where(lane_ids(2 * half) == 0, squares, 0.0)
    acc_ref[:, at:] = stats[:half]
    msg_ref[:, at:] = pack_stats(stats[half:])


def add_kernel(acc_ref, recv_ref, out_ref, msg_ref):
    at = acc_ref.shape[1] - LANES
    total = acc_ref[:, :at] + recv_ref[:, :at].astype(F32)
    out_ref[:, :at] = total
    msg_ref[:, :at] = total.astype(BF16)
    stats = acc_ref[:, at:] + unpack_stats(recv_ref[:, at:])
    stats = jnp.where(lane_ids(stats.shape[0]) == 0, stats, 0.0)
    out_ref[:, at:] = stats
    msg_ref[:, at:] = pack_stats(stats)


def rotate_kernel(heads, kv, hd, features, acc_ref, recv_ref, cos_ref, sin_ref, out_ref):
    at = (heads + 2 * kv) * hd
    squares = acc_ref[:, at:] + unpack_stats(recv_ref[:, at:])
    scale = lax.rsqrt(squares[:, 0:1] / features + 1e-05)
    for index in range(heads + 2 * kv):
        cols = slice(index * hd, (index + 1) * hd)
        value = (acc_ref[:, cols] + recv_ref[:, cols].astype(F32)) * scale
        if index < heads + kv:
            value = value * cos_ref[...] + pltpu.roll(value, hd // 2, 1) * sin_ref[...]
        out_ref[:, cols] = value.astype(BF16)


def attend_kernel(heads, kv, steps, span, far, seq_ref, len_ref, rows_ref, k_ref, v_ref, *refs):
    if far:
        o_own, st_own, o_ref, st_ref, msg_ref = refs[:5]
    else:
        o_ref, st_ref = refs[:2]
    q_buf, kn_buf, vn_buf, s_buf, o_buf, m_buf, l_buf = refs[-7:]
    requests, rows_kv, hd = k_ref.shape
    cut = requests // 2
    half = steps * cut
    group = heads // kv
    block = steps * heads
    fresh = steps * kv
    seq = seq_ref[0]
    first = seq * span
    pair = seq & 1
    head_request = ((1 - pair) if far else pair) * cut

    def spread(buf, index, place, per_step):
        value = rows_ref[:, index * hd : (index + 1) * hd].astype(F32)
        for t in range(steps):
            buf[pl.ds(t * per_step + place, cut, stride=steps * per_step), :] = value[t * cut : (t + 1) * cut]

    for h in range(heads):
        spread(q_buf, h, h, heads)
    for g in range(kv):
        spread(kn_buf, heads + g, g, kv)
        spread(vn_buf, heads + kv + g, g, kv)
    shrink = hd ** (-0.5)
    queries = q_buf[...].astype(BF16)

    row = lax.broadcasted_iota(jnp.int32, (block, rows_kv), 0)
    col = lax.broadcasted_iota(jnp.int32, (block, rows_kv), 1)
    need = jnp.where((row % heads) // group == col % kv, col // kv, 1 << 29)
    for r in range(cut):
        scores = lax.dot_general(
            queries[r * block : (r + 1) * block],
            k_ref[head_request + r],
            (((1,), (1,)), ((), ())),
            preferred_element_type=F32,
        )
        live = need < len_ref[head_request + r] - first
        s_buf[r * block : (r + 1) * block, :] = jnp.where(live, scores * shrink, -1e30)

    k_new = kn_buf[...].astype(BF16)
    v_new = vn_buf[...].astype(BF16)
    shape = (cut * block, cut * fresh)
    row = lax.broadcasted_iota(jnp.int32, shape, 0)
    col = lax.broadcasted_iota(jnp.int32, shape, 1)
    col_row = lax.broadcasted_iota(jnp.int32, (1, shape[1]), 1)
    at_position = (col_row % fresh) // kv - first
    for r in range(cut):
        at_position += jnp.where(col_row // fresh == r, len_ref[head_request + r], 0)
    held = (at_position >= 0) & (at_position < span)
    new_live = (
        (row // block == col // fresh)
        & ((row % heads) // group == col % kv)
        & ((row % block) // heads >= (col % fresh) // kv)
        & held
    )
    new_scores = lax.dot_general(queries, k_new, (((1,), (1,)), ((), ())), preferred_element_type=F32)
    new_scores = jnp.where(new_live, new_scores * shrink, -1e30)

    scores = s_buf[...]
    top = jnp.maximum(jnp.max(scores, axis=1, keepdims=True), jnp.max(new_scores, axis=1, keepdims=True))
    top = jnp.maximum(top, -1e29)
    expo = jnp.exp(scores - top)
    new_expo = jnp.exp(new_scores - top)
    total = jnp.sum(expo, axis=1, keepdims=True) + jnp.sum(new_expo, axis=1, keepdims=True)
    m_buf[...] = jnp.broadcast_to(top, m_buf.shape)
    l_buf[...] = jnp.broadcast_to(total, l_buf.shape)
    expo = expo.astype(BF16)
    new_part = jnp.dot(new_expo.astype(BF16), v_new, preferred_element_type=F32)
    for r in range(cut):
        mine = slice(r * block, (r + 1) * block)
        o_buf[mine, :] = new_part[mine] + jnp.dot(
            expo[mine], v_ref[head_request + r], preferred_element_type=F32
        )

    lane = lane_ids(cut)
    base = pl.multiple_of((1 - pair) * half, half) if far else 0
    for t in range(steps):
        mine = pl.ds(base + t * cut, cut)
        stats = jnp.zeros((cut, LANES), F32)
        for h in range(heads):
            take = pl.ds(t * heads + h, cut, stride=block)
            o_ref[mine, h * hd : (h + 1) * hd] = o_buf[take, :]
            stats = jnp.where(lane == h, m_buf[take, :], stats)
            stats = jnp.where(lane == 24 + h, l_buf[take, :], stats)
        st_ref[mine, :] = stats
    if far:
        mine = pl.ds(pl.multiple_of(pair * half, half), half)
        o_ref[mine, :] = o_own[...]
        st_ref[mine, :] = st_own[...]
        msg_ref[:, : heads * hd] = o_ref[...].astype(BF16)
        msg_ref[:, heads * hd :] = pack_stats(st_ref[...])


def merged(heads, o_ref, st_ref, recv_ref):
    hd = o_ref.shape[1] // heads
    mine = st_ref[...]
    theirs = unpack_stats(recv_ref[:, heads * hd :])
    top = jnp.maximum(mine, theirs)
    keep, take = jnp.exp(mine - top), jnp.exp(theirs - top)
    total = mine * pltpu.roll(keep, 24, 1) + theirs * pltpu.roll(take, 24, 1)
    lane = lane_ids(mine.shape[0])
    stats = jnp.where(lane < heads, top, jnp.where((lane >= 24) & (lane < 24 + heads), total, 0.0))

    def head(h):
        cols = slice(h * hd, (h + 1) * hd)
        return o_ref[:, cols] * keep[:, h : h + 1] + recv_ref[:, cols].astype(F32) * take[:, h : h + 1]

    return stats, head


def merge_kernel(heads, o_ref, st_ref, recv_ref, o_out, st_out, msg_out):
    stats, head = merged(heads, o_ref, st_ref, recv_ref)
    hd = o_ref.shape[1] // heads
    for h in range(heads):
        value = head(h)
        o_out[:, h * hd : (h + 1) * hd] = value
        msg_out[:, h * hd : (h + 1) * hd] = value.astype(BF16)
    st_out[...] = stats
    msg_out[:, heads * hd :] = pack_stats(stats)


def store_kernel(
    heads, steps, span, seq_ref, len_ref, own_ref, far_ref, k_ref, v_ref, after_ref, k_out, v_out, done_ref, buf, win, sems
):
    done_ref[...] = after_ref[...]
    requests, rows_kv, hd = k_ref.shape
    span_rows = win.shape[2]
    kv = rows_kv // span
    cut = requests // 2
    fresh = steps * kv
    seq = seq_ref[0]
    low = (seq & 1) == 0
    caches = ((k_ref, k_out), (v_ref, v_out))
    whole = [pltpu.make_async_copy(c_ref, c_out, sems.at[i, requests]) for i, (c_ref, c_out) in enumerate(caches)]
    for copy in whole:
        copy.start()
    for i in range(2):
        for g in range(kv):
            at = (heads + i * kv + g) * hd
            own, far = (ref[:, at : at + hd].astype(F32) for ref in (own_ref, far_ref))
            for n, value in enumerate((jnp.where(low, own, far), jnp.where(low, far, own))):
                for t in range(steps):
                    buf[pl.ds((i * 2 + n) * cut * fresh + t * kv + g, cut, stride=fresh), :] = value[
                        t * cut : (t + 1) * cut
                    ]
    line = lax.broadcasted_iota(jnp.int32, (span_rows, hd), 0)
    place = lax.broadcasted_iota(jnp.int32, (span_rows, fresh), 0) - lax.broadcasted_iota(
        jnp.int32, (span_rows, fresh), 1
    )
    pieces = []
    for r in range(requests):
        base = (len_ref[r] - seq * span) * kv
        start = pl.multiple_of(jnp.clip((base // 16) * 16, 0, rows_kv - span_rows), 16)
        touched = (base > -fresh) & (base < rows_kv)
        pieces.append((touched, start))

        @pl.when(touched)
        def _():
            pick = jnp.where(place == base - start, 1.0, 0.0).astype(BF16)
            new = (line >= base - start) & (line < base - start + fresh)
            for i, (c_ref, _) in enumerate(caches):
                at = (i * requests + r) * fresh
                put = jnp.dot(pick, buf[at : at + fresh, :].astype(BF16), preferred_element_type=F32)
                old = c_ref[r, pl.ds(start, span_rows), :].astype(F32)
                win[i, r] = jnp.where(new, put, old).astype(BF16)

    for copy in whole:
        copy.wait()
    for act in ("start", "wait"):
        for r, (touched, start) in enumerate(pieces):

            @pl.when(touched)
            def _():
                for i, (_, c_out) in enumerate(caches):
                    copy = pltpu.make_async_copy(
                        win.at[i, r], c_out.at[r, pl.ds(start, span_rows), :], sems.at[i, r]
                    )
                    getattr(copy, act)()


def mix_kernel(heads, core_ref, o_ref, st_ref, recv_ref, w_ref, done_ref, mine_ref, other_ref, att_buf):
    stats, head = merged(heads, o_ref, st_ref, recv_ref)
    hd = o_ref.shape[1] // heads
    for h in range(heads):
        att_buf[:, h * hd : (h + 1) * hd] = (head(h) / stats[:, 24 + h : 25 + h]).astype(BF16)
    part = jnp.dot(att_buf[...], w_ref[...], preferred_element_type=F32)
    half = part.shape[0] // 2
    low = core_ref[0] == 0
    mine_ref[...] = jnp.where(low, part[:half], part[half:])
    other_ref[...] = jnp.where(low, part[half:], part[:half])


def stack_kernel(*refs):
    *in_refs, out_ref = refs
    at = 0
    for ref in in_refs:
        out_ref[at : at + ref.shape[0]] = ref[...]
        at += ref.shape[0]


def round_kernel(mine_ref, recv_ref, msg_ref):
    msg_ref[...] = (mine_ref[...] + recv_ref[...]).astype(BF16)


def sum_kernel(mine_ref, recv_ref, msg_ref):
    msg_ref[...] = (mine_ref[...].astype(F32) + recv_ref[...].astype(F32)).astype(BF16)


def residual_kernel(core_ref, x_ref, gain_ref, mine_ref, recv_ref, mixed_ref, piece_ref):
    low, high = halves(x_ref[...].astype(F32))
    part = mine_ref[...].astype(F32) + recv_ref[...].astype(F32)
    mixed = jnp.where(core_ref[0] == 0, low, high) + part
    mixed_ref[...] = mixed
    squares = jnp.sum(mixed * mixed, axis=1, keepdims=True)
    stats = jnp.where(lane_ids(mixed.shape[0]) == 0, squares, 0.0)
    piece_ref[0, :, :LANES] = pack_stats(stats)
    piece_ref[0, :, LANES:] = (mixed * gain_ref[...].astype(F32)).astype(BF16)


def gather_products(masks, seq, own_ref, far_ref, wg_ref, wu_ref):
    count, width = own_ref.shape[0], own_ref.shape[2] - LANES
    squares = []
    for ref in (own_ref, far_ref):
        total = unpack_stats(ref[0, :, :LANES])
        for j in range(1, count):
            total += unpack_stats(ref[j, :, :LANES])
        squares.append(total)
    gate = up = 0.0
    for j in range(count):
        take = pl.ds(pl.multiple_of((seq ^ masks[j]) * width, 16), width)
        x = jnp.concatenate([own_ref[j, :, LANES:], far_ref[j, :, LANES:]], axis=0)
        gate += jnp.dot(x, wg_ref[take, :], preferred_element_type=F32)
        up += jnp.dot(x, wu_ref[take, :], preferred_element_type=F32)
    return jnp.concatenate(squares, axis=0), gate, up


def begin_kernel(masks, seq_ref, own_ref, far_ref, wg_ref, wu_ref, sq_ref, gate_ref, up_ref):
    squares, gate, up = gather_products(masks, seq_ref[0], own_ref, far_ref, wg_ref, wu_ref)
    sq_ref[...] = squares
    gate_ref[...] = gate
    up_ref[...] = up


def hidden_kernel(
    masks, features, seq_ref, own_ref, far_ref, wg_ref, wu_ref, sq_ref, gate_ref, up_ref, h_ref
):
    squares, gate, up = gather_products(masks, seq_ref[0], own_ref, far_ref, wg_ref, wu_ref)
    scale = lax.rsqrt((squares + sq_ref[...])[:, 0:1] / features + 1e-05)
    gate = (gate + gate_ref[...]) * scale
    up = (up + up_ref[...]) * scale
    h_ref[...] = (gate / (1.0 + jnp.exp(-gate)) * up).astype(BF16)


def down_kernel(masks, seq_ref, h_ref, w_ref, own_ref, far_ref):
    half, width = own_ref.shape[1:]
    hidden = h_ref[...]
    for j, mask in enumerate(masks):
        take = pl.ds(pl.multiple_of((seq_ref[0] ^ mask) * width, LANES), width)
        part = jnp.dot(hidden, w_ref[:, take], preferred_element_type=F32)
        own_ref[j] = part[:half]
        far_ref[j] = part[half:].astype(BF16)


def fold_kernel(acc_ref, *refs):
    *recv_refs, keep_ref, msg_ref = refs
    count = acc_ref.shape[0] // 2
    for j in range(2 * count):
        total = acc_ref[j]
        for ref in recv_refs:
            total += ref[j].astype(F32)
        if j < count:
            keep_ref[j] = total
        else:
            msg_ref[j - count] = total.astype(BF16)


def end_kernel(mixed_ref, mine_ref, recv_ref, out_ref):
    part = mine_ref[0].astype(F32) + recv_ref[0].astype(F32)
    out_ref[...] = (mixed_ref[...] + part).astype(BF16)


def join_kernel(core_ref, own_ref, far_ref, out_ref):
    steps, requests, _ = out_ref.shape
    cut = requests // 2
    low = core_ref[0] == 0
    own, far = own_ref[...].astype(F32), far_ref[...].astype(F32)
    first, second = jnp.where(low, own, far), jnp.where(low, far, own)
    for t in range(steps):
        rows = slice(t * cut, (t + 1) * cut)
        out_ref[t] = jnp.concatenate([first[rows], second[rows]], axis=0).astype(BF16)


def per_device(
    n_seq,
    n_tp,
    tokens,
    attn_gain,
    w_query,
    w_key,
    w_value,
    w_out,
    ffn_gain,
    w_gate,
    w_up,
    w_down,
    key_cache,
    value_cache,
    lengths,
):
    steps, requests, width = tokens.shape
    span, kv, hd = key_cache.shape[1:]
    heads = w_query.shape[1] // hd
    cut = requests // 2
    half = steps * cut
    features = width * n_seq
    hidden_width = w_gate.shape[1]
    wide = w_query.shape[1] + w_key.shape[1] + w_value.shape[1] + LANES
    seq = lax.axis_index("seq").astype(jnp.int32)
    pair = seq & 1
    core = lax.axis_index("tp").astype(jnp.int32) & 1
    seq_arr, core_arr, pair_arr = seq.reshape(1), core.reshape(1), pair.reshape(1)
    seq_bits = [1 << b for b in range(n_seq.bit_length() - 1)]
    tp_bits = [1 << b for b in range(n_tp.bit_length() - 1)]
    masks = [0]
    for bit in reversed(seq_bits):
        masks = masks + [m ^ bit for m in masks]
    near, away = masks[: n_seq // 2], masks[n_seq // 2 :]

    def hop(value, axis, bit):
        size = n_seq if axis == "seq" else n_tp
        return lax.ppermute(value, axis, [(i, i ^ bit) for i in range(size)])

    flat = (requests, span * kv, hd)
    k_flat, v_flat = key_cache.reshape(flat), value_cache.reshape(flat)
    half_lengths = lax.dynamic_slice_in_dim(lengths, pair * cut, cut, 0)
    positions = (half_lengths[None, :] + jnp.arange(steps, dtype=jnp.int32)[:, None]).reshape(half)
    freqs = jnp.exp(jnp.arange(hd // 2, dtype=F32) * (-2.0 * math.log(100000000.0) / hd))
    angles = positions.astype(F32)[:, None] * freqs[None, :]
    cosine, sine = jnp.cos(angles), jnp.sin(angles)
    cosine = jnp.concatenate([cosine, cosine], axis=1)
    sine = jnp.concatenate([-sine, sine], axis=1)

    rows = 2 * half
    with jax.named_scope("project"):
        sums = [sds((half, wide), F32), sds((half, wide), BF16)]
        acc, msg = call(
            project_kernel,
            sums,
            [SMEM] + [HBM] * 5,
            [
                pltpu.VMEM(tokens.shape, BF16),
                pltpu.VMEM(attn_gain.shape, BF16),
                pltpu.VMEM(w_query.shape, BF16),
                pltpu.VMEM(w_key.shape, BF16),
                pltpu.VMEM(w_value.shape, BF16),
                pltpu.SemaphoreType.DMA((5,)),
            ],
            limit=60,
        )(pair_arr, tokens, attn_gain, w_query, w_key, w_value)
        recv = hop(msg, "seq", 1)
        for bit in seq_bits[1:]:
            acc, msg = call(add_kernel, sums, [VMEM] * 2)(acc, recv)
            recv = hop(msg, "seq", bit)
        (finished,) = call(
            functools.partial(rotate_kernel, heads, kv, hd, features),
            [sds((half, wide - LANES), BF16)],
            [VMEM] * 4,
        )(acc, recv, cosine, sine)
        others = hop(finished, "seq", 1)

    with jax.named_scope("attend"):
        block = steps * heads
        fresh = steps * kv
        joint = [
            sds((rows, heads * hd), F32),
            sds((rows, LANES), F32),
            sds((rows, heads * hd + LANES), BF16),
        ]
        scratch = [
            pltpu.VMEM((cut * block, hd), F32),
            pltpu.VMEM((cut * fresh, hd), F32),
            pltpu.VMEM((cut * fresh, hd), F32),
            pltpu.VMEM((cut * block, flat[1]), F32),
            pltpu.VMEM((cut * block, hd), F32),
            pltpu.VMEM((cut * block, hd), F32),
            pltpu.VMEM((cut * block, hd), F32),
        ]
        own = call(
            functools.partial(attend_kernel, heads, kv, steps, span, False),
            [sds((half, heads * hd), F32), sds((half, LANES), F32)],
            [SMEM, SMEM] + [VMEM] * 3,
            scratch,
        )(seq_arr, lengths, finished, k_flat, v_flat)
        o, st, msg = call(
            functools.partial(attend_kernel, heads, kv, steps, span, True),
            joint,
            [SMEM, SMEM] + [VMEM] * 5,
            scratch,
        )(seq_arr, lengths, others, k_flat, v_flat, *own)
        for bit in seq_bits[:-1]:
            o, st, msg = call(functools.partial(merge_kernel, heads), joint, [VMEM] * 3)(
                o, st, hop(msg, "seq", bit)
            )
        keys, values, done = call(
            functools.partial(store_kernel, heads, steps, span),
            [sds(flat, BF16)] * 2 + [sds((rows, LANES), F32)],
            [SMEM, SMEM] + [VMEM] * 5,
            [
                pltpu.VMEM((2 * requests * fresh, hd), F32),
                pltpu.VMEM((2, requests, 16 + -(-fresh // 16) * 16, hd), BF16),
                pltpu.SemaphoreType.DMA((2, requests + 1)),
            ],
            [HBM, HBM, VMEM],
        )(seq_arr, lengths, finished, others, k_flat, v_flat, st)
        recv = hop(msg, "seq", seq_bits[-1])

    with jax.named_scope("mix"):
        mine, other = call(
            functools.partial(mix_kernel, heads),
            [sds((half, width), F32)] * 2,
            [SMEM] + [VMEM] * 5,
            [pltpu.VMEM((rows, heads * hd), BF16)],
        )(core_arr, o, st, recv, w_out, done)
        (part,) = call(round_kernel, [sds((half, width), BF16)], [VMEM] * 2)(mine, hop(other, "tp", 1))
        for bit in tp_bits[1:-1]:
            (part,) = call(sum_kernel, [sds((half, width), BF16)], [VMEM] * 2)(part, hop(part, "tp", bit))
        gain = lax.dynamic_slice_in_dim(ffn_gain, seq * width, width, 0).reshape(1, width)
        mixed, pieces = call(
            residual_kernel,
            [sds((half, width), F32), sds((1, half, LANES + width), BF16)],
            [SMEM] + [VMEM] * 4,
        )(core_arr, tokens, gain, part, hop(part, "tp", tp_bits[-1]))
        for bit in reversed(seq_bits[1:]):
            more = hop(pieces, "seq", bit)
            (pieces,) = call(
                stack_kernel, [sds((2 * pieces.shape[0],) + pieces.shape[1:], BF16)], [VMEM] * 2
            )(pieces, more)

    with jax.named_scope("ffn"):
        more = hop(pieces, "seq", 1)
        partial_products = call(
            functools.partial(begin_kernel, near),
            [sds((rows, LANES), F32)] + [sds((rows, hidden_width), F32)] * 2,
            [SMEM] + [VMEM] * 4,
        )(seq_arr, pieces, hop(pieces, "tp", 1), w_gate, w_up)
        (hidden,) = call(
            functools.partial(hidden_kernel, away, features),
            [sds((rows, hidden_width), BF16)],
            [SMEM] + [VMEM] * 7,
        )(seq_arr, more, hop(more, "tp", 1), w_gate, w_up, *partial_products)

        def down(some):
            shape = (len(some), half, width)
            if width % LANES == 0:
                return call(
                    functools.partial(down_kernel, some),
                    [sds(shape, F32), sds(shape, BF16)],
                    [SMEM] + [VMEM] * 2,
                )(seq_arr, hidden, w_down)
            whole = jnp.dot(hidden, w_down, preferred_element_type=F32)
            whole = whole.reshape(rows, n_seq, width).transpose(1, 0, 2)
            whole = jnp.take(whole, seq ^ jnp.array(some, jnp.int32), axis=0)
            return whole[:, :half], whole[:, half:].astype(BF16)

        away_own, away_far = down(away)
        near_own, near_far = down(near)
        shape = (len(away), half, width)
        (msg,) = call(round_kernel, [sds(shape, BF16)], [VMEM] * 2)(
            away_own, hop(away_far, "tp", 1).astype(F32)
        )
        arrived = [hop(near_far, "tp", 1), hop(msg, "seq", 1)]
        keep = near_own
        for bit in seq_bits[1:]:
            shape = (keep.shape[0] // 2, half, width)
            keep, msg = call(fold_kernel, [sds(shape, F32), sds(shape, BF16)], [VMEM] * (1 + len(arrived)))(
                keep, *arrived
            )
            arrived = [hop(msg, "seq", bit)]
        shape = (1, half, width)
        (part,) = call(sum_kernel, [sds(shape, BF16)], [VMEM] * 2)(keep, arrived[0])
        for bit in tp_bits[1:-1]:
            (part,) = call(sum_kernel, [sds(shape, BF16)], [VMEM] * 2)(part, hop(part, "tp", bit))
        (own,) = call(end_kernel, [sds((half, width), BF16)], [VMEM] * 3)(
            mixed, part, hop(part, "tp", tp_bits[-1])
        )
        (result,) = call(join_kernel, [sds(tokens.shape, BF16)], [SMEM] + [VMEM] * 2)(
            core_arr, own, hop(own, "tp", 1)
        )
    return result, keys.reshape(key_cache.shape), values.reshape(value_cache.shape)


def solution(mesh):
    placed = (
        P(None, None, "seq"),
        P("seq"),
        P("seq", "tp"),
        P("seq", "tp"),
        P("seq", "tp"),
        P("tp", "seq"),
        P(),
        P(None, ("seq", "tp")),
        P(None, ("seq", "tp")),
        P(("seq", "tp"), None),
        P(None, "seq", "tp", None),
        P(None, "seq", "tp", None),
        P(),
    )
    return jax.shard_map(
        functools.partial(per_device, mesh.shape["seq"], mesh.shape["tp"]),
        mesh=mesh,
        in_specs=placed,
        out_specs=(P(None, None, "seq"), P(None, "seq", "tp", None), P(None, "seq", "tp", None)),
        check_vma=False,
    )
```

time: 108 us -> 101 us (0.935)
  waiting for transfers between devices: 62.6 us -> 49.6 us
  starting transfers between devices: 21.9 us -> 30.6 us
  Pallas kernels: 20.2 us -> 17.7 us
    ppermute x21, waiting for transfers between devices: 62.6 us -> 49.6 us  [hop(): return lax.ppermute(value, axis, [(i, i ^ bit) for i in range(size)])]
    ppermute x21, starting transfers between devices: 21.9 us -> 30.6 us  [hop(): return lax.ppermute(value, axis, [(i, i ^ bit) for i in range(size)])]
    pallas_call x8 -> x9, Pallas kernels: 8.58 us -> 6.97 us  [the longest x1 2.93 us: per_device(): call(project_kernel, sums, [SMEM] + [HBM] * 5, [pltpu.VMEM(tokens.shape,...]
    pallas_call x1, Pallas kernels: 4.03 us -> 2.76 us  [per_device(): call(functools.partial(store_kernel, heads, steps, span), [sds(flat, BF16...]
  transfers between devices with their start and end apart: 21 -> 21, of which waited for: 16 -> 17; matrix products, arithmetic and copies ran while one was open for 1% -> 1% of each run, Pallas kernels for 7% -> 7%
where the time goes in v3:
time: 101 us
  waiting for transfers between devices  49.6 us (49%)
  starting transfers between devices  30.6 us (30%)
  Pallas kernels  17.7 us (18%)
  local copies, waits for them, and re-layouts  2.17 us (2%)
    ppermute x21, waiting for transfers between devices, hop(): return lax.ppermute(value, axis, [(i, i ^ bit) for i in range(size)])  49.6 us
    ppermute x21, starting transfers between devices, hop(): return lax.ppermute(value, axis, [(i, i ^ bit) for i in range(size)])  30.6 us
    pallas_call x1, Pallas kernels, per_device(): call(project_kernel, sums, [SMEM] + [HBM] * 5, [pltpu.VMEM(tokens.shape,...  2.93 us
    pallas_call x1, Pallas kernels, per_device(): call(functools.partial(store_kernel, heads, steps, span), [sds(flat, BF16...  2.76 us
    pallas_call x2, Pallas kernels, down(): call(functools.partial(down_kernel, some), [sds(shape, F32), sds(shape, B...  2.35 us
  transfers between devices with their start and end apart: 21, of which 17 were waited for; matrix products, arithmetic and copies ran while one was open for 1% of the time, Pallas kernels for 7%

profile of v3, /device:TPU:0, one launch (start us, length us, event | category | flops | bytes accessed | tf_op | source)
XLA Modules:
  0.0 101.2 jit_solution(13534865165288264047)
XLA Ops:
  0.6 2.9 %project.4 = (f32[32,1664]{1,0:T(8,128)}, bf16[32,1664]{1,0:T(8,128)(2,1)}) custom-call(s32[1]{0:T(128)} %bitcast.2.pair_ref, bf16[4,16,640]{2,1,0:T(8,128)(2,1)} %x_ref.1, bf16[640]{0:T(1024)(128)(2,1)} %gain_hbm.1, bf16[640,1024]{1,0:T(8,128)(2,1)} %wq_hbm.1, bf16[640,256]{1,0:T(8,128)(2,1)} %wk_hbm.1, bf16[640,256]{1,0:T(8,128)(2,1)} %wv_hbm.1), custom_call_target="tpu_custom_call" | custom-call | flops 3449999872 | bytes 1048576 | tf_op jit(solution)/shard_map/project/pallas_call | solution.py:475
  3.6 3.0 %collective-permute-start = (bf16[32,1664]{1,0:T(8,128)(2,1)}, bf16[32,1664]{1,0:T(8,128)(2,1)S(1)}, u32[]{:S(2)}, u32[]{:S(2)}) collective-permute-start(bf16[32,1664]{1,0:T(8,128)(2,1)} %get-tuple-element.39), channel_id=1, source_target_pairs={{0,4},{4,0},{8,12},{12,8},{16,20},{20,16},{24,28},{28,24},{1,5},{5... | collective-permute-start | bytes 319496 | tf_op jit(solution)/shard_map/project/ppermute | solution.py:460
  6.8 3.0 %collective-permute-done.recv_ref = bf16[32,1664]{1,0:T(8,128)(2,1)S(1)} collective-permute-done((bf16[32,1664]{1,0:T(8,128)(2,1)}, bf16[32,1664]{1,0:T(8,128)(2,1)S(1)}, u32[]{:S(2)}, u32[]{:S(2)}) %collective-permute-start) | collective-permute-done | bytes 106528 | tf_op jit(solution)/shard_map/project/ppermute | solution.py:460
  12.8 2.7 %collective-permute-done.1.recv_ref = bf16[32,1664]{1,0:T(8,128)(2,1)S(1)} collective-permute-done((bf16[32,1664]{1,0:T(8,128)(2,1)S(1)}, bf16[32,1664]{1,0:T(8,128)(2,1)S(1)}, u32[]{:S(2)}, u32[]{:S(2)}) %collective-permute-start.1) | collective-permute-done | bytes 106528 | tf_op jit(solution)/shard_map/project/ppermute | solution.py:460
  15.7 2.9 %collective-permute-start.2 = (bf16[32,1664]{1,0:T(8,128)(2,1)S(1)}, bf16[32,1664]{1,0:T(8,128)(2,1)S(1)}, u32[]{:S(2)}, u32[]{:S(2)}) collective-permute-start(bf16[32,1664]{1,0:T(8,128)(2,1)S(1)} %get-tuple-element.43), channel_id=1, source_target_pairs={{0,16},{4,20},{8,24},{12,28},{16,0},{20,4},{24,8},{28,12},{1,17},{... | collective-permute-start | bytes 319496 | tf_op jit(solution)/shard_map/project/ppermute | solution.py:460
  18.7 2.7 %collective-permute-done.2.recv_ref = bf16[32,1664]{1,0:T(8,128)(2,1)S(1)} collective-permute-done((bf16[32,1664]{1,0:T(8,128)(2,1)S(1)}, bf16[32,1664]{1,0:T(8,128)(2,1)S(1)}, u32[]{:S(2)}, u32[]{:S(2)}) %collective-permute-start.2) | collective-permute-done | bytes 106528 | tf_op jit(solution)/shard_map/project/ppermute | solution.py:460
  21.6 2.9 %collective-permute-start.3 = (bf16[32,1536]{1,0:T(8,128)(2,1)S(1)}, bf16[32,1536]{1,0:T(8,128)(2,1)S(1)}, u32[]{:S(2)}, u32[]{:S(2)}) collective-permute-start(bf16[32,1536]{1,0:T(8,128)(2,1)S(1)} %project.7.rows_ref.own_ref), channel_id=1, source_target_pairs={{0,4},{4,0},{8,12},{12,8},{16,20},{20,16},{24,28},{28,24},{1,5},{5... | collective-permute-start | bytes 294920 | tf_op jit(solution)/shard_map/project/ppermute | solution.py:460
  28.9 2.5 %collective-permute-start.4 = (bf16[64,1152]{1,0:T(8,128)(2,1)S(1)}, bf16[64,1152]{1,0:T(8,128)(2,1)S(1)}, u32[]{:S(2)}, u32[]{:S(2)}) collective-permute-start(bf16[64,1152]{1,0:T(8,128)(2,1)S(1)} %get-tuple-element.48), channel_id=1, source_target_pairs={{0,4},{4,0},{8,12},{12,8},{16,20},{20,16},{24,28},{28,24},{1,5},{5... | collective-permute-start | bytes 442376 | tf_op jit(solution)/shard_map/attend/ppermute | solution.py:460
  31.5 3.1 %collective-permute-done.4.recv_ref = bf16[64,1152]{1,0:T(8,128)(2,1)S(1)} collective-permute-done((bf16[64,1152]{1,0:T(8,128)(2,1)S(1)}, bf16[64,1152]{1,0:T(8,128)(2,1)S(1)}, u32[]{:S(2)}, u32[]{:S(2)}) %collective-permute-start.4) | collective-permute-done | bytes 147488 | tf_op jit(solution)/shard_map/attend/ppermute | solution.py:460
  35.8 4.4 %collective-permute-done.5.recv_ref = bf16[64,1152]{1,0:T(8,128)(2,1)S(1)} collective-permute-done((bf16[64,1152]{1,0:T(8,128)(2,1)S(1)}, bf16[64,1152]{1,0:T(8,128)(2,1)S(1)}, u32[]{:S(2)}, u32[]{:S(2)}) %collective-permute-start.5) | collective-permute-done | bytes 147488 | tf_op jit(solution)/shard_map/attend/ppermute | solution.py:460
  40.6 3.0 %collective-permute-start.6 = (bf16[64,1152]{1,0:T(8,128)(2,1)S(1)}, bf16[64,1152]{1,0:T(8,128)(2,1)S(1)}, u32[]{:S(2)}, u32[]{:S(2)}) collective-permute-start(bf16[64,1152]{1,0:T(8,128)(2,1)S(1)} %get-tuple-element.54), channel_id=1, source_target_pairs={{0,16},{4,20},{8,24},{12,28},{16,0},{20,4},{24,8},{28,12},{1,17},{... | collective-permute-start | bytes 442376 | tf_op jit(solution)/shard_map/attend/ppermute | solution.py:460
  43.5 2.8 %attend.9 = (bf16[16,256,128]{2,1,0:T(8,128)(2,1)}, bf16[16,256,128]{2,1,0:T(8,128)(2,1)}, f32[64,128]{1,0:T(8,128)S(1)}) custom-call(s32[1]{0:T(128)} %bitcast.1.seq_ref, s32[16]{0:T(128)S(1)} %copy-done.4, bf16[32,1536]{1,0:T(8,128)(2,1)S(1)} %project.7.rows_ref.own_ref, bf16[32,1536]{1,0:T(8,128)(2,1)S(1)} %collective-permute-done.3.rows_ref.far_ref, ...), custom_call_target="tpu_custom_call" | custom-call | flops 3449999872 | bytes 1048576 | tf_op jit(solution)/shard_map/attend/pallas_call | solution.py:533
  48.7 4.2 %collective-permute-start.8 = (bf16[32,640]{1,0:T(8,128)(2,1)S(1)}, bf16[32,640]{1,0:T(8,128)(2,1)S(1)}, u32[]{:S(2)}, u32[]{:S(2)}) collective-permute-start(bf16[32,640]{1,0:T(8,128)(2,1)S(1)} %mix.6.mine_ref), channel_id=1, source_target_pairs={{0,2},{1,3},{2,0},{3,1},{4,6},{5,7},{6,4},{7,5},{8,10},{9,11},{10,... | collective-permute-start | bytes 122888 | tf_op jit(solution)/shard_map/mix/ppermute | solution.py:460
  56.0 4.7 %collective-permute-done.9.refs_1_ = bf16[1,32,768]{2,1,0:T(8,128)(2,1)S(1)} collective-permute-done((bf16[1,32,768]{2,1,0:T(8,128)(2,1)S(1)}, bf16[1,32,768]{2,1,0:T(8,128)(2,1)S(1)}, u32[]{:S(2)}, u32[]{:S(2)}) %collective-permute-start.9) | collective-permute-done | bytes 49184 | tf_op jit(solution)/shard_map/mix/ppermute | solution.py:460
  61.2 4.2 %collective-permute-done.10.refs_1_ = bf16[2,32,768]{2,1,0:T(8,128)(2,1)S(1)} collective-permute-done((bf16[2,32,768]{2,1,0:T(8,128)(2,1)S(1)}, bf16[2,32,768]{2,1,0:T(8,128)(2,1)S(1)}, u32[]{:S(2)}, u32[]{:S(2)}) %collective-permute-start.10) | collective-permute-done | bytes 98336 | tf_op jit(solution)/shard_map/mix/ppermute | solution.py:460
  65.4 1.9 %collective-permute-start.11 = (bf16[4,32,768]{2,1,0:T(8,128)(2,1)S(1)}, bf16[4,32,768]{2,1,0:T(8,128)(2,1)S(1)}, u32[]{:S(2)}, u32[]{:S(2)}) collective-permute-start(bf16[4,32,768]{2,1,0:T(8,128)(2,1)S(1)} %mix.9.own_ref), channel_id=1, source_target_pairs={{0,4},{4,0},{8,12},{12,8},{16,20},{20,16},{24,28},{28,24},{1,5},{5... | collective-permute-start | bytes 589832 | tf_op jit(solution)/shard_map/ffn/ppermute | solution.py:460
  67.3 3.8 %collective-permute-done.11.own_ref = bf16[4,32,768]{2,1,0:T(8,128)(2,1)S(1)} collective-permute-done((bf16[4,32,768]{2,1,0:T(8,128)(2,1)S(1)}, bf16[4,32,768]{2,1,0:T(8,128)(2,1)S(1)}, u32[]{:S(2)}, u32[]{:S(2)}) %collective-permute-start.11) | collective-permute-done | bytes 196640 | tf_op jit(solution)/shard_map/ffn/ppermute | solution.py:460
  71.3 2.0 %ffn.10 = (f32[64,128]{1,0:T(8,128)S(1)}, f32[64,1024]{1,0:T(8,128)S(1)}, f32[64,1024]{1,0:T(8,128)S(1)}) custom-call(s32[1]{0:T(128)} %bitcast.1.seq_ref, bf16[4,32,768]{2,1,0:T(8,128)(2,1)S(1)} %mix.9.own_ref, bf16[4,32,768]{2,1,0:T(8,128)(2,1)S(1)} %collective-permute-done.13.far_ref, bf16[5120,1024]{1,0:T(8,128)(2,1)S(1)} %bitcast.8, ...), custom_call_target="tpu_custom_call" | custom-call | flops 3449999872 | bytes 1048576 | tf_op jit(solution)/shard_map/ffn/pallas_call | solution.py:570
  73.3 2.0 %ffn.11.h_ref = bf16[64,1024]{1,0:T(8,128)(2,1)S(1)} custom-call(s32[1]{0:T(128)} %bitcast.1.seq_ref, bf16[4,32,768]{2,1,0:T(8,128)(2,1)S(1)} %collective-permute-done.11.own_ref, bf16[4,32,768]{2,1,0:T(8,128)(2,1)S(1)} %collective-permute-done.12.far_ref, bf16[5120,1024]{1,0:T(8,128)(2,1)S(1)} %bitcast.8, bf16[5120,1024]{1,0:T(8,128)(2,1)S(1)} %bitcast.10, ...), custom_call_target="tpu_custom_call" | custom-call | flops 3449999872 | bytes 1048576 | tf_op jit(solution)/shard_map/ffn/pallas_call | solution.py:575
  78.6 1.9 %collective-permute-start.16 = (bf16[4,32,640]{2,1,0:T(8,128)(2,1)S(1)}, bf16[4,32,640]{2,1,0:T(8,128)(2,1)S(1)}, u32[]{:S(2)}, u32[]{:S(2)}) collective-permute-start(bf16[4,32,640]{2,1,0:T(8,128)(2,1)S(1)} %ffn.14), channel_id=1, source_target_pairs={{0,4},{4,0},{8,12},{12,8},{16,20},{20,16},{24,28},{28,24},{1,5},{5... | collective-permute-start | bytes 491528 | tf_op jit(solution)/shard_map/ffn/ppermute | solution.py:460
  80.5 4.8 %collective-permute-done.16.refs_1_ = bf16[4,32,640]{2,1,0:T(8,128)(2,1)S(1)} collective-permute-done((bf16[4,32,640]{2,1,0:T(8,128)(2,1)S(1)}, bf16[4,32,640]{2,1,0:T(8,128)(2,1)S(1)}, u32[]{:S(2)}, u32[]{:S(2)}) %collective-permute-start.16) | collective-permute-done | bytes 163872 | tf_op jit(solution)/shard_map/ffn/ppermute | solution.py:460
  85.9 4.0 %collective-permute-done.17.refs_0_ = bf16[2,32,640]{2,1,0:T(8,128)(2,1)S(1)} collective-permute-done((bf16[2,32,640]{2,1,0:T(8,128)(2,1)S(1)}, bf16[2,32,640]{2,1,0:T(8,128)(2,1)S(1)}, u32[]{:S(2)}, u32[]{:S(2)}) %collective-permute-start.17) | collective-permute-done | bytes 81952 | tf_op jit(solution)/shard_map/ffn/ppermute | solution.py:460
  91.2 4.0 %collective-permute-done.18.recv_ref = bf16[1,32,640]{2,1,0:T(8,128)(2,1)S(1)} collective-permute-done((bf16[1,32,640]{2,1,0:T(8,128)(2,1)S(1)}, bf16[1,32,640]{2,1,0:T(8,128)(2,1)S(1)}, u32[]{:S(2)}, u32[]{:S(2)}) %collective-permute-start.18) | collective-permute-done | bytes 40992 | tf_op jit(solution)/shard_map/ffn/ppermute | solution.py:460
  96.7 2.5 %collective-permute-done.19.recv_ref = bf16[1,32,640]{2,1,0:T(8,128)(2,1)S(1)} collective-permute-done((bf16[1,32,640]{2,1,0:T(8,128)(2,1)S(1)}, bf16[1,32,640]{2,1,0:T(8,128)(2,1)S(1)}, u32[]{:S(2)}, u32[]{:S(2)}) %collective-permute-start.19) | collective-permute-done | bytes 40992 | tf_op jit(solution)/shard_map/ffn/ppermute | solution.py:460
  (84 shorter events, 24.4 us)
Async XLA Ops:
  3.6 6.2 %collective-permute-start = (bf16[32,1664]{1,0:T(8,128)(2,1)}, bf16[32,1664]{1,0:T(8,128)(2,1)S(1)}, u32[]{:S(2)}, u32[]{:S(2)}) collective-permute-start(bf16[32,1664]{1,0:T(8,128)(2,1)} %get-tuple-element.39), channel_id=1, source_target_pairs={{0,4},{4,0},{8,12},{12,8},{16,20},{20,16},{24,28},{28,24},{1,5},{5... | collective-permute-start | bytes 319496 | tf_op jit(solution)/shard_map/project/ppermute | solution.py:460
  10.8 4.7 %collective-permute-start.1 = (bf16[32,1664]{1,0:T(8,128)(2,1)S(1)}, bf16[32,1664]{1,0:T(8,128)(2,1)S(1)}, u32[]{:S(2)}, u32[]{:S(2)}) collective-permute-start(bf16[32,1664]{1,0:T(8,128)(2,1)S(1)} %get-tuple-element.41), channel_id=1, source_target_pairs={{0,8},{4,12},{8,0},{12,4},{16,24},{20,28},{24,16},{28,20},{1,9},{5... | collective-permute-start | bytes 319496 | tf_op jit(solution)/shard_map/project/ppermute | solution.py:460
  15.7 5.6 %collective-permute-start.2 = (bf16[32,1664]{1,0:T(8,128)(2,1)S(1)}, bf16[32,1664]{1,0:T(8,128)(2,1)S(1)}, u32[]{:S(2)}, u32[]{:S(2)}) collective-permute-start(bf16[32,1664]{1,0:T(8,128)(2,1)S(1)} %get-tuple-element.43), channel_id=1, source_target_pairs={{0,16},{4,20},{8,24},{12,28},{16,0},{20,4},{24,8},{28,12},{1,17},{... | collective-permute-start | bytes 319496 | tf_op jit(solution)/shard_map/project/ppermute | solution.py:460
  21.6 5.9 %collective-permute-start.3 = (bf16[32,1536]{1,0:T(8,128)(2,1)S(1)}, bf16[32,1536]{1,0:T(8,128)(2,1)S(1)}, u32[]{:S(2)}, u32[]{:S(2)}) collective-permute-start(bf16[32,1536]{1,0:T(8,128)(2,1)S(1)} %project.7.rows_ref.own_ref), channel_id=1, source_target_pairs={{0,4},{4,0},{8,12},{12,8},{16,20},{20,16},{24,28},{28,24},{1,5},{5... | collective-permute-start | bytes 294920 | tf_op jit(solution)/shard_map/project/ppermute | solution.py:460
  28.9 5.7 %collective-permute-start.4 = (bf16[64,1152]{1,0:T(8,128)(2,1)S(1)}, bf16[64,1152]{1,0:T(8,128)(2,1)S(1)}, u32[]{:S(2)}, u32[]{:S(2)}) collective-permute-start(bf16[64,1152]{1,0:T(8,128)(2,1)S(1)} %get-tuple-element.48), channel_id=1, source_target_pairs={{0,4},{4,0},{8,12},{12,8},{16,20},{20,16},{24,28},{28,24},{1,5},{5... | collective-permute-start | bytes 442376 | tf_op jit(solution)/shard_map/attend/ppermute | solution.py:460
  34.9 5.3 %collective-permute-start.5 = (bf16[64,1152]{1,0:T(8,128)(2,1)S(1)}, bf16[64,1152]{1,0:T(8,128)(2,1)S(1)}, u32[]{:S(2)}, u32[]{:S(2)}) collective-permute-start(bf16[64,1152]{1,0:T(8,128)(2,1)S(1)} %get-tuple-element.51), channel_id=1, source_target_pairs={{0,8},{4,12},{8,0},{12,4},{16,24},{20,28},{24,16},{28,20},{1,9},{5... | collective-permute-start | bytes 442376 | tf_op jit(solution)/shard_map/attend/ppermute | solution.py:460
  40.6 6.1 %collective-permute-start.6 = (bf16[64,1152]{1,0:T(8,128)(2,1)S(1)}, bf16[64,1152]{1,0:T(8,128)(2,1)S(1)}, u32[]{:S(2)}, u32[]{:S(2)}) collective-permute-start(bf16[64,1152]{1,0:T(8,128)(2,1)S(1)} %get-tuple-element.54), channel_id=1, source_target_pairs={{0,16},{4,20},{8,24},{12,28},{16,0},{20,4},{24,8},{28,12},{1,17},{... | collective-permute-start | bytes 442376 | tf_op jit(solution)/shard_map/attend/ppermute | solution.py:460
  47.3 1.3 %collective-permute-start.7 = (f32[32,640]{1,0:T(8,128)S(1)}, f32[32,640]{1,0:T(8,128)S(1)}, u32[]{:S(2)}, u32[]{:S(2)}) collective-permute-start(f32[32,640]{1,0:T(8,128)S(1)} %get-tuple-element.57), channel_id=1, source_target_pairs={{0,1},{1,0},{2,3},{3,2},{4,5},{5,4},{6,7},{7,6},{8,9},{9,8},{10,11... | collective-permute-start | bytes 245768 | tf_op jit(solution)/shard_map/mix/ppermute | solution.py:460
  48.7 6.2 %collective-permute-start.8 = (bf16[32,640]{1,0:T(8,128)(2,1)S(1)}, bf16[32,640]{1,0:T(8,128)(2,1)S(1)}, u32[]{:S(2)}, u32[]{:S(2)}) collective-permute-start(bf16[32,640]{1,0:T(8,128)(2,1)S(1)} %mix.6.mine_ref), channel_id=1, source_target_pairs={{0,2},{1,3},{2,0},{3,1},{4,6},{5,7},{6,4},{7,5},{8,10},{9,11},{10,... | collective-permute-start | bytes 122888 | tf_op jit(solution)/shard_map/mix/ppermute | solution.py:460
  53.7 17.5 %slice-start.3 = ((s8[10485760]{0:T(1024)(128)(4,1)}), s8[4194304]{0:T(1024)(128)(4,1)S(1)}, s32[]{:S(2)}) async-start(s8[10485760]{0:T(1024)(128)(4,1)} %bitcast.9), calls=%async_computation.3 | async-start | bytes 8388608
  53.7 17.5 %slice-start.4 = ((s8[10485760]{0:T(1024)(128)(4,1)}), s8[4194304]{0:T(1024)(128)(4,1)S(1)}, s32[]{:S(2)}) async-start(s8[10485760]{0:T(1024)(128)(4,1)} %bitcast.9), calls=%async_computation.4 | async-start | bytes 8388608
  55.1 16.1 %slice-start.5 = ((s8[10485760]{0:T(1024)(128)(4,1)}), s8[2097152]{0:T(1024)(128)(4,1)S(1)}, s32[]{:S(2)}) async-start(s8[10485760]{0:T(1024)(128)(4,1)} %bitcast.9), calls=%async_computation.5 | async-start | bytes 4194304
  55.1 5.6 %collective-permute-start.9 = (bf16[1,32,768]{2,1,0:T(8,128)(2,1)S(1)}, bf16[1,32,768]{2,1,0:T(8,128)(2,1)S(1)}, u32[]{:S(2)}, u32[]{:S(2)}) collective-permute-start(bf16[1,32,768]{2,1,0:T(8,128)(2,1)S(1)} %get-tuple-element.59.refs_0_), channel_id=1, source_target_pairs={{0,16},{4,20},{8,24},{12,28},{16,0},{20,4},{24,8},{28,12},{1,17},{... | collective-permute-start | bytes 147464 | tf_op jit(solution)/shard_map/mix/ppermute | solution.py:460
  60.7 4.7 %collective-permute-start.10 = (bf16[2,32,768]{2,1,0:T(8,128)(2,1)S(1)}, bf16[2,32,768]{2,1,0:T(8,128)(2,1)S(1)}, u32[]{:S(2)}, u32[]{:S(2)}) collective-permute-start(bf16[2,32,768]{2,1,0:T(8,128)(2,1)S(1)} %mix.8.refs_0_), channel_id=1, source_target_pairs={{0,8},{4,12},{8,0},{12,4},{16,24},{20,28},{24,16},{28,20},{1,9},{5... | collective-permute-start | bytes 294920 | tf_op jit(solution)/shard_map/mix/ppermute | solution.py:460
  65.4 5.7 %collective-permute-start.11 = (bf16[4,32,768]{2,1,0:T(8,128)(2,1)S(1)}, bf16[4,32,768]{2,1,0:T(8,128)(2,1)S(1)}, u32[]{:S(2)}, u32[]{:S(2)}) collective-permute-start(bf16[4,32,768]{2,1,0:T(8,128)(2,1)S(1)} %mix.9.own_ref), channel_id=1, source_target_pairs={{0,4},{4,0},{8,12},{12,8},{16,20},{20,16},{24,28},{28,24},{1,5},{5... | collective-permute-start | bytes 589832 | tf_op jit(solution)/shard_map/ffn/ppermute | solution.py:460
  67.3 3.9 %collective-permute-start.13 = (bf16[4,32,768]{2,1,0:T(8,128)(2,1)S(1)}, bf16[4,32,768]{2,1,0:T(8,128)(2,1)S(1)}, u32[]{:S(2)}, u32[]{:S(2)}) collective-permute-start(bf16[4,32,768]{2,1,0:T(8,128)(2,1)S(1)} %mix.9.own_ref), channel_id=1, source_target_pairs={{0,1},{1,0},{2,3},{3,2},{4,5},{5,4},{6,7},{7,6},{8,9},{9,8},{10,11... | collective-permute-start | bytes 589832 | tf_op jit(solution)/shard_map/ffn/ppermute | solution.py:460
  71.1 2.1 %collective-permute-start.12 = (bf16[4,32,768]{2,1,0:T(8,128)(2,1)S(1)}, bf16[4,32,768]{2,1,0:T(8,128)(2,1)S(1)}, u32[]{:S(2)}, u32[]{:S(2)}) collective-permute-start(bf16[4,32,768]{2,1,0:T(8,128)(2,1)S(1)} %collective-permute-done.11.own_ref), channel_id=1, source_target_pairs={{0,1},{1,0},{2,3},{3,2},{4,5},{5,4},{6,7},{7,6},{8,9},{9,8},{10,11... | collective-permute-start | bytes 589832 | tf_op jit(solution)/shard_map/ffn/ppermute | solution.py:460
  76.7 1.8 %collective-permute-start.15 = (bf16[4,32,640]{2,1,0:T(8,128)(2,1)S(1)}, bf16[4,32,640]{2,1,0:T(8,128)(2,1)S(1)}, u32[]{:S(2)}, u32[]{:S(2)}) collective-permute-start(bf16[4,32,640]{2,1,0:T(8,128)(2,1)S(1)} %get-tuple-element.66), channel_id=1, source_target_pairs={{0,1},{1,0},{2,3},{3,2},{4,5},{5,4},{6,7},{7,6},{8,9},{9,8},{10,11... | collective-permute-start | bytes 491528 | tf_op jit(solution)/shard_map/ffn/ppermute | solution.py:460
  78.4 2.0 %collective-permute-start.14 = (bf16[4,32,640]{2,1,0:T(8,128)(2,1)S(1)}, bf16[4,32,640]{2,1,0:T(8,128)(2,1)S(1)}, u32[]{:S(2)}, u32[]{:S(2)}) collective-permute-start(bf16[4,32,640]{2,1,0:T(8,128)(2,1)S(1)} %get-tuple-element.64), channel_id=1, source_target_pairs={{0,1},{1,0},{2,3},{3,2},{4,5},{5,4},{6,7},{7,6},{8,9},{9,8},{10,11... | collective-permute-start | bytes 491528 | tf_op jit(solution)/shard_map/ffn/ppermute | solution.py:460
  78.6 6.7 %collective-permute-start.16 = (bf16[4,32,640]{2,1,0:T(8,128)(2,1)S(1)}, bf16[4,32,640]{2,1,0:T(8,128)(2,1)S(1)}, u32[]{:S(2)}, u32[]{:S(2)}) collective-permute-start(bf16[4,32,640]{2,1,0:T(8,128)(2,1)S(1)} %ffn.14), channel_id=1, source_target_pairs={{0,4},{4,0},{8,12},{12,8},{16,20},{20,16},{24,28},{28,24},{1,5},{5... | collective-permute-start | bytes 491528 | tf_op jit(solution)/shard_map/ffn/ppermute | solution.py:460
  85.4 4.5 %collective-permute-start.17 = (bf16[2,32,640]{2,1,0:T(8,128)(2,1)S(1)}, bf16[2,32,640]{2,1,0:T(8,128)(2,1)S(1)}, u32[]{:S(2)}, u32[]{:S(2)}) collective-permute-start(bf16[2,32,640]{2,1,0:T(8,128)(2,1)S(1)} %get-tuple-element.68), channel_id=1, source_target_pairs={{0,8},{4,12},{8,0},{12,4},{16,24},{20,28},{24,16},{28,20},{1,9},{5... | collective-permute-start | bytes 245768 | tf_op jit(solution)/shard_map/ffn/ppermute | solution.py:460
  89.9 5.2 %collective-permute-start.18 = (bf16[1,32,640]{2,1,0:T(8,128)(2,1)S(1)}, bf16[1,32,640]{2,1,0:T(8,128)(2,1)S(1)}, u32[]{:S(2)}, u32[]{:S(2)}) collective-permute-start(bf16[1,32,640]{2,1,0:T(8,128)(2,1)S(1)} %get-tuple-element.70), channel_id=1, source_target_pairs={{0,16},{4,20},{8,24},{12,28},{16,0},{20,4},{24,8},{28,12},{1,17},{... | collective-permute-start | bytes 122888 | tf_op jit(solution)/shard_map/ffn/ppermute | solution.py:460
  95.2 4.1 %collective-permute-start.19 = (bf16[1,32,640]{2,1,0:T(8,128)(2,1)S(1)}, bf16[1,32,640]{2,1,0:T(8,128)(2,1)S(1)}, u32[]{:S(2)}, u32[]{:S(2)}) collective-permute-start(bf16[1,32,640]{2,1,0:T(8,128)(2,1)S(1)} %ffn.17.mine_ref), channel_id=1, source_target_pairs={{0,2},{1,3},{2,0},{3,1},{4,6},{5,7},{6,4},{7,5},{8,10},{9,11},{10,... | collective-permute-start | bytes 122888 | tf_op jit(solution)/shard_map/ffn/ppermute | solution.py:460
  99.3 1.3 %collective-permute-start.20 = (bf16[32,640]{1,0:T(8,128)(2,1)S(1)}, bf16[32,640]{1,0:T(8,128)(2,1)S(1)}, u32[]{:S(2)}, u32[]{:S(2)}) collective-permute-start(bf16[32,640]{1,0:T(8,128)(2,1)S(1)} %ffn.18.own_ref), channel_id=1, source_target_pairs={{0,1},{1,0},{2,3},{3,2},{4,5},{5,4},{6,7},{7,6},{8,9},{9,8},{10,11... | collective-permute-start | bytes 122888 | tf_op jit(solution)/shard_map/ffn/ppermute | solution.py:460
  (12 other events, 92.5 us)

commit v4 on v3

v4 whole, which is shorter than its diff:
```python
import functools
import math

import jax
import jax.numpy as jnp
from jax import lax
from jax.experimental import pallas as pl
from jax.experimental.pallas import tpu as pltpu
from jax.sharding import PartitionSpec as P

F32 = jnp.float32
BF16 = jnp.bfloat16
LANES = 128
VMEM = pl.BlockSpec(memory_space=pltpu.VMEM)
SMEM = pl.BlockSpec(memory_space=pltpu.SMEM)
HBM = pl.BlockSpec(memory_space=pltpu.HBM)


def call(body, outs, ins, scratch=(), places=None, cost=3, limit=8):
    return pl.pallas_call(
        body,
        out_shape=outs,
        in_specs=ins,
        out_specs=places or [VMEM] * len(outs),
        scratch_shapes=list(scratch),
        cost_estimate=pl.CostEstimate(flops=int(cost * 1.15e9), bytes_accessed=1 << 20, transcendentals=0),
        compiler_params=pltpu.CompilerParams(vmem_limit_bytes=int(limit * 2**20)),
    )


def sds(shape, dtype):
    return jax.ShapeDtypeStruct(shape, dtype)


def lane_ids(rows):
    return lax.broadcasted_iota(jnp.int32, (rows, LANES), 1)


def split3(value):
    high = value.astype(BF16)
    rest = value - high.astype(F32)
    mid = rest.astype(BF16)
    low = (rest - mid.astype(F32)).astype(BF16)
    return high, mid, low


def pack_stats(stats):
    high, mid, low = (part.astype(F32) for part in split3(stats))
    return (high + pltpu.roll(mid, 8, 1) + pltpu.roll(low, 16, 1)).astype(BF16)


def unpack_stats(packed):
    packed = packed.astype(F32)
    return (packed + pltpu.roll(packed, LANES - 8, 1)) + pltpu.roll(packed, LANES - 16, 1)


def reorder(rows, source, x):
    shape = (rows, x.shape[0])
    row = lax.broadcasted_iota(jnp.int32, shape, 0)
    col = lax.broadcasted_iota(jnp.int32, shape, 1)
    pick = jnp.where(col == source(row), 1.0, 0.0).astype(BF16)
    return jnp.dot(pick, x, preferred_element_type=F32)


def project_kernel(
    steps,
    seq_ref,
    x_hbm,
    gain_hbm,
    wq_hbm,
    wk_hbm,
    wv_hbm,
    acc_ref,
    msg1_ref,
    msg2_ref,
    msg3_ref,
    x_ref,
    gain_ref,
    wq_ref,
    wk_ref,
    wv_ref,
    sems,
):
    copies = [
        pltpu.make_async_copy(source, target, sems.at[i])
        for i, (source, target) in enumerate(
            (
                (x_hbm, x_ref),
                (gain_hbm, gain_ref),
                (wq_hbm, wq_ref),
                (wk_hbm, wk_ref),
                (wv_hbm, wv_ref),
            )
        )
    ]
    for copy in copies:
        copy.start()
    copies[0].wait()
    copies[1].wait()
    rows = x_ref.shape[0]
    requests = rows // steps
    cut = requests // 4
    part = rows // 4
    place = seq_ref[0] & 3

    def source(row):
        return row % steps * requests + ((row // part) ^ place) * cut + row % part // steps

    x = reorder(rows, source, x_ref[...])
    normed = (x * gain_ref[...].astype(F32)).astype(BF16)
    squares = jnp.sum(x * x, axis=1, keepdims=True)
    msgs = (msg1_ref, msg2_ref, msg3_ref)
    at = 0
    for copy, w_ref in zip(copies[2:], (wq_ref, wk_ref, wv_ref)):
        copy.wait()
        width = w_ref.shape[1]
        product = jnp.dot(normed, w_ref[...], preferred_element_type=F32)
        acc_ref[:, at : at + width] = product[:part]
        for j, ref in enumerate(msgs):
            ref[:, at : at + width] = product[(j + 1) * part : (j + 2) * part].astype(BF16)
        at += width
    stats = jnp.where(lane_ids(rows) == 0, squares, 0.0)
    acc_ref[:, at:] = stats[:part]
    packed = pack_stats(stats)
    for j, ref in enumerate(msgs):
        ref[:, at:] = packed[(j + 1) * part : (j + 2) * part]


def keep_kernel(in_ref, out_ref):
    out_ref[...] = in_ref[...]


def add_kernel(acc_ref, *refs):
    *recv_refs, out_ref, msg_ref = refs
    at = acc_ref.shape[1] - LANES
    total, stats = acc_ref[:, :at], acc_ref[:, at:]
    for ref in recv_refs:
        total += ref[:, :at].astype(F32)
        stats += unpack_stats(ref[:, at:])
    stats = jnp.where(lane_ids(stats.shape[0]) == 0, stats, 0.0)
    out_ref[:, :at] = total
    msg_ref[:, :at] = total.astype(BF16)
    out_ref[:, at:] = stats
    msg_ref[:, at:] = pack_stats(stats)


def rotate_kernel(heads, kv, hd, features, acc_ref, recv_ref, cos_ref, sin_ref, out_ref):
    at = (heads + 2 * kv) * hd
    squares = acc_ref[:, at:] + unpack_stats(recv_ref[:, at:])
    scale = lax.rsqrt(squares[:, 0:1] / features + 1e-05)
    for index in range(heads + 2 * kv):
        cols = slice(index * hd, (index + 1) * hd)
        value = (acc_ref[:, cols] + recv_ref[:, cols].astype(F32)) * scale
        if index < heads + kv:
            value = value * cos_ref[...] + pltpu.roll(value, hd // 2, 1) * sin_ref[...]
        out_ref[:, cols] = value.astype(BF16)


def attend_kernel(heads, kv, steps, span, slot, seq_ref, len_ref, rows_ref, k_ref, v_ref, *refs):
    q_buf, kn_buf, vn_buf, s_buf, o_buf, m_buf, l_buf, o_all, st_all = refs[-9:]
    if slot == 0:
        o_all, st_all = refs[:2]
    requests, rows_kv, hd = k_ref.shape
    cut = requests // 4
    group = heads // kv
    block = steps * heads
    fresh = steps * kv
    seq = seq_ref[0]
    first = seq * span
    head_request = ((seq & 3) ^ slot) * cut

    def spread(buf, index, place, per_step):
        value = rows_ref[:, index * hd : (index + 1) * hd].astype(F32)
        buf[pl.ds(place, cut * steps, stride=per_step), :] = value

    for h in range(heads):
        spread(q_buf, h, h, heads)
    for g in range(kv):
        spread(kn_buf, heads + g, g, kv)
        spread(vn_buf, heads + kv + g, g, kv)
    shrink = hd ** (-0.5)
    queries = q_buf[...].astype(BF16)

    row = lax.broadcasted_iota(jnp.int32, (block, rows_kv), 0)
    col = lax.broadcasted_iota(jnp.int32, (block, rows_kv), 1)
    need = jnp.where((row % heads) // group == col % kv, col // kv, 1 << 29)
    for r in range(cut):
        scores = lax.dot_general(
            queries[r * block : (r + 1) * block],
            k_ref[head_request + r],
            (((1,), (1,)), ((), ())),
            preferred_element_type=F32,
        )
        live = need < len_ref[head_request + r] - first
        s_buf[r * block : (r + 1) * block, :] = jnp.where(live, scores * shrink, -1e30)

    k_new = kn_buf[...].astype(BF16)
    v_new = vn_buf[...].astype(BF16)
    shape = (cut * block, cut * fresh)
    row = lax.broadcasted_iota(jnp.int32, shape, 0)
    col = lax.broadcasted_iota(jnp.int32, shape, 1)
    col_row = lax.broadcasted_iota(jnp.int32, (1, shape[1]), 1)
    at_position = (col_row % fresh) // kv - first
    for r in range(cut):
        at_position += jnp.where(col_row // fresh == r, len_ref[head_request + r], 0)
    held = (at_position >= 0) & (at_position < span)
    new_live = (
        (row // block == col // fresh)
        & ((row % heads) // group == col % kv)
        & ((row % block) // heads >= (col % fresh) // kv)
        & held
    )
    new_scores = lax.dot_general(queries, k_new, (((1,), (1,)), ((), ())), preferred_element_type=F32)
    new_scores = jnp.where(new_live, new_scores * shrink, -1e30)

    scores = s_buf[...]
    top = jnp.maximum(jnp.max(scores, axis=1, keepdims=True), jnp.max(new_scores, axis=1, keepdims=True))
    top = jnp.maximum(top, -1e29)
    expo = jnp.exp(scores - top)
    new_expo = jnp.exp(new_scores - top)
    total = jnp.sum(expo, axis=1, keepdims=True) + jnp.sum(new_expo, axis=1, keepdims=True)
    m_buf[...] = jnp.broadcast_to(top, m_buf.shape)
    l_buf[...] = jnp.broadcast_to(total, l_buf.shape)
    expo = expo.astype(BF16)
    new_part = jnp.dot(new_expo.astype(BF16), v_new, preferred_element_type=F32)
    for r in range(cut):
        mine = slice(r * block, (r + 1) * block)
        o_buf[mine, :] = new_part[mine] + jnp.dot(
            expo[mine], v_ref[head_request + r], preferred_element_type=F32
        )

    lane = lane_ids(cut * steps)
    stats = jnp.zeros((cut * steps, LANES), F32)
    for h in range(heads):
        take = pl.ds(h, cut * steps, stride=heads)
        o_all[:, h * hd : (h + 1) * hd] = o_buf[take, :]
        stats = jnp.where(lane == h, m_buf[take, :], stats)
        stats = jnp.where(lane == 24 + h, l_buf[take, :], stats)
    st_all[...] = stats
    if slot != 0:
        msg_ref = refs[0]
        msg_ref[:, : heads * hd] = o_all[...].astype(BF16)
        msg_ref[:, heads * hd :] = pack_stats(st_all[...])


def merged(heads, o_ref, st_ref, recv_refs):
    hd = o_ref.shape[1] // heads
    stats = [st_ref[...]] + [unpack_stats(ref[:, heads * hd :]) for ref in recv_refs]
    top = functools.reduce(jnp.maximum, stats)
    factors = [jnp.exp(one - top) for one in stats]
    total = sum(one * pltpu.roll(factor, 24, 1) for one, factor in zip(stats, factors))
    lane = lane_ids(top.shape[0])
    joint = jnp.where(lane < heads, top, jnp.where((lane >= 24) & (lane < 24 + heads), total, 0.0))

    def head(h):
        cols = slice(h * hd, (h + 1) * hd)
        value = o_ref[:, cols] * factors[0][:, h : h + 1]
        for ref, factor in zip(recv_refs, factors[1:]):
            value += ref[:, cols].astype(F32) * factor[:, h : h + 1]
        return value

    return joint, head


def merge_kernel(heads, o_ref, st_ref, *refs):
    *recv_refs, o_out, st_out, msg_out = refs
    stats, head = merged(heads, o_ref, st_ref, recv_refs)
    hd = o_ref.shape[1] // heads
    for h in range(heads):
        value = head(h)
        o_out[:, h * hd : (h + 1) * hd] = value
        msg_out[:, h * hd : (h + 1) * hd] = value.astype(BF16)
    st_out[...] = stats
    msg_out[:, heads * hd :] = pack_stats(stats)


def finish_kernel(heads, o_ref, st_ref, recv_ref, after_ref, att_ref, done_ref):
    stats, head = merged(heads, o_ref, st_ref, [recv_ref])
    done_ref[...] = after_ref[...]
    hd = o_ref.shape[1] // heads
    for h in range(heads):
        att_ref[:, h * hd : (h + 1) * hd] = (head(h) / stats[:, 24 + h : 25 + h]).astype(BF16)


def store_kernel(column, steps, span, seq_ref, len_ref, *refs):
    slot_refs, (c_ref, after_ref, c_out, done_ref, buf, win, sems) = refs[:4], refs[4:]
    done_ref[...] = after_ref[...]
    requests, rows_kv, hd = c_ref.shape
    window = win.shape[1]
    kv = rows_kv // span
    cut = requests // 4
    fresh = steps * kv
    seq = seq_ref[0]
    whole = pltpu.make_async_copy(c_ref, c_out, sems.at[requests])
    whole.start()
    for g in range(kv):
        at = column + g * hd
        for j, ref in enumerate(slot_refs):
            buf[pl.ds(j * cut * fresh + g, cut * steps, stride=kv), :] = ref[:, at : at + hd].astype(F32)
    line = lax.broadcasted_iota(jnp.int32, (window, hd), 0)
    place = lax.broadcasted_iota(jnp.int32, (window, fresh), 0) - lax.broadcasted_iota(
        jnp.int32, (window, fresh), 1
    )
    pieces = []
    for n in range(requests):
        request = ((seq & 3) ^ (n // cut)) * cut + n % cut
        base = (len_ref[request] - seq * span) * kv
        start = pl.multiple_of(jnp.clip((base // 16) * 16, 0, rows_kv - window), 16)
        touched = (base > -fresh) & (base < rows_kv)
        pieces.append((touched, start, request))

        @pl.when(touched)
        def _():
            pick = jnp.where(place == base - start, 1.0, 0.0).astype(BF16)
            new = (line >= base - start) & (line < base - start + fresh)
            rows = buf[n * fresh : (n + 1) * fresh, :].astype(BF16)
            put = jnp.dot(pick, rows, preferred_element_type=F32)
            old = c_ref[request, pl.ds(start, window), :].astype(F32)
            win[n] = jnp.where(new, put, old).astype(BF16)

    whole.wait()
    for act in ("start", "wait"):
        for n, (touched, start, request) in enumerate(pieces):

            @pl.when(touched)
            def _():
                copy = pltpu.make_async_copy(win.at[n], c_out.at[request, pl.ds(start, window), :], sems.at[n])
                getattr(copy, act)()


def mix_kernel(seq_ref, core_ref, a0_ref, a1_ref, a2_ref, a3_ref, w_ref, done_ref, mine_ref, other_ref, att_buf):
    part = a0_ref.shape[0]
    for j, ref in enumerate((a0_ref, a1_ref, a2_ref, a3_ref)):
        att_buf[pl.ds(pl.multiple_of(((seq_ref[0] & 3) ^ j) * part, 16), part), :] = ref[...]
    product = jnp.dot(att_buf[...], w_ref[...], preferred_element_type=F32)
    half = product.shape[0] // 2
    low = core_ref[0] == 0
    mine_ref[...] = jnp.where(low, product[:half], product[half:])
    other_ref[...] = jnp.where(low, product[half:], product[:half])


def stack_kernel(*refs):
    *in_refs, out_ref = refs
    at = 0
    for ref in in_refs:
        out_ref[at : at + ref.shape[0]] = ref[...]
        at += ref.shape[0]


def relay_kernel(in_ref, after_ref, out_ref):
    del after_ref
    out_ref[...] = in_ref[...]


def sum_kernel(mine_ref, recv_ref, msg_ref):
    msg_ref[...] = (mine_ref[...].astype(F32) + recv_ref[...].astype(F32)).astype(BF16)


def residual_kernel(steps, core_ref, x_ref, gain_ref, mine_ref, recv_ref, mixed_ref, piece_ref):
    rows = mine_ref.shape[0]
    requests = x_ref.shape[0] // steps
    cut = requests // 4
    core = core_ref[0]

    def source(row):
        quarter = row // (rows // 2)
        request = quarter * cut + row % (rows // 2) // steps
        return row % steps * requests + core * (requests // 2) + request

    part = mine_ref[...].astype(F32) + recv_ref[...].astype(F32)
    mixed = reorder(rows, source, x_ref[...]) + part
    mixed_ref[...] = mixed
    squares = jnp.sum(mixed * mixed, axis=1, keepdims=True)
    stats = jnp.where(lane_ids(rows) == 0, squares, 0.0)
    piece_ref[0, :, :LANES] = pack_stats(stats)
    piece_ref[0, :, LANES:] = (mixed * gain_ref[...].astype(F32)).astype(BF16)


def gather_products(masks, seq, own_ref, far_ref, wg_ref, wu_ref, so_far):
    width = own_ref.shape[2] - LANES
    squares = []
    for ref in (own_ref, far_ref):
        squares.append(sum(unpack_stats(ref[j, :, :LANES]) for j in range(len(masks))))
    squares = jnp.concatenate(squares, axis=0)
    gate = up = 0.0
    for j, mask in enumerate(masks):
        take = pl.ds(pl.multiple_of((seq ^ mask) * width, 16), width)
        x = jnp.concatenate([own_ref[j, :, LANES:], far_ref[j, :, LANES:]], axis=0)
        gate += jnp.dot(x, wg_ref[take, :], preferred_element_type=F32)
        up += jnp.dot(x, wu_ref[take, :], preferred_element_type=F32)
    return [new + ref[...] for new, ref in zip((squares, gate, up), so_far)] if so_far else (squares, gate, up)


def products_kernel(masks, seq_ref, own_ref, far_ref, wg_ref, wu_ref, *refs):
    found = gather_products(masks, seq_ref[0], own_ref, far_ref, wg_ref, wu_ref, refs[:-3])
    for ref, value in zip(refs[-3:], found):
        ref[...] = value


def hidden_kernel(masks, features, seq_ref, own_ref, far_ref, wg_ref, wu_ref, sq_ref, gate_ref, up_ref, h_ref):
    squares, gate, up = gather_products(
        masks, seq_ref[0], own_ref, far_ref, wg_ref, wu_ref, (sq_ref, gate_ref, up_ref)
    )
    scale = lax.rsqrt(squares[:, 0:1] / features + 1e-05)
    gate = gate * scale
    up = up * scale
    h_ref[...] = (gate / (1.0 + jnp.exp(-gate)) * up).astype(BF16)


def down_kernel(masks, seq_ref, h_ref, w_ref, *refs):
    own_ref, far_ref = refs[-2:]
    half, width = own_ref.shape[1:]
    hidden = h_ref[...]
    for j, mask in enumerate(masks):
        take = pl.ds(pl.multiple_of((seq_ref[0] ^ mask) * width, LANES), width)
        part = jnp.dot(hidden, w_ref[:, take], preferred_element_type=F32)
        own_ref[j] = part[:half]
        far_ref[j] = part[half:].astype(BF16)


def fold_kernel(acc_ref, *refs):
    *recv_refs, keep_ref, msg_ref = refs
    count = acc_ref.shape[0] // 2
    for j in range(2 * count):
        total = acc_ref[j]
        for ref in recv_refs:
            total += ref[j].astype(F32)
        if j < count:
            keep_ref[j] = total
        else:
            msg_ref[j - count] = total.astype(BF16)


def end_kernel(mixed_ref, mine_ref, recv_ref, out_ref):
    part = mine_ref[0].astype(F32) + recv_ref[0].astype(F32)
    out_ref[...] = (mixed_ref[...] + part).astype(BF16)


def join_kernel(steps, core_ref, own_ref, far_ref, out_ref):
    rows = out_ref.shape[0]
    requests = rows // steps
    cut = requests // 4
    low = core_ref[0] == 0
    own, far = own_ref[...], far_ref[...]
    whole = jnp.concatenate([jnp.where(low, own, far), jnp.where(low, far, own)], axis=0)

    def source(row):
        request = row % requests
        return request * steps + row // requests

    out_ref[...] = reorder(rows, source, whole).astype(BF16)


def per_device(
    n_seq,
    n_tp,
    tokens,
    attn_gain,
    w_query,
    w_key,
    w_value,
    w_out,
    ffn_gain,
    w_gate,
    w_up,
    w_down,
    key_cache,
    value_cache,
    lengths,
):
    steps, requests, width = tokens.shape
    span, kv, hd = key_cache.shape[1:]
    heads = w_query.shape[1] // hd
    cut = requests // 4
    part = steps * cut
    half, rows = 2 * part, 4 * part
    features = width * n_seq
    hidden_width = w_gate.shape[1]
    wide = w_query.shape[1] + w_key.shape[1] + w_value.shape[1] + LANES
    seq = lax.axis_index("seq").astype(jnp.int32)
    core = lax.axis_index("tp").astype(jnp.int32) & 1
    seq_arr, core_arr = seq.reshape(1), core.reshape(1)
    rest = [1 << b for b in range(2, n_seq.bit_length() - 1)]
    tp_bits = [1 << b for b in range(n_tp.bit_length() - 1)]
    masks = [0]
    for bit in reversed(rest):
        masks = masks + [m ^ bit for m in masks]
    slots = [[m ^ j for m in masks] for j in range(4)]

    def hop(value, axis, bit):
        size = n_seq if axis == "seq" else n_tp
        return lax.ppermute(value, axis, [(i, i ^ bit) for i in range(size)])

    x = tokens.reshape(rows, width)
    flat = (requests, span * kv, hd)
    k_flat, v_flat = key_cache.reshape(flat), value_cache.reshape(flat)

    own_lengths = lax.dynamic_slice_in_dim(lengths, (seq & 3) * cut, cut, 0)
    positions = (own_lengths[:, None] + jnp.arange(steps, dtype=jnp.int32)[None, :]).reshape(part)
    freqs = jnp.exp(jnp.arange(hd // 2, dtype=F32) * (-2.0 * math.log(100000000.0) / hd))
    angles = positions.astype(F32)[:, None] * freqs[None, :]
    cosine, sine = jnp.cos(angles), jnp.sin(angles)
    cosine = jnp.concatenate([cosine, cosine], axis=1)
    sine = jnp.concatenate([-sine, sine], axis=1)

    with jax.named_scope("project"):
        sums = [sds((part, wide), F32), sds((part, wide), BF16)]
        acc, *msgs = call(
            functools.partial(project_kernel, steps),
            sums + sums[1:] * 2,
            [SMEM] + [HBM] * 5,
            [
                pltpu.VMEM(x.shape, BF16),
                pltpu.VMEM(attn_gain.shape, BF16),
                pltpu.VMEM(w_query.shape, BF16),
                pltpu.VMEM(w_key.shape, BF16),
                pltpu.VMEM(w_value.shape, BF16),
                pltpu.SemaphoreType.DMA((5,)),
            ],
            limit=60,
        )(seq_arr, x, attn_gain, w_query, w_key, w_value)
        arrived = [hop(msgs[j - 1], "seq", j) for j in (3, 2, 1)]
        (acc,) = call(keep_kernel, sums[:1], [VMEM])(acc)
        for bit in rest:
            acc, msg = call(add_kernel, sums, [VMEM] * (1 + len(arrived)))(acc, *arrived)
            arrived = [hop(msg, "seq", bit)]
        (finished,) = call(
            functools.partial(rotate_kernel, heads, kv, hd, features),
            [sds((part, wide - LANES), BF16)],
            [VMEM] * 4,
        )(acc, arrived[0], cosine, sine)
        found = {j: hop(finished, "seq", j) for j in (3, 2, 1)}
        found[0] = finished

    with jax.named_scope("attend"):
        block = steps * heads
        fresh = steps * kv
        joint = [
            sds((part, heads * hd), F32),
            sds((part, LANES), F32),
            sds((part, heads * hd + LANES), BF16),
        ]
        scratch = [
            pltpu.VMEM((cut * block, hd), F32),
            pltpu.VMEM((cut * fresh, hd), F32),
            pltpu.VMEM((cut * fresh, hd), F32),
            pltpu.VMEM((cut * block, flat[1]), F32),
            pltpu.VMEM((cut * block, hd), F32),
            pltpu.VMEM((cut * block, hd), F32),
            pltpu.VMEM((cut * block, hd), F32),
            pltpu.VMEM((part, heads * hd), F32),
            pltpu.VMEM((part, LANES), F32),
        ]

        def attend(slot):
            return call(
                functools.partial(attend_kernel, heads, kv, steps, span, slot),
                joint[2:] if slot else joint[:2],
                [SMEM, SMEM] + [VMEM] * 3,
                scratch,
                cost=20,
            )(seq_arr, lengths, found[slot], k_flat, v_flat)

        o, st = attend(0)
        arrived = [hop(attend(j)[0], "seq", j) for j in (3, 2, 1)]
        for bit in rest:
            o, st, msg = call(
                functools.partial(merge_kernel, heads), joint, [VMEM] * (2 + len(arrived))
            )(o, st, *arrived)
            arrived = [hop(msg, "seq", bit)]

        def store(column, cache, after):
            return call(
                functools.partial(store_kernel, column * hd, steps, span),
                [sds(flat, BF16), sds((part, LANES), F32)],
                [SMEM, SMEM] + [VMEM] * 6,
                [
                    pltpu.VMEM((requests * fresh, hd), F32),
                    pltpu.VMEM((requests, 16 + -(-fresh // 16) * 16, hd), BF16),
                    pltpu.SemaphoreType.DMA((requests + 1,)),
                ],
                [HBM, VMEM],
            )(seq_arr, lengths, *(found[j] for j in range(4)), cache, after)

        keys, done = store(heads, k_flat, st)
        attended, done = call(
            functools.partial(finish_kernel, heads),
            [sds((part, heads * hd), BF16), sds((part, LANES), F32)],
            [VMEM] * 4,
        )(o, st, arrived[0], done)
        values, done = store(heads + kv, v_flat, done)
        found = {j: hop(attended, "seq", j) for j in (3, 2, 1)}
        found[0] = attended

    with jax.named_scope("mix"):
        mine, other = call(
            mix_kernel,
            [sds((half, width), F32)] * 2,
            [SMEM, SMEM] + [VMEM] * 6,
            [pltpu.VMEM((rows, heads * hd), BF16)],
        )(seq_arr, core_arr, *(found[j] for j in range(4)), w_out, done)
        summed = mine, hop(other, "tp", 1)
        for bit in tp_bits[1:]:
            (msg,) = call(sum_kernel, [sds((half, width), BF16)], [VMEM] * 2)(*summed)
            summed = msg, hop(msg, "tp", bit)
        gain = lax.dynamic_slice_in_dim(ffn_gain, seq * width, width, 0).reshape(1, width)
        mixed, pieces = call(
            functools.partial(residual_kernel, steps),
            [sds((half, width), F32), sds((1, half, LANES + width), BF16)],
            [SMEM] + [VMEM] * 4,
            cost=6,
        )(core_arr, x, gain, *summed)
        for bit in reversed(rest):
            (pieces,) = call(
                stack_kernel,
                [sds((2 * pieces.shape[0],) + pieces.shape[1:], BF16)],
                [VMEM] * 2,
                cost=8,
            )(pieces, hop(pieces, "seq", bit))

    with jax.named_scope("ffn"):
        found = {j: hop(pieces, "seq", j) for j in (3, 2, 1)}
        found[0] = pieces
        order = (0, 3, 2, 1)
        state = []
        earlier = []
        for n, j in enumerate(order):
            piece = found[j]
            if n:
                (piece,) = call(relay_kernel, [sds(piece.shape, BF16)], [VMEM] * 2, cost=1)(
                    piece, earlier[max(n - 2, 0)]
                )
            last = n == 3
            state = call(
                functools.partial(hidden_kernel, slots[j], features)
                if last
                else functools.partial(products_kernel, slots[j]),
                [sds((rows, hidden_width), BF16)]
                if last
                else [sds((rows, LANES), F32)] + [sds((rows, hidden_width), F32)] * 2,
                [SMEM] + [VMEM] * (4 + len(state)),
                cost=1,
            )(seq_arr, found[j], hop(piece, "tp", 1), w_gate, w_up, *state)
            earlier.append(state[0])
        (hidden,) = state

        shape = (len(masks), half, width)

        def down(some, *after):
            if width % LANES == 0:
                return call(
                    functools.partial(down_kernel, some),
                    [sds(shape, F32), sds(shape, BF16)],
                    [SMEM] + [VMEM] * (2 + len(after)),
                    cost=1,
                )(seq_arr, hidden, w_down, *after)
            whole = jnp.dot(hidden, w_down, preferred_element_type=F32)
            whole = whole.reshape(rows, n_seq, width).transpose(1, 0, 2)
            whole = jnp.take(whole, seq ^ jnp.array(some, jnp.int32), axis=0)
            return whole[:, :half], whole[:, half:].astype(BF16)

        arrived = []
        for j in (3, 2, 1):
            own, far = down(slots[j])
            (msg,) = call(sum_kernel, [sds(shape, BF16)], [VMEM] * 2)(own, hop(far, "tp", 1))
            arrived.append(hop(msg, "seq", j))
        keep, far = down(slots[0], msg)
        arrived.append(hop(far, "tp", 1))
        for bit in rest:
            shape = (keep.shape[0] // 2, half, width)
            keep, msg = call(fold_kernel, [sds(shape, F32), sds(shape, BF16)], [VMEM] * (1 + len(arrived)))(
                keep, *arrived
            )
            arrived = [hop(msg, "seq", bit)]
        shape = (1, half, width)
        summed = keep, arrived[0]
        for bit in tp_bits[1:]:
            (msg,) = call(sum_kernel, [sds(shape, BF16)], [VMEM] * 2)(*summed)
            summed = msg, hop(msg, "tp", bit)
        (own,) = call(end_kernel, [sds((half, width), BF16)], [VMEM] * 3)(mixed, *summed)
        (result,) = call(functools.partial(join_kernel, steps), [sds(x.shape, BF16)], [SMEM] + [VMEM] * 2)(
            core_arr, own, hop(own, "tp", 1)
        )
    return result.reshape(tokens.shape), keys.reshape(key_cache.shape), values.reshape(value_cache.shape)


def solution(mesh):
    placed = (
        P(None, None, "seq"),
        P("seq"),
        P("seq", "tp"),
        P("seq", "tp"),
        P("seq", "tp"),
        P("tp", "seq"),
        P(),
        P(None, ("seq", "tp")),
        P(None, ("seq", "tp")),
        P(("seq", "tp"), None),
        P(None, "seq", "tp", None),
        P(None, "seq", "tp", None),
        P(),
    )
    return jax.shard_map(
        functools.partial(per_device, mesh.shape["seq"], mesh.shape["tp"]),
        mesh=mesh,
        in_specs=placed,
        out_specs=(P(None, None, "seq"), P(None, "seq", "tp", None), P(None, "seq", "tp", None)),
        check_vma=False,
    )
```

time: 101 us -> 93.2 us (0.923)
  waiting for transfers between devices: 49.6 us -> 28.6 us
  starting transfers between devices: 30.6 us -> 38.1 us
  Pallas kernels: 17.7 us -> 21 us
  local copies, waits for them, and re-layouts: 2.17 us -> 3.97 us
    ppermute x21 -> x34, waiting for transfers between devices: 49.6 us -> 28.6 us  [hop(): return lax.ppermute(value, axis, [(i, i ^ bit) for i in range(size)])]
    ppermute x21 -> x34, starting transfers between devices: 30.6 us -> 38.1 us  [hop(): return lax.ppermute(value, axis, [(i, i ^ bit) for i in range(size)])]
    pallas_call x18 -> x28, Pallas kernels: 15.2 us -> 18.3 us  [the longest x2 4.52 us: store(): call(functools.partial(store_kernel, column * hd, steps, span), [sds(flat...]
    unnamed x30, local copies, waits for them, and re-layouts: 1.24 us -> 3.05 us
    pallas_call x2 -> x4, Pallas kernels: 2.35 us -> 2.61 us  [down(): call(functools.partial(down_kernel, some), [sds(shape, F32), sds(shape, B...]
  transfers between devices with their start and end apart: 21 -> 34, of which waited for: 17 -> 20; matrix products, arithmetic and copies ran while one was open for 1% -> 1% of each run, Pallas kernels for 7% -> 14%
where the time goes in v4:
time: 93.2 us; the launch traced here: 93 us
  starting transfers between devices  38.1 us (41%)
  waiting for transfers between devices  28.6 us (31%)
  Pallas kernels  21 us (23%)
  local copies, waits for them, and re-layouts  3.97 us (4%)
  between operations  1.04 us (1%)
    ppermute x34, starting transfers between devices, hop(): return lax.ppermute(value, axis, [(i, i ^ bit) for i in range(size)])  38.1 us
    ppermute x34, waiting for transfers between devices, hop(): return lax.ppermute(value, axis, [(i, i ^ bit) for i in range(size)])  28.6 us
    pallas_call x2, Pallas kernels, store(): call(functools.partial(store_kernel, column * hd, steps, span), [sds(flat...  4.52 us
    pallas_call x4, Pallas kernels, attend(): call(functools.partial(attend_kernel, heads, kv, steps, span, slot), join...  4.22 us
    pallas_call x4, Pallas kernels, per_device(): call(functools.partial(hidden_kernel, slots[j], features) if last else fu...  4.19 us
    unnamed x30, local copies, waits for them, and re-layouts  3.05 us
    pallas_call x1, Pallas kernels, per_device(): call(functools.partial(project_kernel, steps), sums + sums[1:] * 2, [SMEM...  2.9 us
    pallas_call x4, Pallas kernels, down(): call(functools.partial(down_kernel, some), [sds(shape, F32), sds(shape, B...  2.61 us
  transfers between devices with their start and end apart: 34, of which 20 were waited for; matrix products, arithmetic and copies ran while one was open for 1% of the time, Pallas kernels for 14%

profile of v4, /device:TPU:0, one launch (start us, length us, event | category | flops | bytes accessed | tf_op | source)
XLA Modules:
  0.0 93.0 jit_solution(16154915627624766069)
XLA Ops:
  0.6 2.9 %project.4 = (f32[16,1664]{1,0:T(8,128)}, bf16[16,1664]{1,0:T(8,128)(2,1)}, bf16[16,1664]{1,0:T(8,128)(2,1)}, bf16[16,1664]{1,0:T(8,128)(2,1)}) custom-call(s32[1]{0:T(128)} %bitcast.2.seq_ref, bf16[64,640]{1,0:T(8,128)(2,1)} %bitcast.24, bf16[640]{0:T(1024)(128)(2,1)} %gain_hbm.1, bf16[640,1024]{1,0:T(8,128)(2,1)} %wq_hbm.1, bf16[640,256]{1,0:T(8,128)(2,1)} %wk_hbm.1, ...), custom_call_target="tpu_custom_call" | custom-call | flops 3449999872 | bytes 1048576 | tf_op jit(solution)/shard_map/project/pallas_call | solution.py:508
  3.6 4.0 %collective-permute-start = (bf16[16,1664]{1,0:T(8,128)(2,1)}, bf16[16,1664]{1,0:T(8,128)(2,1)S(1)}, u32[]{:S(2)}, u32[]{:S(2)}) collective-permute-start(bf16[16,1664]{1,0:T(8,128)(2,1)} %get-tuple-element.44), channel_id=1, source_target_pairs={{0,12},{4,8},{8,4},{12,0},{16,28},{20,24},{24,20},{28,16},{1,13},{... | collective-permute-start | bytes 159752 | tf_op jit(solution)/shard_map/project/ppermute | solution.py:492
  9.9 2.0 %collective-permute-done.1.refs_1_ = bf16[16,1664]{1,0:T(8,128)(2,1)S(1)} collective-permute-done((bf16[16,1664]{1,0:T(8,128)(2,1)}, bf16[16,1664]{1,0:T(8,128)(2,1)S(1)}, u32[]{:S(2)}, u32[]{:S(2)}) %collective-permute-start.1) | collective-permute-done | bytes 53280 | tf_op jit(solution)/shard_map/project/ppermute | solution.py:492
  12.5 2.6 %collective-permute-start.3 = (bf16[16,1664]{1,0:T(8,128)(2,1)S(1)}, bf16[16,1664]{1,0:T(8,128)(2,1)S(1)}, u32[]{:S(2)}, u32[]{:S(2)}) collective-permute-start(bf16[16,1664]{1,0:T(8,128)(2,1)S(1)} %get-tuple-element.48), channel_id=1, source_target_pairs={{0,16},{4,20},{8,24},{12,28},{16,0},{20,4},{24,8},{28,12},{1,17},{... | collective-permute-start | bytes 159752 | tf_op jit(solution)/shard_map/project/ppermute | solution.py:492
  15.2 2.4 %collective-permute-done.3.recv_ref = bf16[16,1664]{1,0:T(8,128)(2,1)S(1)} collective-permute-done((bf16[16,1664]{1,0:T(8,128)(2,1)S(1)}, bf16[16,1664]{1,0:T(8,128)(2,1)S(1)}, u32[]{:S(2)}, u32[]{:S(2)}) %collective-permute-start.3) | collective-permute-done | bytes 53280 | tf_op jit(solution)/shard_map/project/ppermute | solution.py:492
  17.8 1.6 %collective-permute-start.4 = (bf16[16,1536]{1,0:T(8,128)(2,1)S(1)}, bf16[16,1536]{1,0:T(8,128)(2,1)S(1)}, u32[]{:S(2)}, u32[]{:S(2)}) collective-permute-start(bf16[16,1536]{1,0:T(8,128)(2,1)S(1)} %project.7.rows_ref.refs_0_), channel_id=1, source_target_pairs={{0,12},{4,8},{8,4},{12,0},{16,28},{20,24},{24,20},{28,16},{1,13},{... | collective-permute-start | bytes 147464 | tf_op jit(solution)/shard_map/project/ppermute | solution.py:492
  19.7 1.7 %collective-permute-start.8 = (bf16[16,1536]{1,0:T(8,128)(2,1)S(1)}, bf16[16,1536]{1,0:T(8,128)(2,1)S(1)}, u32[]{:S(2)}, u32[]{:S(2)}) collective-permute-start(bf16[16,1536]{1,0:T(8,128)(2,1)S(1)} %project.7.rows_ref.refs_0_), channel_id=1, source_target_pairs={{0,4},{4,0},{8,12},{12,8},{16,20},{20,16},{24,28},{28,24},{1,5},{5... | collective-permute-start | bytes 147464 | tf_op jit(solution)/shard_map/project/ppermute | solution.py:492
  24.0 1.6 %collective-permute-start.5 = (bf16[16,1152]{1,0:T(8,128)(2,1)S(1)}, bf16[16,1152]{1,0:T(8,128)(2,1)S(1)}, u32[]{:S(2)}, u32[]{:S(2)}) collective-permute-start(bf16[16,1152]{1,0:T(8,128)(2,1)S(1)} %attend.9), channel_id=1, source_target_pairs={{0,12},{4,8},{8,4},{12,0},{16,28},{20,24},{24,20},{28,16},{1,13},{... | collective-permute-start | bytes 110600 | tf_op jit(solution)/shard_map/attend/ppermute | solution.py:492
  27.9 1.8 %collective-permute-start.9 = (bf16[16,1152]{1,0:T(8,128)(2,1)S(1)}, bf16[16,1152]{1,0:T(8,128)(2,1)S(1)}, u32[]{:S(2)}, u32[]{:S(2)}) collective-permute-start(bf16[16,1152]{1,0:T(8,128)(2,1)S(1)} %attend.11), channel_id=1, source_target_pairs={{0,4},{4,0},{8,12},{12,8},{16,20},{20,16},{24,28},{28,24},{1,5},{5... | collective-permute-start | bytes 110600 | tf_op jit(solution)/shard_map/attend/ppermute | solution.py:492
  32.2 2.9 %collective-permute-start.10 = (bf16[16,1152]{1,0:T(8,128)(2,1)S(1)}, bf16[16,1152]{1,0:T(8,128)(2,1)S(1)}, u32[]{:S(2)}, u32[]{:S(2)}) collective-permute-start(bf16[16,1152]{1,0:T(8,128)(2,1)S(1)} %get-tuple-element.53), channel_id=1, source_target_pairs={{0,16},{4,20},{8,24},{12,28},{16,0},{20,4},{24,8},{28,12},{1,17},{... | collective-permute-start | bytes 110600 | tf_op jit(solution)/shard_map/attend/ppermute | solution.py:492
  35.1 2.3 %attend.13 = (bf16[16,256,128]{2,1,0:T(8,128)(2,1)}, f32[16,128]{1,0:T(8,128)S(1)}) custom-call(s32[1]{0:T(128)} %bitcast.2.seq_ref, s32[16]{0:T(128)S(1)} %copy-done.4, bf16[16,1536]{1,0:T(8,128)(2,1)S(1)} %project.7.rows_ref.refs_0_, bf16[16,1536]{1,0:T(8,128)(2,1)S(1)} %collective-permute-done.8.rows_ref.refs_1_, ...), custom_call_target="tpu_custom_call" | custom-call | flops 3449999872 | bytes 1048576 | tf_op jit(solution)/shard_map/attend/pallas_call | solution.py:573
  39.2 2.0 %collective-permute-start.12 = (bf16[16,1024]{1,0:T(8,128)(2,1)S(1)}, bf16[16,1024]{1,0:T(8,128)(2,1)S(1)}, u32[]{:S(2)}, u32[]{:S(2)}) collective-permute-start(bf16[16,1024]{1,0:T(8,128)(2,1)S(1)} %get-tuple-element.55.a0_ref), channel_id=1, source_target_pairs={{0,8},{4,12},{8,0},{12,4},{16,24},{20,28},{24,16},{28,20},{1,9},{5... | collective-permute-start | bytes 98312 | tf_op jit(solution)/shard_map/attend/ppermute | solution.py:492
  41.2 2.3 %attend.15 = (bf16[16,256,128]{2,1,0:T(8,128)(2,1)}, f32[16,128]{1,0:T(8,128)S(1)}) custom-call(s32[1]{0:T(128)} %bitcast.2.seq_ref, s32[16]{0:T(128)S(1)} %copy-done.4, bf16[16,1536]{1,0:T(8,128)(2,1)S(1)} %project.7.rows_ref.refs_0_, bf16[16,1536]{1,0:T(8,128)(2,1)S(1)} %collective-permute-done.8.rows_ref.refs_1_, ...), custom_call_target="tpu_custom_call" | custom-call | flops 3449999872 | bytes 1048576 | tf_op jit(solution)/shard_map/attend/pallas_call | solution.py:573
  43.5 2.5 %collective-permute-done.13.a3_ref = bf16[16,1024]{1,0:T(8,128)(2,1)S(1)} collective-permute-done((bf16[16,1024]{1,0:T(8,128)(2,1)S(1)}, bf16[16,1024]{1,0:T(8,128)(2,1)S(1)}, u32[]{:S(2)}, u32[]{:S(2)}) %collective-permute-start.13) | collective-permute-done | bytes 32800 | tf_op jit(solution)/shard_map/attend/ppermute | solution.py:492
  47.7 1.6 %collective-permute-start.15 = (bf16[32,640]{1,0:T(8,128)(2,1)S(1)}, bf16[32,640]{1,0:T(8,128)(2,1)S(1)}, u32[]{:S(2)}, u32[]{:S(2)}) collective-permute-start(bf16[32,640]{1,0:T(8,128)(2,1)S(1)} %mix.5.mine_ref), channel_id=1, source_target_pairs={{0,2},{1,3},{2,0},{3,1},{4,6},{5,7},{6,4},{7,5},{8,10},{9,11},{10,... | collective-permute-start | bytes 122888 | tf_op jit(solution)/shard_map/mix/ppermute | solution.py:492
  50.1 1.7 %collective-permute-done.15.recv_ref = bf16[32,640]{1,0:T(8,128)(2,1)S(1)} collective-permute-done((bf16[32,640]{1,0:T(8,128)(2,1)S(1)}, bf16[32,640]{1,0:T(8,128)(2,1)S(1)}, u32[]{:S(2)}, u32[]{:S(2)}) %collective-permute-start.15) | collective-permute-done | bytes 40992 | tf_op jit(solution)/shard_map/mix/ppermute | solution.py:492
  52.2 2.6 %collective-permute-start.16 = (bf16[1,32,768]{2,1,0:T(8,128)(2,1)S(1)}, bf16[1,32,768]{2,1,0:T(8,128)(2,1)S(1)}, u32[]{:S(2)}, u32[]{:S(2)}) collective-permute-start(bf16[1,32,768]{2,1,0:T(8,128)(2,1)S(1)} %get-tuple-element.61.refs_0_), channel_id=1, source_target_pairs={{0,16},{4,20},{8,24},{12,28},{16,0},{20,4},{24,8},{28,12},{1,17},{... | collective-permute-start | bytes 147464 | tf_op jit(solution)/shard_map/mix/ppermute | solution.py:492
  54.8 2.4 %collective-permute-done.16.refs_1_ = bf16[1,32,768]{2,1,0:T(8,128)(2,1)S(1)} collective-permute-done((bf16[1,32,768]{2,1,0:T(8,128)(2,1)S(1)}, bf16[1,32,768]{2,1,0:T(8,128)(2,1)S(1)}, u32[]{:S(2)}, u32[]{:S(2)}) %collective-permute-start.16) | collective-permute-done | bytes 49184 | tf_op jit(solution)/shard_map/mix/ppermute | solution.py:492
  58.9 2.0 %collective-permute-start.22 = (bf16[2,32,768]{2,1,0:T(8,128)(2,1)S(1)}, bf16[2,32,768]{2,1,0:T(8,128)(2,1)S(1)}, u32[]{:S(2)}, u32[]{:S(2)}) collective-permute-start(bf16[2,32,768]{2,1,0:T(8,128)(2,1)S(1)} %mix.7.own_ref), channel_id=1, source_target_pairs={{0,8},{4,12},{8,0},{12,4},{16,24},{20,28},{24,16},{28,20},{1,9},{5... | collective-permute-start | bytes 294920 | tf_op jit(solution)/shard_map/ffn/ppermute | solution.py:492
  62.0 2.9 %collective-permute-done.18.in_ref.own_ref = bf16[2,32,768]{2,1,0:T(8,128)(2,1)S(1)} collective-permute-done((bf16[2,32,768]{2,1,0:T(8,128)(2,1)S(1)}, bf16[2,32,768]{2,1,0:T(8,128)(2,1)S(1)}, u32[]{:S(2)}, u32[]{:S(2)}) %collective-permute-start.18) | collective-permute-done | bytes 98336 | tf_op jit(solution)/shard_map/ffn/ppermute | solution.py:492
  77.0 2.3 %collective-permute-start.28 = (bf16[2,32,640]{2,1,0:T(8,128)(2,1)S(1)}, bf16[2,32,640]{2,1,0:T(8,128)(2,1)S(1)}, u32[]{:S(2)}, u32[]{:S(2)}) collective-permute-start(bf16[2,32,640]{2,1,0:T(8,128)(2,1)S(1)} %ffn.31), channel_id=1, source_target_pairs={{0,8},{4,12},{8,0},{12,4},{16,24},{20,28},{24,16},{28,20},{1,9},{5... | collective-permute-start | bytes 245768 | tf_op jit(solution)/shard_map/ffn/ppermute | solution.py:492
  81.8 2.6 %collective-permute-start.31 = (bf16[1,32,640]{2,1,0:T(8,128)(2,1)S(1)}, bf16[1,32,640]{2,1,0:T(8,128)(2,1)S(1)}, u32[]{:S(2)}, u32[]{:S(2)}) collective-permute-start(bf16[1,32,640]{2,1,0:T(8,128)(2,1)S(1)} %get-tuple-element.80), channel_id=1, source_target_pairs={{0,16},{4,20},{8,24},{12,28},{16,0},{20,4},{24,8},{28,12},{1,17},{... | collective-permute-start | bytes 122888 | tf_op jit(solution)/shard_map/ffn/ppermute | solution.py:492
  84.5 2.4 %collective-permute-done.31.recv_ref = bf16[1,32,640]{2,1,0:T(8,128)(2,1)S(1)} collective-permute-done((bf16[1,32,640]{2,1,0:T(8,128)(2,1)S(1)}, bf16[1,32,640]{2,1,0:T(8,128)(2,1)S(1)}, u32[]{:S(2)}, u32[]{:S(2)}) %collective-permute-start.31) | collective-permute-done | bytes 40992 | tf_op jit(solution)/shard_map/ffn/ppermute | solution.py:492
  88.4 2.5 %collective-permute-done.32.recv_ref = bf16[1,32,640]{2,1,0:T(8,128)(2,1)S(1)} collective-permute-done((bf16[1,32,640]{2,1,0:T(8,128)(2,1)S(1)}, bf16[1,32,640]{2,1,0:T(8,128)(2,1)S(1)}, u32[]{:S(2)}, u32[]{:S(2)}) %collective-permute-start.32) | collective-permute-done | bytes 40992 | tf_op jit(solution)/shard_map/ffn/ppermute | solution.py:492
  (119 shorter events, 36.4 us)
Async XLA Ops:
  3.6 6.3 %collective-permute-start = (bf16[16,1664]{1,0:T(8,128)(2,1)}, bf16[16,1664]{1,0:T(8,128)(2,1)S(1)}, u32[]{:S(2)}, u32[]{:S(2)}) collective-permute-start(bf16[16,1664]{1,0:T(8,128)(2,1)} %get-tuple-element.44), channel_id=1, source_target_pairs={{0,12},{4,8},{8,4},{12,0},{16,28},{20,24},{24,20},{28,16},{1,13},{... | collective-permute-start | bytes 159752 | tf_op jit(solution)/shard_map/project/ppermute | solution.py:492
  7.6 4.3 %collective-permute-start.1 = (bf16[16,1664]{1,0:T(8,128)(2,1)}, bf16[16,1664]{1,0:T(8,128)(2,1)S(1)}, u32[]{:S(2)}, u32[]{:S(2)}) collective-permute-start(bf16[16,1664]{1,0:T(8,128)(2,1)} %get-tuple-element.45), channel_id=1, source_target_pairs={{0,8},{4,12},{8,0},{12,4},{16,24},{20,28},{24,16},{28,20},{1,9},{5... | collective-permute-start | bytes 159752 | tf_op jit(solution)/shard_map/project/ppermute | solution.py:492
  8.0 4.3 %collective-permute-start.2 = (bf16[16,1664]{1,0:T(8,128)(2,1)}, bf16[16,1664]{1,0:T(8,128)(2,1)S(1)}, u32[]{:S(2)}, u32[]{:S(2)}) collective-permute-start(bf16[16,1664]{1,0:T(8,128)(2,1)} %get-tuple-element.46), channel_id=1, source_target_pairs={{0,4},{4,0},{8,12},{12,8},{16,20},{20,16},{24,28},{28,24},{1,5},{5... | collective-permute-start | bytes 159752 | tf_op jit(solution)/shard_map/project/ppermute | solution.py:492
  12.5 5.1 %collective-permute-start.3 = (bf16[16,1664]{1,0:T(8,128)(2,1)S(1)}, bf16[16,1664]{1,0:T(8,128)(2,1)S(1)}, u32[]{:S(2)}, u32[]{:S(2)}) collective-permute-start(bf16[16,1664]{1,0:T(8,128)(2,1)S(1)} %get-tuple-element.48), channel_id=1, source_target_pairs={{0,16},{4,20},{8,24},{12,28},{16,0},{20,4},{24,8},{28,12},{1,17},{... | collective-permute-start | bytes 159752 | tf_op jit(solution)/shard_map/project/ppermute | solution.py:492
  17.8 5.1 %collective-permute-start.4 = (bf16[16,1536]{1,0:T(8,128)(2,1)S(1)}, bf16[16,1536]{1,0:T(8,128)(2,1)S(1)}, u32[]{:S(2)}, u32[]{:S(2)}) collective-permute-start(bf16[16,1536]{1,0:T(8,128)(2,1)S(1)} %project.7.rows_ref.refs_0_), channel_id=1, source_target_pairs={{0,12},{4,8},{8,4},{12,0},{16,28},{20,24},{24,20},{28,16},{1,13},{... | collective-permute-start | bytes 147464 | tf_op jit(solution)/shard_map/project/ppermute | solution.py:492
  19.4 6.1 %collective-permute-start.6 = (bf16[16,1536]{1,0:T(8,128)(2,1)S(1)}, bf16[16,1536]{1,0:T(8,128)(2,1)S(1)}, u32[]{:S(2)}, u32[]{:S(2)}) collective-permute-start(bf16[16,1536]{1,0:T(8,128)(2,1)S(1)} %project.7.rows_ref.refs_0_), channel_id=1, source_target_pairs={{0,8},{4,12},{8,0},{12,4},{16,24},{20,28},{24,16},{28,20},{1,9},{5... | collective-permute-start | bytes 147464 | tf_op jit(solution)/shard_map/project/ppermute | solution.py:492
  19.7 7.2 %collective-permute-start.8 = (bf16[16,1536]{1,0:T(8,128)(2,1)S(1)}, bf16[16,1536]{1,0:T(8,128)(2,1)S(1)}, u32[]{:S(2)}, u32[]{:S(2)}) collective-permute-start(bf16[16,1536]{1,0:T(8,128)(2,1)S(1)} %project.7.rows_ref.refs_0_), channel_id=1, source_target_pairs={{0,4},{4,0},{8,12},{12,8},{16,20},{20,16},{24,28},{28,24},{1,5},{5... | collective-permute-start | bytes 147464 | tf_op jit(solution)/shard_map/project/ppermute | solution.py:492
  24.0 6.8 %collective-permute-start.5 = (bf16[16,1152]{1,0:T(8,128)(2,1)S(1)}, bf16[16,1152]{1,0:T(8,128)(2,1)S(1)}, u32[]{:S(2)}, u32[]{:S(2)}) collective-permute-start(bf16[16,1152]{1,0:T(8,128)(2,1)S(1)} %attend.9), channel_id=1, source_target_pairs={{0,12},{4,8},{8,4},{12,0},{16,28},{20,24},{24,20},{28,16},{1,13},{... | collective-permute-start | bytes 110600 | tf_op jit(solution)/shard_map/attend/ppermute | solution.py:492
  26.6 4.1 %collective-permute-start.7 = (bf16[16,1152]{1,0:T(8,128)(2,1)S(1)}, bf16[16,1152]{1,0:T(8,128)(2,1)S(1)}, u32[]{:S(2)}, u32[]{:S(2)}) collective-permute-start(bf16[16,1152]{1,0:T(8,128)(2,1)S(1)} %attend.10), channel_id=1, source_target_pairs={{0,8},{4,12},{8,0},{12,4},{16,24},{20,28},{24,16},{28,20},{1,9},{5... | collective-permute-start | bytes 110600 | tf_op jit(solution)/shard_map/attend/ppermute | solution.py:492
  27.9 4.0 %collective-permute-start.9 = (bf16[16,1152]{1,0:T(8,128)(2,1)S(1)}, bf16[16,1152]{1,0:T(8,128)(2,1)S(1)}, u32[]{:S(2)}, u32[]{:S(2)}) collective-permute-start(bf16[16,1152]{1,0:T(8,128)(2,1)S(1)} %attend.11), channel_id=1, source_target_pairs={{0,4},{4,0},{8,12},{12,8},{16,20},{20,16},{24,28},{28,24},{1,5},{5... | collective-permute-start | bytes 110600 | tf_op jit(solution)/shard_map/attend/ppermute | solution.py:492
  32.2 5.2 %collective-permute-start.10 = (bf16[16,1152]{1,0:T(8,128)(2,1)S(1)}, bf16[16,1152]{1,0:T(8,128)(2,1)S(1)}, u32[]{:S(2)}, u32[]{:S(2)}) collective-permute-start(bf16[16,1152]{1,0:T(8,128)(2,1)S(1)} %get-tuple-element.53), channel_id=1, source_target_pairs={{0,16},{4,20},{8,24},{12,28},{16,0},{20,4},{24,8},{28,12},{1,17},{... | collective-permute-start | bytes 110600 | tf_op jit(solution)/shard_map/attend/ppermute | solution.py:492
  37.7 5.8 %collective-permute-start.11 = (bf16[16,1024]{1,0:T(8,128)(2,1)S(1)}, bf16[16,1024]{1,0:T(8,128)(2,1)S(1)}, u32[]{:S(2)}, u32[]{:S(2)}) collective-permute-start(bf16[16,1024]{1,0:T(8,128)(2,1)S(1)} %get-tuple-element.55.a0_ref), channel_id=1, source_target_pairs={{0,4},{4,0},{8,12},{12,8},{16,20},{20,16},{24,28},{28,24},{1,5},{5... | collective-permute-start | bytes 98312 | tf_op jit(solution)/shard_map/attend/ppermute | solution.py:492
  39.2 4.3 %collective-permute-start.12 = (bf16[16,1024]{1,0:T(8,128)(2,1)S(1)}, bf16[16,1024]{1,0:T(8,128)(2,1)S(1)}, u32[]{:S(2)}, u32[]{:S(2)}) collective-permute-start(bf16[16,1024]{1,0:T(8,128)(2,1)S(1)} %get-tuple-element.55.a0_ref), channel_id=1, source_target_pairs={{0,8},{4,12},{8,0},{12,4},{16,24},{20,28},{24,16},{28,20},{1,9},{5... | collective-permute-start | bytes 98312 | tf_op jit(solution)/shard_map/attend/ppermute | solution.py:492
  41.2 4.8 %collective-permute-start.13 = (bf16[16,1024]{1,0:T(8,128)(2,1)S(1)}, bf16[16,1024]{1,0:T(8,128)(2,1)S(1)}, u32[]{:S(2)}, u32[]{:S(2)}) collective-permute-start(bf16[16,1024]{1,0:T(8,128)(2,1)S(1)} %get-tuple-element.55.a0_ref), channel_id=1, source_target_pairs={{0,12},{4,8},{8,4},{12,0},{16,28},{20,24},{24,20},{28,16},{1,13},{... | collective-permute-start | bytes 98312 | tf_op jit(solution)/shard_map/attend/ppermute | solution.py:492
  47.7 4.1 %collective-permute-start.15 = (bf16[32,640]{1,0:T(8,128)(2,1)S(1)}, bf16[32,640]{1,0:T(8,128)(2,1)S(1)}, u32[]{:S(2)}, u32[]{:S(2)}) collective-permute-start(bf16[32,640]{1,0:T(8,128)(2,1)S(1)} %mix.5.mine_ref), channel_id=1, source_target_pairs={{0,2},{1,3},{2,0},{3,1},{4,6},{5,7},{6,4},{7,5},{8,10},{9,11},{10,... | collective-permute-start | bytes 122888 | tf_op jit(solution)/shard_map/mix/ppermute | solution.py:492
  52.2 5.1 %collective-permute-start.16 = (bf16[1,32,768]{2,1,0:T(8,128)(2,1)S(1)}, bf16[1,32,768]{2,1,0:T(8,128)(2,1)S(1)}, u32[]{:S(2)}, u32[]{:S(2)}) collective-permute-start(bf16[1,32,768]{2,1,0:T(8,128)(2,1)S(1)} %get-tuple-element.61.refs_0_), channel_id=1, source_target_pairs={{0,16},{4,20},{8,24},{12,28},{16,0},{20,4},{24,8},{28,12},{1,17},{... | collective-permute-start | bytes 147464 | tf_op jit(solution)/shard_map/mix/ppermute | solution.py:492
  57.3 10.0 %collective-permute-start.17 = (bf16[2,32,768]{2,1,0:T(8,128)(2,1)S(1)}, bf16[2,32,768]{2,1,0:T(8,128)(2,1)S(1)}, u32[]{:S(2)}, u32[]{:S(2)}) collective-permute-start(bf16[2,32,768]{2,1,0:T(8,128)(2,1)S(1)} %mix.7.own_ref), channel_id=1, source_target_pairs={{0,4},{4,0},{8,12},{12,8},{16,20},{20,16},{24,28},{28,24},{1,5},{5... | collective-permute-start | bytes 294920 | tf_op jit(solution)/shard_map/ffn/ppermute | solution.py:492
  58.3 6.6 %collective-permute-start.18 = (bf16[2,32,768]{2,1,0:T(8,128)(2,1)S(1)}, bf16[2,32,768]{2,1,0:T(8,128)(2,1)S(1)}, u32[]{:S(2)}, u32[]{:S(2)}) collective-permute-start(bf16[2,32,768]{2,1,0:T(8,128)(2,1)S(1)} %mix.7.own_ref), channel_id=1, source_target_pairs={{0,12},{4,8},{8,4},{12,0},{16,28},{20,24},{24,20},{28,16},{1,13},{... | collective-permute-start | bytes 294920 | tf_op jit(solution)/shard_map/ffn/ppermute | solution.py:492
  58.9 7.0 %collective-permute-start.22 = (bf16[2,32,768]{2,1,0:T(8,128)(2,1)S(1)}, bf16[2,32,768]{2,1,0:T(8,128)(2,1)S(1)}, u32[]{:S(2)}, u32[]{:S(2)}) collective-permute-start(bf16[2,32,768]{2,1,0:T(8,128)(2,1)S(1)} %mix.7.own_ref), channel_id=1, source_target_pairs={{0,8},{4,12},{8,0},{12,4},{16,24},{20,28},{24,16},{28,20},{1,9},{5... | collective-permute-start | bytes 294920 | tf_op jit(solution)/shard_map/ffn/ppermute | solution.py:492
  74.9 5.7 %collective-permute-start.26 = (bf16[2,32,640]{2,1,0:T(8,128)(2,1)S(1)}, bf16[2,32,640]{2,1,0:T(8,128)(2,1)S(1)}, u32[]{:S(2)}, u32[]{:S(2)}) collective-permute-start(bf16[2,32,640]{2,1,0:T(8,128)(2,1)S(1)} %ffn.29), channel_id=1, source_target_pairs={{0,12},{4,8},{8,4},{12,0},{16,28},{20,24},{24,20},{28,16},{1,13},{... | collective-permute-start | bytes 245768 | tf_op jit(solution)/shard_map/ffn/ppermute | solution.py:492
  75.3 6.5 %collective-permute-start.29 = (bf16[2,32,640]{2,1,0:T(8,128)(2,1)S(1)}, bf16[2,32,640]{2,1,0:T(8,128)(2,1)S(1)}, u32[]{:S(2)}, u32[]{:S(2)}) collective-permute-start(bf16[2,32,640]{2,1,0:T(8,128)(2,1)S(1)} %ffn.26.refs_0_), channel_id=1, source_target_pairs={{0,4},{4,0},{8,12},{12,8},{16,20},{20,16},{24,28},{28,24},{1,5},{5... | collective-permute-start | bytes 245768 | tf_op jit(solution)/shard_map/ffn/ppermute | solution.py:492
  77.0 4.7 %collective-permute-start.28 = (bf16[2,32,640]{2,1,0:T(8,128)(2,1)S(1)}, bf16[2,32,640]{2,1,0:T(8,128)(2,1)S(1)}, u32[]{:S(2)}, u32[]{:S(2)}) collective-permute-start(bf16[2,32,640]{2,1,0:T(8,128)(2,1)S(1)} %ffn.31), channel_id=1, source_target_pairs={{0,8},{4,12},{8,0},{12,4},{16,24},{20,28},{24,16},{28,20},{1,9},{5... | collective-permute-start | bytes 245768 | tf_op jit(solution)/shard_map/ffn/ppermute | solution.py:492
  81.8 5.0 %collective-permute-start.31 = (bf16[1,32,640]{2,1,0:T(8,128)(2,1)S(1)}, bf16[1,32,640]{2,1,0:T(8,128)(2,1)S(1)}, u32[]{:S(2)}, u32[]{:S(2)}) collective-permute-start(bf16[1,32,640]{2,1,0:T(8,128)(2,1)S(1)} %get-tuple-element.80), channel_id=1, source_target_pairs={{0,16},{4,20},{8,24},{12,28},{16,0},{20,4},{24,8},{28,12},{1,17},{... | collective-permute-start | bytes 122888 | tf_op jit(solution)/shard_map/ffn/ppermute | solution.py:492
  86.8 4.1 %collective-permute-start.32 = (bf16[1,32,640]{2,1,0:T(8,128)(2,1)S(1)}, bf16[1,32,640]{2,1,0:T(8,128)(2,1)S(1)}, u32[]{:S(2)}, u32[]{:S(2)}) collective-permute-start(bf16[1,32,640]{2,1,0:T(8,128)(2,1)S(1)} %ffn.33.mine_ref), channel_id=1, source_target_pairs={{0,2},{1,3},{2,0},{3,1},{4,6},{5,7},{6,4},{7,5},{8,10},{9,11},{10,... | collective-permute-start | bytes 122888 | tf_op jit(solution)/shard_map/ffn/ppermute | solution.py:492
  (25 other events, 131.0 us)

commit v5 on v4

--- a/solution.py
+++ b/solution.py
@@ -156,53 +156,56 @@
         out_ref[:, cols] = value.astype(BF16)
 
 
-def attend_kernel(heads, kv, steps, span, slot, seq_ref, len_ref, rows_ref, k_ref, v_ref, *refs):
-    q_buf, kn_buf, vn_buf, s_buf, o_buf, m_buf, l_buf, o_all, st_all = refs[-9:]
-    if slot == 0:
-        o_all, st_all = refs[:2]
+def attend_kernel(heads, kv, steps, span, slots, seq_ref, len_ref, *refs):
+    rows_refs, refs = refs[: len(slots)], refs[len(slots) :]
+    k_ref, v_ref, *outs = refs[:-7]
+    q_buf, kn_buf, vn_buf, s_buf, o_buf, m_buf, l_buf = refs[-7:]
     requests, rows_kv, hd = k_ref.shape
     cut = requests // 4
+    part = cut * steps
     group = heads // kv
     block = steps * heads
     fresh = steps * kv
     seq = seq_ref[0]
     first = seq * span
-    head_request = ((seq & 3) ^ slot) * cut
-
-    def spread(buf, index, place, per_step):
-        value = rows_ref[:, index * hd : (index + 1) * hd].astype(F32)
-        buf[pl.ds(place, cut * steps, stride=per_step), :] = value
-
-    for h in range(heads):
-        spread(q_buf, h, h, heads)
-    for g in range(kv):
-        spread(kn_buf, heads + g, g, kv)
-        spread(vn_buf, heads + kv + g, g, kv)
+    taken = [((seq & 3) ^ slot) * cut + r for slot in slots for r in range(cut)]
+
+    for n, rows_ref in enumerate(rows_refs):
+
+        def spread(buf, index, place, per_row):
+            value = rows_ref[:, index * hd : (index + 1) * hd].astype(F32)
+            buf[pl.ds(n * part * per_row + place, part, stride=per_row), :] = value
+
+        for h in range(heads):
+            spread(q_buf, h, h, heads)
+        for g in range(kv):
+            spread(kn_buf, heads + g, g, kv)
+            spread(vn_buf, heads + kv + g, g, kv)
     shrink = hd ** (-0.5)
     queries = q_buf[...].astype(BF16)
 
     row = lax.broadcasted_iota(jnp.int32, (block, rows_kv), 0)
     col = lax.broadcasted_iota(jnp.int32, (block, rows_kv), 1)
     need = jnp.where((row % heads) // group == col % kv, col // kv, 1 << 29)
-    for r in range(cut):
+    for r, request in enumerate(taken):
         scores = lax.dot_general(
             queries[r * block : (r + 1) * block],
-            k_ref[head_request + r],
+            k_ref[request],
             (((1,), (1,)), ((), ())),
             preferred_element_type=F32,
         )
-        live = need < len_ref[head_request + r] - first
+        live = need < len_ref[request] - first
         s_buf[r * block : (r + 1) * block, :] = jnp.where(live, scores * shrink, -1e30)
 
     k_new = kn_buf[...].astype(BF16)
     v_new = vn_buf[...].astype(BF16)
-    shape = (cut * block, cut * fresh)
+    shape = (len(taken) * block, len(taken) * fresh)
     row = lax.broadcasted_iota(jnp.int32, shape, 0)
     col = lax.broadcasted_iota(jnp.int32, shape, 1)
     col_row = lax.broadcasted_iota(jnp.int32, (1, shape[1]), 1)
     at_position = (col_row % fresh) // kv - first
-    for r in range(cut):
-        at_position += jnp.where(col_row // fresh == r, len_ref[head_request + r], 0)
+    for r, request in enumerate(taken):
+        at_position += jnp.where(col_row // fresh == r, len_ref[request], 0)
     held = (at_position >= 0) & (at_position < span)
     new_live = (
         (row // block == col // fresh)
@@ -223,24 +226,27 @@
     l_buf[...] = jnp.broadcast_to(total, l_buf.shape)
     expo = expo.astype(BF16)
     new_part = jnp.dot(new_expo.astype(BF16), v_new, preferred_element_type=F32)
-    for r in range(cut):
+    for r, request in enumerate(taken):
         mine = slice(r * block, (r + 1) * block)
-        o_buf[mine, :] = new_part[mine] + jnp.dot(
-            expo[mine], v_ref[head_request + r], preferred_element_type=F32
-        )
-
-    lane = lane_ids(cut * steps)
-    stats = jnp.zeros((cut * steps, LANES), F32)
-    for h in range(heads):
-        take = pl.ds(h, cut * steps, stride=heads)
-        o_all[:, h * hd : (h + 1) * hd] = o_buf[take, :]
-        stats = jnp.where(lane == h, m_buf[take, :], stats)
-        stats = jnp.where(lane == 24 + h, l_buf[take, :], stats)
-    st_all[...] = stats
-    if slot != 0:
-        msg_ref = refs[0]
-        msg_ref[:, : heads * hd] = o_all[...].astype(BF16)
-        msg_ref[:, heads * hd :] = pack_stats(st_all[...])
+        o_buf[mine, :] = new_part[mine] + jnp.dot(expo[mine], v_ref[request], preferred_element_type=F32)
+
+    lane = lane_ids(part)
+    for n, slot in enumerate(slots):
+        stats = jnp.zeros((part, LANES), F32)
+        for h in range(heads):
+            take = pl.ds(n * part * heads + h, part, stride=heads)
+            value = o_buf[take, :]
+            cols = slice(h * hd, (h + 1) * hd)
+            if slot:
+                outs[n][:, cols] = value.astype(BF16)
+            else:
+                outs[0][:, cols] = value
+            stats = jnp.where(lane == h, m_buf[take, :], stats)
+            stats = jnp.where(lane == 24 + h, l_buf[take, :], stats)
+        if slot:
+            outs[n][:, heads * hd :] = pack_stats(stats)
+        else:
+            outs[1][...] = stats
 
 
 def merged(heads, o_ref, st_ref, recv_refs):
@@ -352,8 +358,11 @@
     out_ref[...] = in_ref[...]
 
 
-def sum_kernel(mine_ref, recv_ref, msg_ref):
-    msg_ref[...] = (mine_ref[...].astype(F32) + recv_ref[...].astype(F32)).astype(BF16)
+def sum_kernel(mine_ref, recv_ref, *msg_refs):
+    count = mine_ref.shape[0] // len(msg_refs)
+    for i, ref in enumerate(msg_refs):
+        some = slice(i * count, (i + 1) * count)
+        ref[...] = (mine_ref[some].astype(F32) + recv_ref[some].astype(F32)).astype(BF16)
 
 
 def residual_kernel(steps, core_ref, x_ref, gain_ref, mine_ref, recv_ref, mixed_ref, piece_ref):
@@ -391,31 +400,45 @@
     return [new + ref[...] for new, ref in zip((squares, gate, up), so_far)] if so_far else (squares, gate, up)
 
 
-def products_kernel(masks, seq_ref, own_ref, far_ref, wg_ref, wu_ref, *refs):
-    found = gather_products(masks, seq_ref[0], own_ref, far_ref, wg_ref, wu_ref, refs[:-3])
-    for ref, value in zip(refs[-3:], found):
+def products_kernel(masks, features, taken, seq_ref, own_ref, far_ref, wg_ref, wu_ref, *refs):
+    copies = []
+    if taken:
+        w_hbm, *refs = refs
+        refs, w_refs, sems = refs[: -len(taken) - 1], refs[-len(taken) - 1 : -1], refs[-1]
+        for i, (some, w_ref) in enumerate(zip(taken, w_refs)):
+            width = w_ref.shape[2]
+            for j, mask in enumerate(some):
+                at = pl.multiple_of((seq_ref[0] ^ mask) * width, LANES)
+                copies.append(pltpu.make_async_copy(w_hbm.at[:, pl.ds(at, width)], w_ref.at[j], sems.at[i, j]))
+                copies[-1].start()
+    outs = refs[-1:] if features else refs[-3:]
+    found = gather_products(masks, seq_ref[0], own_ref, far_ref, wg_ref, wu_ref, refs[: -len(outs)])
+    if features:
+        found = [hidden_units(features, *found)]
+    for ref, value in zip(outs, found):
         ref[...] = value
-
-
-def hidden_kernel(masks, features, seq_ref, own_ref, far_ref, wg_ref, wu_ref, sq_ref, gate_ref, up_ref, h_ref):
-    squares, gate, up = gather_products(
-        masks, seq_ref[0], own_ref, far_ref, wg_ref, wu_ref, (sq_ref, gate_ref, up_ref)
-    )
+    for copy in copies:
+        copy.wait()
+
+
+def hidden_units(features, squares, gate, up):
     scale = lax.rsqrt(squares[:, 0:1] / features + 1e-05)
     gate = gate * scale
     up = up * scale
-    h_ref[...] = (gate / (1.0 + jnp.exp(-gate)) * up).astype(BF16)
-
-
-def down_kernel(masks, seq_ref, h_ref, w_ref, *refs):
+    return (gate / (1.0 + jnp.exp(-gate)) * up).astype(BF16)
+
+
+def down_kernel(count, h_ref, *refs):
     own_ref, far_ref = refs[-2:]
-    half, width = own_ref.shape[1:]
+    half = own_ref.shape[1]
     hidden = h_ref[...]
-    for j, mask in enumerate(masks):
-        take = pl.ds(pl.multiple_of((seq_ref[0] ^ mask) * width, LANES), width)
-        part = jnp.dot(hidden, w_ref[:, take], preferred_element_type=F32)
-        own_ref[j] = part[:half]
-        far_ref[j] = part[half:].astype(BF16)
+    at = 0
+    for w_ref in refs[:count]:
+        for j in range(w_ref.shape[0]):
+            part = jnp.dot(hidden, w_ref[j], preferred_element_type=F32)
+            own_ref[at + j] = part[:half]
+            far_ref[at + j] = part[half:].astype(BF16)
+        at += w_ref.shape[0]
 
 
 def fold_kernel(acc_ref, *refs):
@@ -540,29 +563,26 @@
             sds((part, LANES), F32),
             sds((part, heads * hd + LANES), BF16),
         ]
-        scratch = [
-            pltpu.VMEM((cut * block, hd), F32),
-            pltpu.VMEM((cut * fresh, hd), F32),
-            pltpu.VMEM((cut * fresh, hd), F32),
-            pltpu.VMEM((cut * block, flat[1]), F32),
-            pltpu.VMEM((cut * block, hd), F32),
-            pltpu.VMEM((cut * block, hd), F32),
-            pltpu.VMEM((cut * block, hd), F32),
-            pltpu.VMEM((part, heads * hd), F32),
-            pltpu.VMEM((part, LANES), F32),
-        ]
-
-        def attend(slot):
+        def attend(*some):
+            count = len(some) * cut
             return call(
-                functools.partial(attend_kernel, heads, kv, steps, span, slot),
-                joint[2:] if slot else joint[:2],
-                [SMEM, SMEM] + [VMEM] * 3,
-                scratch,
+                functools.partial(attend_kernel, heads, kv, steps, span, some),
+                joint[2:] * len(some) if some[0] else joint[:2],
+                [SMEM, SMEM] + [VMEM] * (len(some) + 2),
+                [
+                    pltpu.VMEM((count * block, hd), F32),
+                    pltpu.VMEM((count * fresh, hd), F32),
+                    pltpu.VMEM((count * fresh, hd), F32),
+                    pltpu.VMEM((count * block, flat[1]), F32),
+                    pltpu.VMEM((count * block, hd), F32),
+                    pltpu.VMEM((count * block, hd), F32),
+                    pltpu.VMEM((count * block, hd), F32),
+                ],
                 cost=20,
-            )(seq_arr, lengths, found[slot], k_flat, v_flat)
+            )(seq_arr, lengths, *(found[j] for j in some), k_flat, v_flat)
 
         o, st = attend(0)
-        arrived = [hop(attend(j)[0], "seq", j) for j in (3, 2, 1)]
+        arrived = [hop(msg, "seq", j) for some in ((3,), (1, 2)) for j, msg in zip(some, attend(*some))]
         for bit in rest:
             o, st, msg = call(
                 functools.partial(merge_kernel, heads), joint, [VMEM] * (2 + len(arrived))
@@ -622,49 +642,63 @@
         found = {j: hop(pieces, "seq", j) for j in (3, 2, 1)}
         found[0] = pieces
         order = (0, 3, 2, 1)
+        reads = ((3,), (2,), (1,), (0,))
         state = []
         earlier = []
+        quarter = {}
         for n, j in enumerate(order):
             piece = found[j]
             if n:
                 (piece,) = call(relay_kernel, [sds(piece.shape, BF16)], [VMEM] * 2, cost=1)(
                     piece, earlier[max(n - 2, 0)]
                 )
-            last = n == 3
+            taken = reads[n] if width % LANES == 0 else ()
             state = call(
-                functools.partial(hidden_kernel, slots[j], features)
-                if last
-                else functools.partial(products_kernel, slots[j]),
-                [sds((rows, hidden_width), BF16)]
-                if last
-                else [sds((rows, LANES), F32)] + [sds((rows, hidden_width), F32)] * 2,
-                [SMEM] + [VMEM] * (4 + len(state)),
+                functools.partial(
+                    products_kernel, slots[j], features if n == 3 else 0, [slots[i] for i in taken]
+                ),
+                (
+                    [sds((rows, hidden_width), BF16)]
+                    if n == 3
+                    else [sds((rows, LANES), F32)] + [sds((rows, hidden_width), F32)] * 2
+                )
+                + [sds((len(masks), hidden_width, width), BF16)] * len(taken),
+                [SMEM] + [VMEM] * 4 + [HBM] * (len(taken) > 0) + [VMEM] * len(state),
+                [pltpu.SemaphoreType.DMA((len(taken), len(masks)))] * (len(taken) > 0),
                 cost=1,
-            )(seq_arr, found[j], hop(piece, "tp", 1), w_gate, w_up, *state)
+            )(seq_arr, found[j], hop(piece, "tp", 1), w_gate, w_up, *[w_down] * (len(taken) > 0), *state)
+            if taken:
+                quarter.update(zip(taken, state[-len(taken) :]))
+                state = state[: -len(taken)]
             earlier.append(state[0])
         (hidden,) = state
 
-        shape = (len(masks), half, width)
-
         def down(some, *after):
-            if width % LANES == 0:
+            shape = (len(some) * len(masks), half, width)
+            if quarter:
                 return call(
-                    functools.partial(down_kernel, some),
+                    functools.partial(down_kernel, len(some)),
                     [sds(shape, F32), sds(shape, BF16)],
-                    [SMEM] + [VMEM] * (2 + len(after)),
+                    [VMEM] * (1 + len(some) + len(after)),
                     cost=1,
-                )(seq_arr, hidden, w_down, *after)
+                )(hidden, *(quarter[j] for j in some), *after)
             whole = jnp.dot(hidden, w_down, preferred_element_type=F32)
             whole = whole.reshape(rows, n_seq, width).transpose(1, 0, 2)
-            whole = jnp.take(whole, seq ^ jnp.array(some, jnp.int32), axis=0)
+            places = [m for j in some for m in slots[j]]
+            whole = jnp.take(whole, seq ^ jnp.array(places, jnp.int32), axis=0)
             return whole[:, :half], whole[:, half:].astype(BF16)
 
+        shape = (len(masks), half, width)
         arrived = []
-        for j in (3, 2, 1):
-            own, far = down(slots[j])
-            (msg,) = call(sum_kernel, [sds(shape, BF16)], [VMEM] * 2)(own, hop(far, "tp", 1))
-            arrived.append(hop(msg, "seq", j))
-        keep, far = down(slots[0], msg)
+        sent = []
+        after = []
+        for some in ((3,), (1, 2)):
+            own, far = down(some, *after)
+            after = [far]
+            msgs = call(sum_kernel, [sds(shape, BF16)] * len(some), [VMEM] * 2)(own, hop(far, "tp", 1))
+            sent += msgs
+            arrived += [hop(msg, "seq", j) for j, msg in zip(some, msgs)]
+        keep, far = down((0,), *sent)
         arrived.append(hop(far, "tp", 1))
         for bit in rest:
             shape = (keep.shape[0] // 2, half, width)

time: 93.2 us -> 91.1 us (0.977)
  local copies, waits for them, and re-layouts: 3.97 us -> 2.32 us
    unnamed x30, local copies, waits for them, and re-layouts: 3.05 us -> 1.39 us
    ppermute x34 -> x33, starting transfers between devices: 38.1 us -> 37.6 us  [hop(): return lax.ppermute(value, axis, [(i, i ^ bit) for i in range(size)])]
    pallas_call x15 -> x12, Pallas kernels: 11.1 us -> 11.3 us  [the longest x4 5.73 us: per_device(): call(functools.partial(products_kernel, slots[j], features if n == 3 else...]
    ppermute x34 -> x33, waiting for transfers between devices: 28.6 us -> 28.5 us  [hop(): return lax.ppermute(value, axis, [(i, i ^ bit) for i in range(size)])]
  transfers between devices with their start and end apart: 34 -> 33, of which waited for: 20 -> 19; matrix products, arithmetic and copies ran while one was open for 1% -> 1% of each run, Pallas kernels for 14% -> 15%
where the time goes in v5:
time: 91.1 us; the launch traced here: 90.9 us
  starting transfers between devices  37.6 us (41%)
  waiting for transfers between devices  28.5 us (31%)
  Pallas kernels  21.1 us (23%)
  local copies, waits for them, and re-layouts  2.32 us (3%)
  between operations  1.02 us (1%)
    ppermute x33, starting transfers between devices, hop(): return lax.ppermute(value, axis, [(i, i ^ bit) for i in range(size)])  37.6 us
    ppermute x33, waiting for transfers between devices, hop(): return lax.ppermute(value, axis, [(i, i ^ bit) for i in range(size)])  28.5 us
    pallas_call x4, Pallas kernels, per_device(): call(functools.partial(products_kernel, slots[j], features if n == 3 else...  5.73 us
    pallas_call x2, Pallas kernels, store(): call(functools.partial(store_kernel, column * hd, steps, span), [sds(flat...  4.52 us
    pallas_call x3, Pallas kernels, attend(): call(functools.partial(attend_kernel, heads, kv, steps, span, some), join...  3.3 us
    pallas_call x1, Pallas kernels, per_device(): call(functools.partial(project_kernel, steps), sums + sums[1:] * 2, [SMEM...  2.91 us
    pallas_call x3, Pallas kernels, down(): call(functools.partial(down_kernel, len(some)), [sds(shape, F32), sds(sha...  2.17 us
  transfers between devices with their start and end apart: 33, of which 19 were waited for; matrix products, arithmetic and copies ran while one was open for 1% of the time, Pallas kernels for 15%

profile of v5, /device:TPU:0, one launch (start us, length us, event | category | flops | bytes accessed | tf_op | source)
XLA Modules:
  0.0 90.9 jit_solution(5312388738872241609)
XLA Ops:
  0.6 2.9 %project.4 = (f32[16,1664]{1,0:T(8,128)}, bf16[16,1664]{1,0:T(8,128)(2,1)}, bf16[16,1664]{1,0:T(8,128)(2,1)}, bf16[16,1664]{1,0:T(8,128)(2,1)}) custom-call(s32[1]{0:T(128)} %bitcast.2.seq_ref, bf16[64,640]{1,0:T(8,128)(2,1)} %bitcast.22, bf16[640]{0:T(1024)(128)(2,1)} %gain_hbm.1, bf16[640,1024]{1,0:T(8,128)(2,1)} %wq_hbm.1, bf16[640,256]{1,0:T(8,128)(2,1)} %wk_hbm.1, ...), custom_call_target="tpu_custom_call" | custom-call | flops 3449999872 | bytes 1048576 | tf_op jit(solution)/shard_map/project/pallas_call | solution.py:531
  3.6 4.0 %collective-permute-start = (bf16[16,1664]{1,0:T(8,128)(2,1)}, bf16[16,1664]{1,0:T(8,128)(2,1)S(1)}, u32[]{:S(2)}, u32[]{:S(2)}) collective-permute-start(bf16[16,1664]{1,0:T(8,128)(2,1)} %get-tuple-element.51), channel_id=1, source_target_pairs={{0,12},{4,8},{8,4},{12,0},{16,28},{20,24},{24,20},{28,16},{1,13},{... | collective-permute-start | bytes 159752 | tf_op jit(solution)/shard_map/project/ppermute | solution.py:515
  9.9 2.0 %collective-permute-done.1.refs_1_ = bf16[16,1664]{1,0:T(8,128)(2,1)S(1)} collective-permute-done((bf16[16,1664]{1,0:T(8,128)(2,1)}, bf16[16,1664]{1,0:T(8,128)(2,1)S(1)}, u32[]{:S(2)}, u32[]{:S(2)}) %collective-permute-start.1) | collective-permute-done | bytes 53280 | tf_op jit(solution)/shard_map/project/ppermute | solution.py:515
  12.5 2.6 %collective-permute-start.3 = (bf16[16,1664]{1,0:T(8,128)(2,1)S(1)}, bf16[16,1664]{1,0:T(8,128)(2,1)S(1)}, u32[]{:S(2)}, u32[]{:S(2)}) collective-permute-start(bf16[16,1664]{1,0:T(8,128)(2,1)S(1)} %get-tuple-element.55), channel_id=1, source_target_pairs={{0,16},{4,20},{8,24},{12,28},{16,0},{20,4},{24,8},{28,12},{1,17},{... | collective-permute-start | bytes 159752 | tf_op jit(solution)/shard_map/project/ppermute | solution.py:515
  15.2 2.4 %collective-permute-done.3.recv_ref = bf16[16,1664]{1,0:T(8,128)(2,1)S(1)} collective-permute-done((bf16[16,1664]{1,0:T(8,128)(2,1)S(1)}, bf16[16,1664]{1,0:T(8,128)(2,1)S(1)}, u32[]{:S(2)}, u32[]{:S(2)}) %collective-permute-start.3) | collective-permute-done | bytes 53280 | tf_op jit(solution)/shard_map/project/ppermute | solution.py:515
  17.8 1.6 %collective-permute-start.4 = (bf16[16,1536]{1,0:T(8,128)(2,1)S(1)}, bf16[16,1536]{1,0:T(8,128)(2,1)S(1)}, u32[]{:S(2)}, u32[]{:S(2)}) collective-permute-start(bf16[16,1536]{1,0:T(8,128)(2,1)S(1)} %project.7.refs_0_), channel_id=1, source_target_pairs={{0,12},{4,8},{8,4},{12,0},{16,28},{20,24},{24,20},{28,16},{1,13},{... | collective-permute-start | bytes 147464 | tf_op jit(solution)/shard_map/project/ppermute | solution.py:515
  19.7 1.7 %collective-permute-start.6 = (bf16[16,1536]{1,0:T(8,128)(2,1)S(1)}, bf16[16,1536]{1,0:T(8,128)(2,1)S(1)}, u32[]{:S(2)}, u32[]{:S(2)}) collective-permute-start(bf16[16,1536]{1,0:T(8,128)(2,1)S(1)} %project.7.refs_0_), channel_id=1, source_target_pairs={{0,4},{4,0},{8,12},{12,8},{16,20},{20,16},{24,28},{28,24},{1,5},{5... | collective-permute-start | bytes 147464 | tf_op jit(solution)/shard_map/project/ppermute | solution.py:515
  21.4 1.5 %collective-permute-done.4.refs_0_.refs_3_ = bf16[16,1536]{1,0:T(8,128)(2,1)S(1)} collective-permute-done((bf16[16,1536]{1,0:T(8,128)(2,1)S(1)}, bf16[16,1536]{1,0:T(8,128)(2,1)S(1)}, u32[]{:S(2)}, u32[]{:S(2)}) %collective-permute-start.4) | collective-permute-done | bytes 49184 | tf_op jit(solution)/shard_map/project/ppermute | solution.py:515
  24.0 1.6 %collective-permute-start.5 = (bf16[16,1152]{1,0:T(8,128)(2,1)S(1)}, bf16[16,1152]{1,0:T(8,128)(2,1)S(1)}, u32[]{:S(2)}, u32[]{:S(2)}) collective-permute-start(bf16[16,1152]{1,0:T(8,128)(2,1)S(1)} %attend.8), channel_id=1, source_target_pairs={{0,12},{4,8},{8,4},{12,0},{16,28},{20,24},{24,20},{28,16},{1,13},{... | collective-permute-start | bytes 110600 | tf_op jit(solution)/shard_map/attend/ppermute | solution.py:515
  26.8 1.5 %collective-permute-start.8 = (bf16[16,1152]{1,0:T(8,128)(2,1)S(1)}, bf16[16,1152]{1,0:T(8,128)(2,1)S(1)}, u32[]{:S(2)}, u32[]{:S(2)}) collective-permute-start(bf16[16,1152]{1,0:T(8,128)(2,1)S(1)} %get-tuple-element.58), channel_id=1, source_target_pairs={{0,4},{4,0},{8,12},{12,8},{16,20},{20,16},{24,28},{28,24},{1,5},{5... | collective-permute-start | bytes 110600 | tf_op jit(solution)/shard_map/attend/ppermute | solution.py:515
  32.5 3.1 %collective-permute-start.10 = (bf16[16,1152]{1,0:T(8,128)(2,1)S(1)}, bf16[16,1152]{1,0:T(8,128)(2,1)S(1)}, u32[]{:S(2)}, u32[]{:S(2)}) collective-permute-start(bf16[16,1152]{1,0:T(8,128)(2,1)S(1)} %get-tuple-element.62), channel_id=1, source_target_pairs={{0,16},{4,20},{8,24},{12,28},{16,0},{20,4},{24,8},{28,12},{1,17},{... | collective-permute-start | bytes 110600 | tf_op jit(solution)/shard_map/attend/ppermute | solution.py:515
  35.6 2.3 %attend.11 = (bf16[16,256,128]{2,1,0:T(8,128)(2,1)}, f32[16,128]{1,0:T(8,128)S(1)}) custom-call(s32[1]{0:T(128)} %bitcast.2.seq_ref, s32[16]{0:T(128)S(1)} %copy-done.4, bf16[16,1536]{1,0:T(8,128)(2,1)S(1)} %project.7.refs_0_, bf16[16,1536]{1,0:T(8,128)(2,1)S(1)} %collective-permute-done.6.refs_0_.refs_1_, ...), custom_call_target="tpu_custom_call" | custom-call | flops 3449999872 | bytes 1048576 | tf_op jit(solution)/shard_map/attend/pallas_call | solution.py:593
  41.7 2.3 %attend.13 = (bf16[16,256,128]{2,1,0:T(8,128)(2,1)}, f32[16,128]{1,0:T(8,128)S(1)}) custom-call(s32[1]{0:T(128)} %bitcast.2.seq_ref, s32[16]{0:T(128)S(1)} %copy-done.4, bf16[16,1536]{1,0:T(8,128)(2,1)S(1)} %project.7.refs_0_, bf16[16,1536]{1,0:T(8,128)(2,1)S(1)} %collective-permute-done.6.refs_0_.refs_1_, ...), custom_call_target="tpu_custom_call" | custom-call | flops 3449999872 | bytes 1048576 | tf_op jit(solution)/shard_map/attend/pallas_call | solution.py:593
  45.9 1.6 %collective-permute-start.15 = (bf16[32,640]{1,0:T(8,128)(2,1)S(1)}, bf16[32,640]{1,0:T(8,128)(2,1)S(1)}, u32[]{:S(2)}, u32[]{:S(2)}) collective-permute-start(bf16[32,640]{1,0:T(8,128)(2,1)S(1)} %mix.5.mine_ref), channel_id=1, source_target_pairs={{0,2},{1,3},{2,0},{3,1},{4,6},{5,7},{6,4},{7,5},{8,10},{9,11},{10,... | collective-permute-start | bytes 122888 | tf_op jit(solution)/shard_map/mix/ppermute | solution.py:515
  48.2 1.7 %collective-permute-done.15.recv_ref = bf16[32,640]{1,0:T(8,128)(2,1)S(1)} collective-permute-done((bf16[32,640]{1,0:T(8,128)(2,1)S(1)}, bf16[32,640]{1,0:T(8,128)(2,1)S(1)}, u32[]{:S(2)}, u32[]{:S(2)}) %collective-permute-start.15) | collective-permute-done | bytes 40992 | tf_op jit(solution)/shard_map/mix/ppermute | solution.py:515
  50.3 2.6 %collective-permute-start.16 = (bf16[1,32,768]{2,1,0:T(8,128)(2,1)S(1)}, bf16[1,32,768]{2,1,0:T(8,128)(2,1)S(1)}, u32[]{:S(2)}, u32[]{:S(2)}) collective-permute-start(bf16[1,32,768]{2,1,0:T(8,128)(2,1)S(1)} %get-tuple-element.70.refs_0_), channel_id=1, source_target_pairs={{0,16},{4,20},{8,24},{12,28},{16,0},{20,4},{24,8},{28,12},{1,17},{... | collective-permute-start | bytes 147464 | tf_op jit(solution)/shard_map/mix/ppermute | solution.py:515
  52.9 2.9 %collective-permute-done.16.refs_1_ = bf16[1,32,768]{2,1,0:T(8,128)(2,1)S(1)} collective-permute-done((bf16[1,32,768]{2,1,0:T(8,128)(2,1)S(1)}, bf16[1,32,768]{2,1,0:T(8,128)(2,1)S(1)}, u32[]{:S(2)}, u32[]{:S(2)}) %collective-permute-start.16) | collective-permute-done | bytes 49184 | tf_op jit(solution)/shard_map/mix/ppermute | solution.py:515
  56.3 2.4 %collective-permute-start.18 = (bf16[2,32,768]{2,1,0:T(8,128)(2,1)S(1)}, bf16[2,32,768]{2,1,0:T(8,128)(2,1)S(1)}, u32[]{:S(2)}, u32[]{:S(2)}) collective-permute-start(bf16[2,32,768]{2,1,0:T(8,128)(2,1)S(1)} %mix.7.own_ref), channel_id=1, source_target_pairs={{0,12},{4,8},{8,4},{12,0},{16,28},{20,24},{24,20},{28,16},{1,13},{... | collective-permute-start | bytes 294920 | tf_op jit(solution)/shard_map/ffn/ppermute | solution.py:515
  61.5 2.5 %collective-permute-done.18.in_ref.own_ref = bf16[2,32,768]{2,1,0:T(8,128)(2,1)S(1)} collective-permute-done((bf16[2,32,768]{2,1,0:T(8,128)(2,1)S(1)}, bf16[2,32,768]{2,1,0:T(8,128)(2,1)S(1)}, u32[]{:S(2)}, u32[]{:S(2)}) %collective-permute-start.18) | collective-permute-done | bytes 98336 | tf_op jit(solution)/shard_map/ffn/ppermute | solution.py:515
  78.0 1.7 %collective-permute-done.27.refs_1_ = bf16[2,32,640]{2,1,0:T(8,128)(2,1)S(1)} collective-permute-done((bf16[2,32,640]{2,1,0:T(8,128)(2,1)S(1)}, bf16[2,32,640]{2,1,0:T(8,128)(2,1)S(1)}, u32[]{:S(2)}, u32[]{:S(2)}) %collective-permute-start.27) | collective-permute-done | bytes 81952 | tf_op jit(solution)/shard_map/ffn/ppermute | solution.py:515
  79.7 2.4 %collective-permute-start.30 = (bf16[1,32,640]{2,1,0:T(8,128)(2,1)S(1)}, bf16[1,32,640]{2,1,0:T(8,128)(2,1)S(1)}, u32[]{:S(2)}, u32[]{:S(2)}) collective-permute-start(bf16[1,32,640]{2,1,0:T(8,128)(2,1)S(1)} %get-tuple-element.94), channel_id=1, source_target_pairs={{0,16},{4,20},{8,24},{12,28},{16,0},{20,4},{24,8},{28,12},{1,17},{... | collective-permute-start | bytes 122888 | tf_op jit(solution)/shard_map/ffn/ppermute | solution.py:515
  82.2 2.5 %collective-permute-done.30.recv_ref = bf16[1,32,640]{2,1,0:T(8,128)(2,1)S(1)} collective-permute-done((bf16[1,32,640]{2,1,0:T(8,128)(2,1)S(1)}, bf16[1,32,640]{2,1,0:T(8,128)(2,1)S(1)}, u32[]{:S(2)}, u32[]{:S(2)}) %collective-permute-start.30) | collective-permute-done | bytes 40992 | tf_op jit(solution)/shard_map/ffn/ppermute | solution.py:515
  84.7 1.6 %collective-permute-start.31 = (bf16[1,32,640]{2,1,0:T(8,128)(2,1)S(1)}, bf16[1,32,640]{2,1,0:T(8,128)(2,1)S(1)}, u32[]{:S(2)}, u32[]{:S(2)}) collective-permute-start(bf16[1,32,640]{2,1,0:T(8,128)(2,1)S(1)} %ffn.29.mine_ref), channel_id=1, source_target_pairs={{0,2},{1,3},{2,0},{3,1},{4,6},{5,7},{6,4},{7,5},{8,10},{9,11},{10,... | collective-permute-start | bytes 122888 | tf_op jit(solution)/shard_map/ffn/ppermute | solution.py:515
  86.3 2.5 %collective-permute-done.31.recv_ref = bf16[1,32,640]{2,1,0:T(8,128)(2,1)S(1)} collective-permute-done((bf16[1,32,640]{2,1,0:T(8,128)(2,1)S(1)}, bf16[1,32,640]{2,1,0:T(8,128)(2,1)S(1)}, u32[]{:S(2)}, u32[]{:S(2)}) %collective-permute-start.31) | collective-permute-done | bytes 40992 | tf_op jit(solution)/shard_map/ffn/ppermute | solution.py:515
  (114 shorter events, 35.8 us)
Async XLA Ops:
  3.6 6.3 %collective-permute-start = (bf16[16,1664]{1,0:T(8,128)(2,1)}, bf16[16,1664]{1,0:T(8,128)(2,1)S(1)}, u32[]{:S(2)}, u32[]{:S(2)}) collective-permute-start(bf16[16,1664]{1,0:T(8,128)(2,1)} %get-tuple-element.51), channel_id=1, source_target_pairs={{0,12},{4,8},{8,4},{12,0},{16,28},{20,24},{24,20},{28,16},{1,13},{... | collective-permute-start | bytes 159752 | tf_op jit(solution)/shard_map/project/ppermute | solution.py:515
  7.6 4.3 %collective-permute-start.1 = (bf16[16,1664]{1,0:T(8,128)(2,1)}, bf16[16,1664]{1,0:T(8,128)(2,1)S(1)}, u32[]{:S(2)}, u32[]{:S(2)}) collective-permute-start(bf16[16,1664]{1,0:T(8,128)(2,1)} %get-tuple-element.52), channel_id=1, source_target_pairs={{0,8},{4,12},{8,0},{12,4},{16,24},{20,28},{24,16},{28,20},{1,9},{5... | collective-permute-start | bytes 159752 | tf_op jit(solution)/shard_map/project/ppermute | solution.py:515
  8.0 4.3 %collective-permute-start.2 = (bf16[16,1664]{1,0:T(8,128)(2,1)}, bf16[16,1664]{1,0:T(8,128)(2,1)S(1)}, u32[]{:S(2)}, u32[]{:S(2)}) collective-permute-start(bf16[16,1664]{1,0:T(8,128)(2,1)} %get-tuple-element.53), channel_id=1, source_target_pairs={{0,4},{4,0},{8,12},{12,8},{16,20},{20,16},{24,28},{28,24},{1,5},{5... | collective-permute-start | bytes 159752 | tf_op jit(solution)/shard_map/project/ppermute | solution.py:515
  12.5 5.1 %collective-permute-start.3 = (bf16[16,1664]{1,0:T(8,128)(2,1)S(1)}, bf16[16,1664]{1,0:T(8,128)(2,1)S(1)}, u32[]{:S(2)}, u32[]{:S(2)}) collective-permute-start(bf16[16,1664]{1,0:T(8,128)(2,1)S(1)} %get-tuple-element.55), channel_id=1, source_target_pairs={{0,16},{4,20},{8,24},{12,28},{16,0},{20,4},{24,8},{28,12},{1,17},{... | collective-permute-start | bytes 159752 | tf_op jit(solution)/shard_map/project/ppermute | solution.py:515
  17.8 5.1 %collective-permute-start.4 = (bf16[16,1536]{1,0:T(8,128)(2,1)S(1)}, bf16[16,1536]{1,0:T(8,128)(2,1)S(1)}, u32[]{:S(2)}, u32[]{:S(2)}) collective-permute-start(bf16[16,1536]{1,0:T(8,128)(2,1)S(1)} %project.7.refs_0_), channel_id=1, source_target_pairs={{0,12},{4,8},{8,4},{12,0},{16,28},{20,24},{24,20},{28,16},{1,13},{... | collective-permute-start | bytes 147464 | tf_op jit(solution)/shard_map/project/ppermute | solution.py:515
  19.5 6.1 %collective-permute-start.7 = (bf16[16,1536]{1,0:T(8,128)(2,1)S(1)}, bf16[16,1536]{1,0:T(8,128)(2,1)S(1)}, u32[]{:S(2)}, u32[]{:S(2)}) collective-permute-start(bf16[16,1536]{1,0:T(8,128)(2,1)S(1)} %project.7.refs_0_), channel_id=1, source_target_pairs={{0,8},{4,12},{8,0},{12,4},{16,24},{20,28},{24,16},{28,20},{1,9},{5... | collective-permute-start | bytes 147464 | tf_op jit(solution)/shard_map/project/ppermute | solution.py:515
  19.7 5.9 %collective-permute-start.6 = (bf16[16,1536]{1,0:T(8,128)(2,1)S(1)}, bf16[16,1536]{1,0:T(8,128)(2,1)S(1)}, u32[]{:S(2)}, u32[]{:S(2)}) collective-permute-start(bf16[16,1536]{1,0:T(8,128)(2,1)S(1)} %project.7.refs_0_), channel_id=1, source_target_pairs={{0,4},{4,0},{8,12},{12,8},{16,20},{20,16},{24,28},{28,24},{1,5},{5... | collective-permute-start | bytes 147464 | tf_op jit(solution)/shard_map/project/ppermute | solution.py:515
  24.0 5.8 %collective-permute-start.5 = (bf16[16,1152]{1,0:T(8,128)(2,1)S(1)}, bf16[16,1152]{1,0:T(8,128)(2,1)S(1)}, u32[]{:S(2)}, u32[]{:S(2)}) collective-permute-start(bf16[16,1152]{1,0:T(8,128)(2,1)S(1)} %attend.8), channel_id=1, source_target_pairs={{0,12},{4,8},{8,4},{12,0},{16,28},{20,24},{24,20},{28,16},{1,13},{... | collective-permute-start | bytes 110600 | tf_op jit(solution)/shard_map/attend/ppermute | solution.py:515
  26.8 4.0 %collective-permute-start.8 = (bf16[16,1152]{1,0:T(8,128)(2,1)S(1)}, bf16[16,1152]{1,0:T(8,128)(2,1)S(1)}, u32[]{:S(2)}, u32[]{:S(2)}) collective-permute-start(bf16[16,1152]{1,0:T(8,128)(2,1)S(1)} %get-tuple-element.58), channel_id=1, source_target_pairs={{0,4},{4,0},{8,12},{12,8},{16,20},{20,16},{24,28},{28,24},{1,5},{5... | collective-permute-start | bytes 110600 | tf_op jit(solution)/shard_map/attend/ppermute | solution.py:515
  28.3 4.0 %collective-permute-start.9 = (bf16[16,1152]{1,0:T(8,128)(2,1)S(1)}, bf16[16,1152]{1,0:T(8,128)(2,1)S(1)}, u32[]{:S(2)}, u32[]{:S(2)}) collective-permute-start(bf16[16,1152]{1,0:T(8,128)(2,1)S(1)} %get-tuple-element.59), channel_id=1, source_target_pairs={{0,8},{4,12},{8,0},{12,4},{16,24},{20,28},{24,16},{28,20},{1,9},{5... | collective-permute-start | bytes 110600 | tf_op jit(solution)/shard_map/attend/ppermute | solution.py:515
  32.5 5.4 %collective-permute-start.10 = (bf16[16,1152]{1,0:T(8,128)(2,1)S(1)}, bf16[16,1152]{1,0:T(8,128)(2,1)S(1)}, u32[]{:S(2)}, u32[]{:S(2)}) collective-permute-start(bf16[16,1152]{1,0:T(8,128)(2,1)S(1)} %get-tuple-element.62), channel_id=1, source_target_pairs={{0,16},{4,20},{8,24},{12,28},{16,0},{20,4},{24,8},{28,12},{1,17},{... | collective-permute-start | bytes 110600 | tf_op jit(solution)/shard_map/attend/ppermute | solution.py:515
  38.2 5.8 %collective-permute-start.13 = (bf16[16,1024]{1,0:T(8,128)(2,1)S(1)}, bf16[16,1024]{1,0:T(8,128)(2,1)S(1)}, u32[]{:S(2)}, u32[]{:S(2)}) collective-permute-start(bf16[16,1024]{1,0:T(8,128)(2,1)S(1)} %get-tuple-element.64.a0_ref), channel_id=1, source_target_pairs={{0,12},{4,8},{8,4},{12,0},{16,28},{20,24},{24,20},{28,16},{1,13},{... | collective-permute-start | bytes 98312 | tf_op jit(solution)/shard_map/attend/ppermute | solution.py:515
  38.9 5.1 %collective-permute-start.12 = (bf16[16,1024]{1,0:T(8,128)(2,1)S(1)}, bf16[16,1024]{1,0:T(8,128)(2,1)S(1)}, u32[]{:S(2)}, u32[]{:S(2)}) collective-permute-start(bf16[16,1024]{1,0:T(8,128)(2,1)S(1)} %get-tuple-element.64.a0_ref), channel_id=1, source_target_pairs={{0,8},{4,12},{8,0},{12,4},{16,24},{20,28},{24,16},{28,20},{1,9},{5... | collective-permute-start | bytes 98312 | tf_op jit(solution)/shard_map/attend/ppermute | solution.py:515
  40.2 3.9 %collective-permute-start.11 = (bf16[16,1024]{1,0:T(8,128)(2,1)S(1)}, bf16[16,1024]{1,0:T(8,128)(2,1)S(1)}, u32[]{:S(2)}, u32[]{:S(2)}) collective-permute-start(bf16[16,1024]{1,0:T(8,128)(2,1)S(1)} %get-tuple-element.64.a0_ref), channel_id=1, source_target_pairs={{0,4},{4,0},{8,12},{12,8},{16,20},{20,16},{24,28},{28,24},{1,5},{5... | collective-permute-start | bytes 98312 | tf_op jit(solution)/shard_map/attend/ppermute | solution.py:515
  45.9 4.1 %collective-permute-start.15 = (bf16[32,640]{1,0:T(8,128)(2,1)S(1)}, bf16[32,640]{1,0:T(8,128)(2,1)S(1)}, u32[]{:S(2)}, u32[]{:S(2)}) collective-permute-start(bf16[32,640]{1,0:T(8,128)(2,1)S(1)} %mix.5.mine_ref), channel_id=1, source_target_pairs={{0,2},{1,3},{2,0},{3,1},{4,6},{5,7},{6,4},{7,5},{8,10},{9,11},{10,... | collective-permute-start | bytes 122888 | tf_op jit(solution)/shard_map/mix/ppermute | solution.py:515
  50.3 5.6 %collective-permute-start.16 = (bf16[1,32,768]{2,1,0:T(8,128)(2,1)S(1)}, bf16[1,32,768]{2,1,0:T(8,128)(2,1)S(1)}, u32[]{:S(2)}, u32[]{:S(2)}) collective-permute-start(bf16[1,32,768]{2,1,0:T(8,128)(2,1)S(1)} %get-tuple-element.70.refs_0_), channel_id=1, source_target_pairs={{0,16},{4,20},{8,24},{12,28},{16,0},{20,4},{24,8},{28,12},{1,17},{... | collective-permute-start | bytes 147464 | tf_op jit(solution)/shard_map/mix/ppermute | solution.py:515
  56.0 8.1 %collective-permute-start.22 = (bf16[2,32,768]{2,1,0:T(8,128)(2,1)S(1)}, bf16[2,32,768]{2,1,0:T(8,128)(2,1)S(1)}, u32[]{:S(2)}, u32[]{:S(2)}) collective-permute-start(bf16[2,32,768]{2,1,0:T(8,128)(2,1)S(1)} %mix.7.own_ref), channel_id=1, source_target_pairs={{0,8},{4,12},{8,0},{12,4},{16,24},{20,28},{24,16},{28,20},{1,9},{5... | collective-permute-start | bytes 294920 | tf_op jit(solution)/shard_map/ffn/ppermute | solution.py:515
  56.3 7.7 %collective-permute-start.18 = (bf16[2,32,768]{2,1,0:T(8,128)(2,1)S(1)}, bf16[2,32,768]{2,1,0:T(8,128)(2,1)S(1)}, u32[]{:S(2)}, u32[]{:S(2)}) collective-permute-start(bf16[2,32,768]{2,1,0:T(8,128)(2,1)S(1)} %mix.7.own_ref), channel_id=1, source_target_pairs={{0,12},{4,8},{8,4},{12,0},{16,28},{20,24},{24,20},{28,16},{1,13},{... | collective-permute-start | bytes 294920 | tf_op jit(solution)/shard_map/ffn/ppermute | solution.py:515
  58.7 8.1 %collective-permute-start.17 = (bf16[2,32,768]{2,1,0:T(8,128)(2,1)S(1)}, bf16[2,32,768]{2,1,0:T(8,128)(2,1)S(1)}, u32[]{:S(2)}, u32[]{:S(2)}) collective-permute-start(bf16[2,32,768]{2,1,0:T(8,128)(2,1)S(1)} %mix.7.own_ref), channel_id=1, source_target_pairs={{0,4},{4,0},{8,12},{12,8},{16,20},{20,16},{24,28},{28,24},{1,5},{5... | collective-permute-start | bytes 294920 | tf_op jit(solution)/shard_map/ffn/ppermute | solution.py:515
  72.3 5.7 %collective-permute-start.26 = (bf16[2,32,640]{2,1,0:T(8,128)(2,1)S(1)}, bf16[2,32,640]{2,1,0:T(8,128)(2,1)S(1)}, u32[]{:S(2)}, u32[]{:S(2)}) collective-permute-start(bf16[2,32,640]{2,1,0:T(8,128)(2,1)S(1)} %ffn.24.refs_1_), channel_id=1, source_target_pairs={{0,12},{4,8},{8,4},{12,0},{16,28},{20,24},{24,20},{28,16},{1,13},{... | collective-permute-start | bytes 245768 | tf_op jit(solution)/shard_map/ffn/ppermute | solution.py:515
  74.3 5.4 %collective-permute-start.27 = (bf16[2,32,640]{2,1,0:T(8,128)(2,1)S(1)}, bf16[2,32,640]{2,1,0:T(8,128)(2,1)S(1)}, u32[]{:S(2)}, u32[]{:S(2)}) collective-permute-start(bf16[2,32,640]{2,1,0:T(8,128)(2,1)S(1)} %get-tuple-element.89.refs_2_), channel_id=1, source_target_pairs={{0,4},{4,0},{8,12},{12,8},{16,20},{20,16},{24,28},{28,24},{1,5},{5... | collective-permute-start | bytes 245768 | tf_op jit(solution)/shard_map/ffn/ppermute | solution.py:515
  75.2 4.5 %collective-permute-start.28 = (bf16[2,32,640]{2,1,0:T(8,128)(2,1)S(1)}, bf16[2,32,640]{2,1,0:T(8,128)(2,1)S(1)}, u32[]{:S(2)}, u32[]{:S(2)}) collective-permute-start(bf16[2,32,640]{2,1,0:T(8,128)(2,1)S(1)} %get-tuple-element.90.refs_3_), channel_id=1, source_target_pairs={{0,8},{4,12},{8,0},{12,4},{16,24},{20,28},{24,16},{28,20},{1,9},{5... | collective-permute-start | bytes 245768 | tf_op jit(solution)/shard_map/ffn/ppermute | solution.py:515
  79.7 5.0 %collective-permute-start.30 = (bf16[1,32,640]{2,1,0:T(8,128)(2,1)S(1)}, bf16[1,32,640]{2,1,0:T(8,128)(2,1)S(1)}, u32[]{:S(2)}, u32[]{:S(2)}) collective-permute-start(bf16[1,32,640]{2,1,0:T(8,128)(2,1)S(1)} %get-tuple-element.94), channel_id=1, source_target_pairs={{0,16},{4,20},{8,24},{12,28},{16,0},{20,4},{24,8},{28,12},{1,17},{... | collective-permute-start | bytes 122888 | tf_op jit(solution)/shard_map/ffn/ppermute | solution.py:515
  84.7 4.1 %collective-permute-start.31 = (bf16[1,32,640]{2,1,0:T(8,128)(2,1)S(1)}, bf16[1,32,640]{2,1,0:T(8,128)(2,1)S(1)}, u32[]{:S(2)}, u32[]{:S(2)}) collective-permute-start(bf16[1,32,640]{2,1,0:T(8,128)(2,1)S(1)} %ffn.29.mine_ref), channel_id=1, source_target_pairs={{0,2},{1,3},{2,0},{3,1},{4,6},{5,7},{6,4},{7,5},{8,10},{9,11},{10,... | collective-permute-start | bytes 122888 | tf_op jit(solution)/shard_map/ffn/ppermute | solution.py:515
  (24 other events, 129.7 us)

commit v6 on v5

--- a/solution.py
+++ b/solution.py
@@ -641,7 +641,7 @@
     with jax.named_scope("ffn"):
         found = {j: hop(pieces, "seq", j) for j in (3, 2, 1)}
         found[0] = pieces
-        order = (0, 3, 2, 1)
+        order = (0, 2, 1, 3)
         reads = ((3,), (2,), (1,), (0,))
         state = []
         earlier = []

time: 91.1 us -> 89.9 us (0.987)
  no operation moved by 1% of the time
where the time goes in v6:
time: 89.9 us; the launch traced here: 89.8 us
  starting transfers between devices  37.1 us (41%)
  waiting for transfers between devices  27.9 us (31%)
  Pallas kernels  21.1 us (23%)
  local copies, waits for them, and re-layouts  2.32 us (3%)
  between operations  1.02 us (1%)
    ppermute x33, starting transfers between devices, hop(): return lax.ppermute(value, axis, [(i, i ^ bit) for i in range(size)])  37.1 us
    ppermute x33, waiting for transfers between devices, hop(): return lax.ppermute(value, axis, [(i, i ^ bit) for i in range(size)])  27.9 us
    pallas_call x4, Pallas kernels, per_device(): call(functools.partial(products_kernel, slots[j], features if n == 3 else...  5.74 us
    pallas_call x2, Pallas kernels, store(): call(functools.partial(store_kernel, column * hd, steps, span), [sds(flat...  4.52 us
    pallas_call x3, Pallas kernels, attend(): call(functools.partial(attend_kernel, heads, kv, steps, span, some), join...  3.3 us
    pallas_call x1, Pallas kernels, per_device(): call(functools.partial(project_kernel, steps), sums + sums[1:] * 2, [SMEM...  2.91 us
    pallas_call x3, Pallas kernels, down(): call(functools.partial(down_kernel, len(some)), [sds(shape, F32), sds(sha...  2.17 us
  transfers between devices with their start and end apart: 33, of which 19 were waited for; matrix products, arithmetic and copies ran while one was open for 1% of the time, Pallas kernels for 15%

profile of v6, /device:TPU:0, one launch (start us, length us, event | category | flops | bytes accessed | tf_op | source)
XLA Modules:
  0.0 89.8 jit_solution(14353538318354577521)
XLA Ops:
  0.6 2.9 %project.4 = (f32[16,1664]{1,0:T(8,128)}, bf16[16,1664]{1,0:T(8,128)(2,1)}, bf16[16,1664]{1,0:T(8,128)(2,1)}, bf16[16,1664]{1,0:T(8,128)(2,1)}) custom-call(s32[1]{0:T(128)} %bitcast.2.seq_ref, bf16[64,640]{1,0:T(8,128)(2,1)} %bitcast.22, bf16[640]{0:T(1024)(128)(2,1)} %gain_hbm.1, bf16[640,1024]{1,0:T(8,128)(2,1)} %wq_hbm.1, bf16[640,256]{1,0:T(8,128)(2,1)} %wk_hbm.1, ...), custom_call_target="tpu_custom_call" | custom-call | flops 3449999872 | bytes 1048576 | tf_op jit(solution)/shard_map/project/pallas_call | solution.py:531
  3.6 4.0 %collective-permute-start = (bf16[16,1664]{1,0:T(8,128)(2,1)}, bf16[16,1664]{1,0:T(8,128)(2,1)S(1)}, u32[]{:S(2)}, u32[]{:S(2)}) collective-permute-start(bf16[16,1664]{1,0:T(8,128)(2,1)} %get-tuple-element.51), channel_id=1, source_target_pairs={{0,12},{4,8},{8,4},{12,0},{16,28},{20,24},{24,20},{28,16},{1,13},{... | collective-permute-start | bytes 159752 | tf_op jit(solution)/shard_map/project/ppermute | solution.py:515
  9.9 2.0 %collective-permute-done.1.refs_1_ = bf16[16,1664]{1,0:T(8,128)(2,1)S(1)} collective-permute-done((bf16[16,1664]{1,0:T(8,128)(2,1)}, bf16[16,1664]{1,0:T(8,128)(2,1)S(1)}, u32[]{:S(2)}, u32[]{:S(2)}) %collective-permute-start.1) | collective-permute-done | bytes 53280 | tf_op jit(solution)/shard_map/project/ppermute | solution.py:515
  12.5 2.6 %collective-permute-start.3 = (bf16[16,1664]{1,0:T(8,128)(2,1)S(1)}, bf16[16,1664]{1,0:T(8,128)(2,1)S(1)}, u32[]{:S(2)}, u32[]{:S(2)}) collective-permute-start(bf16[16,1664]{1,0:T(8,128)(2,1)S(1)} %get-tuple-element.55), channel_id=1, source_target_pairs={{0,16},{4,20},{8,24},{12,28},{16,0},{20,4},{24,8},{28,12},{1,17},{... | collective-permute-start | bytes 159752 | tf_op jit(solution)/shard_map/project/ppermute | solution.py:515
  15.2 2.4 %collective-permute-done.3.recv_ref = bf16[16,1664]{1,0:T(8,128)(2,1)S(1)} collective-permute-done((bf16[16,1664]{1,0:T(8,128)(2,1)S(1)}, bf16[16,1664]{1,0:T(8,128)(2,1)S(1)}, u32[]{:S(2)}, u32[]{:S(2)}) %collective-permute-start.3) | collective-permute-done | bytes 53280 | tf_op jit(solution)/shard_map/project/ppermute | solution.py:515
  17.8 1.6 %collective-permute-start.4 = (bf16[16,1536]{1,0:T(8,128)(2,1)S(1)}, bf16[16,1536]{1,0:T(8,128)(2,1)S(1)}, u32[]{:S(2)}, u32[]{:S(2)}) collective-permute-start(bf16[16,1536]{1,0:T(8,128)(2,1)S(1)} %project.7.refs_0_), channel_id=1, source_target_pairs={{0,12},{4,8},{8,4},{12,0},{16,28},{20,24},{24,20},{28,16},{1,13},{... | collective-permute-start | bytes 147464 | tf_op jit(solution)/shard_map/project/ppermute | solution.py:515
  19.7 1.7 %collective-permute-start.6 = (bf16[16,1536]{1,0:T(8,128)(2,1)S(1)}, bf16[16,1536]{1,0:T(8,128)(2,1)S(1)}, u32[]{:S(2)}, u32[]{:S(2)}) collective-permute-start(bf16[16,1536]{1,0:T(8,128)(2,1)S(1)} %project.7.refs_0_), channel_id=1, source_target_pairs={{0,4},{4,0},{8,12},{12,8},{16,20},{20,16},{24,28},{28,24},{1,5},{5... | collective-permute-start | bytes 147464 | tf_op jit(solution)/shard_map/project/ppermute | solution.py:515
  21.4 1.5 %collective-permute-done.4.refs_0_.refs_3_ = bf16[16,1536]{1,0:T(8,128)(2,1)S(1)} collective-permute-done((bf16[16,1536]{1,0:T(8,128)(2,1)S(1)}, bf16[16,1536]{1,0:T(8,128)(2,1)S(1)}, u32[]{:S(2)}, u32[]{:S(2)}) %collective-permute-start.4) | collective-permute-done | bytes 49184 | tf_op jit(solution)/shard_map/project/ppermute | solution.py:515
  24.0 1.6 %collective-permute-start.5 = (bf16[16,1152]{1,0:T(8,128)(2,1)S(1)}, bf16[16,1152]{1,0:T(8,128)(2,1)S(1)}, u32[]{:S(2)}, u32[]{:S(2)}) collective-permute-start(bf16[16,1152]{1,0:T(8,128)(2,1)S(1)} %attend.8), channel_id=1, source_target_pairs={{0,12},{4,8},{8,4},{12,0},{16,28},{20,24},{24,20},{28,16},{1,13},{... | collective-permute-start | bytes 110600 | tf_op jit(solution)/shard_map/attend/ppermute | solution.py:515
  26.8 1.5 %collective-permute-start.8 = (bf16[16,1152]{1,0:T(8,128)(2,1)S(1)}, bf16[16,1152]{1,0:T(8,128)(2,1)S(1)}, u32[]{:S(2)}, u32[]{:S(2)}) collective-permute-start(bf16[16,1152]{1,0:T(8,128)(2,1)S(1)} %get-tuple-element.58), channel_id=1, source_target_pairs={{0,4},{4,0},{8,12},{12,8},{16,20},{20,16},{24,28},{28,24},{1,5},{5... | collective-permute-start | bytes 110600 | tf_op jit(solution)/shard_map/attend/ppermute | solution.py:515
  32.5 3.1 %collective-permute-start.10 = (bf16[16,1152]{1,0:T(8,128)(2,1)S(1)}, bf16[16,1152]{1,0:T(8,128)(2,1)S(1)}, u32[]{:S(2)}, u32[]{:S(2)}) collective-permute-start(bf16[16,1152]{1,0:T(8,128)(2,1)S(1)} %get-tuple-element.62), channel_id=1, source_target_pairs={{0,16},{4,20},{8,24},{12,28},{16,0},{20,4},{24,8},{28,12},{1,17},{... | collective-permute-start | bytes 110600 | tf_op jit(solution)/shard_map/attend/ppermute | solution.py:515
  35.6 2.3 %attend.11 = (bf16[16,256,128]{2,1,0:T(8,128)(2,1)}, f32[16,128]{1,0:T(8,128)S(1)}) custom-call(s32[1]{0:T(128)} %bitcast.2.seq_ref, s32[16]{0:T(128)S(1)} %copy-done.4, bf16[16,1536]{1,0:T(8,128)(2,1)S(1)} %project.7.refs_0_, bf16[16,1536]{1,0:T(8,128)(2,1)S(1)} %collective-permute-done.6.refs_0_.refs_1_, ...), custom_call_target="tpu_custom_call" | custom-call | flops 3449999872 | bytes 1048576 | tf_op jit(solution)/shard_map/attend/pallas_call | solution.py:593
  40.2 1.5 %collective-permute-start.11 = (bf16[16,1024]{1,0:T(8,128)(2,1)S(1)}, bf16[16,1024]{1,0:T(8,128)(2,1)S(1)}, u32[]{:S(2)}, u32[]{:S(2)}) collective-permute-start(bf16[16,1024]{1,0:T(8,128)(2,1)S(1)} %get-tuple-element.64.a0_ref), channel_id=1, source_target_pairs={{0,4},{4,0},{8,12},{12,8},{16,20},{20,16},{24,28},{28,24},{1,5},{5... | collective-permute-start | bytes 98312 | tf_op jit(solution)/shard_map/attend/ppermute | solution.py:515
  41.7 2.3 %attend.13 = (bf16[16,256,128]{2,1,0:T(8,128)(2,1)}, f32[16,128]{1,0:T(8,128)S(1)}) custom-call(s32[1]{0:T(128)} %bitcast.2.seq_ref, s32[16]{0:T(128)S(1)} %copy-done.4, bf16[16,1536]{1,0:T(8,128)(2,1)S(1)} %project.7.refs_0_, bf16[16,1536]{1,0:T(8,128)(2,1)S(1)} %collective-permute-done.6.refs_0_.refs_1_, ...), custom_call_target="tpu_custom_call" | custom-call | flops 3449999872 | bytes 1048576 | tf_op jit(solution)/shard_map/attend/pallas_call | solution.py:593
  45.9 1.6 %collective-permute-start.15 = (bf16[32,640]{1,0:T(8,128)(2,1)S(1)}, bf16[32,640]{1,0:T(8,128)(2,1)S(1)}, u32[]{:S(2)}, u32[]{:S(2)}) collective-permute-start(bf16[32,640]{1,0:T(8,128)(2,1)S(1)} %mix.5.mine_ref), channel_id=1, source_target_pairs={{0,2},{1,3},{2,0},{3,1},{4,6},{5,7},{6,4},{7,5},{8,10},{9,11},{10,... | collective-permute-start | bytes 122888 | tf_op jit(solution)/shard_map/mix/ppermute | solution.py:515
  48.2 1.7 %collective-permute-done.15.recv_ref = bf16[32,640]{1,0:T(8,128)(2,1)S(1)} collective-permute-done((bf16[32,640]{1,0:T(8,128)(2,1)S(1)}, bf16[32,640]{1,0:T(8,128)(2,1)S(1)}, u32[]{:S(2)}, u32[]{:S(2)}) %collective-permute-start.15) | collective-permute-done | bytes 40992 | tf_op jit(solution)/shard_map/mix/ppermute | solution.py:515
  50.3 2.6 %collective-permute-start.16 = (bf16[1,32,768]{2,1,0:T(8,128)(2,1)S(1)}, bf16[1,32,768]{2,1,0:T(8,128)(2,1)S(1)}, u32[]{:S(2)}, u32[]{:S(2)}) collective-permute-start(bf16[1,32,768]{2,1,0:T(8,128)(2,1)S(1)} %get-tuple-element.70.refs_0_), channel_id=1, source_target_pairs={{0,16},{4,20},{8,24},{12,28},{16,0},{20,4},{24,8},{28,12},{1,17},{... | collective-permute-start | bytes 147464 | tf_op jit(solution)/shard_map/mix/ppermute | solution.py:515
  52.9 2.9 %collective-permute-done.16.refs_1_ = bf16[1,32,768]{2,1,0:T(8,128)(2,1)S(1)} collective-permute-done((bf16[1,32,768]{2,1,0:T(8,128)(2,1)S(1)}, bf16[1,32,768]{2,1,0:T(8,128)(2,1)S(1)}, u32[]{:S(2)}, u32[]{:S(2)}) %collective-permute-start.16) | collective-permute-done | bytes 49184 | tf_op jit(solution)/shard_map/mix/ppermute | solution.py:515
  57.3 2.2 %collective-permute-start.17 = (bf16[2,32,768]{2,1,0:T(8,128)(2,1)S(1)}, bf16[2,32,768]{2,1,0:T(8,128)(2,1)S(1)}, u32[]{:S(2)}, u32[]{:S(2)}) collective-permute-start(bf16[2,32,768]{2,1,0:T(8,128)(2,1)S(1)} %mix.7.own_ref), channel_id=1, source_target_pairs={{0,12},{4,8},{8,4},{12,0},{16,28},{20,24},{24,20},{28,16},{1,13},{... | collective-permute-start | bytes 294920 | tf_op jit(solution)/shard_map/ffn/ppermute | solution.py:515
  76.9 1.7 %collective-permute-done.27.refs_1_ = bf16[2,32,640]{2,1,0:T(8,128)(2,1)S(1)} collective-permute-done((bf16[2,32,640]{2,1,0:T(8,128)(2,1)S(1)}, bf16[2,32,640]{2,1,0:T(8,128)(2,1)S(1)}, u32[]{:S(2)}, u32[]{:S(2)}) %collective-permute-start.27) | collective-permute-done | bytes 81952 | tf_op jit(solution)/shard_map/ffn/ppermute | solution.py:515
  78.6 2.4 %collective-permute-start.30 = (bf16[1,32,640]{2,1,0:T(8,128)(2,1)S(1)}, bf16[1,32,640]{2,1,0:T(8,128)(2,1)S(1)}, u32[]{:S(2)}, u32[]{:S(2)}) collective-permute-start(bf16[1,32,640]{2,1,0:T(8,128)(2,1)S(1)} %get-tuple-element.94), channel_id=1, source_target_pairs={{0,16},{4,20},{8,24},{12,28},{16,0},{20,4},{24,8},{28,12},{1,17},{... | collective-permute-start | bytes 122888 | tf_op jit(solution)/shard_map/ffn/ppermute | solution.py:515
  81.0 2.6 %collective-permute-done.30.recv_ref = bf16[1,32,640]{2,1,0:T(8,128)(2,1)S(1)} collective-permute-done((bf16[1,32,640]{2,1,0:T(8,128)(2,1)S(1)}, bf16[1,32,640]{2,1,0:T(8,128)(2,1)S(1)}, u32[]{:S(2)}, u32[]{:S(2)}) %collective-permute-start.30) | collective-permute-done | bytes 40992 | tf_op jit(solution)/shard_map/ffn/ppermute | solution.py:515
  83.6 1.6 %collective-permute-start.31 = (bf16[1,32,640]{2,1,0:T(8,128)(2,1)S(1)}, bf16[1,32,640]{2,1,0:T(8,128)(2,1)S(1)}, u32[]{:S(2)}, u32[]{:S(2)}) collective-permute-start(bf16[1,32,640]{2,1,0:T(8,128)(2,1)S(1)} %ffn.29.mine_ref), channel_id=1, source_target_pairs={{0,2},{1,3},{2,0},{3,1},{4,6},{5,7},{6,4},{7,5},{8,10},{9,11},{10,... | collective-permute-start | bytes 122888 | tf_op jit(solution)/shard_map/ffn/ppermute | solution.py:515
  85.1 2.5 %collective-permute-done.31.recv_ref = bf16[1,32,640]{2,1,0:T(8,128)(2,1)S(1)} collective-permute-done((bf16[1,32,640]{2,1,0:T(8,128)(2,1)S(1)}, bf16[1,32,640]{2,1,0:T(8,128)(2,1)S(1)}, u32[]{:S(2)}, u32[]{:S(2)}) %collective-permute-start.31) | collective-permute-done | bytes 40992 | tf_op jit(solution)/shard_map/ffn/ppermute | solution.py:515
  (114 shorter events, 35.9 us)
Async XLA Ops:
  3.6 6.3 %collective-permute-start = (bf16[16,1664]{1,0:T(8,128)(2,1)}, bf16[16,1664]{1,0:T(8,128)(2,1)S(1)}, u32[]{:S(2)}, u32[]{:S(2)}) collective-permute-start(bf16[16,1664]{1,0:T(8,128)(2,1)} %get-tuple-element.51), channel_id=1, source_target_pairs={{0,12},{4,8},{8,4},{12,0},{16,28},{20,24},{24,20},{28,16},{1,13},{... | collective-permute-start | bytes 159752 | tf_op jit(solution)/shard_map/project/ppermute | solution.py:515
  7.6 4.3 %collective-permute-start.1 = (bf16[16,1664]{1,0:T(8,128)(2,1)}, bf16[16,1664]{1,0:T(8,128)(2,1)S(1)}, u32[]{:S(2)}, u32[]{:S(2)}) collective-permute-start(bf16[16,1664]{1,0:T(8,128)(2,1)} %get-tuple-element.52), channel_id=1, source_target_pairs={{0,8},{4,12},{8,0},{12,4},{16,24},{20,28},{24,16},{28,20},{1,9},{5... | collective-permute-start | bytes 159752 | tf_op jit(solution)/shard_map/project/ppermute | solution.py:515
  8.0 4.3 %collective-permute-start.2 = (bf16[16,1664]{1,0:T(8,128)(2,1)}, bf16[16,1664]{1,0:T(8,128)(2,1)S(1)}, u32[]{:S(2)}, u32[]{:S(2)}) collective-permute-start(bf16[16,1664]{1,0:T(8,128)(2,1)} %get-tuple-element.53), channel_id=1, source_target_pairs={{0,4},{4,0},{8,12},{12,8},{16,20},{20,16},{24,28},{28,24},{1,5},{5... | collective-permute-start | bytes 159752 | tf_op jit(solution)/shard_map/project/ppermute | solution.py:515
  12.5 5.1 %collective-permute-start.3 = (bf16[16,1664]{1,0:T(8,128)(2,1)S(1)}, bf16[16,1664]{1,0:T(8,128)(2,1)S(1)}, u32[]{:S(2)}, u32[]{:S(2)}) collective-permute-start(bf16[16,1664]{1,0:T(8,128)(2,1)S(1)} %get-tuple-element.55), channel_id=1, source_target_pairs={{0,16},{4,20},{8,24},{12,28},{16,0},{20,4},{24,8},{28,12},{1,17},{... | collective-permute-start | bytes 159752 | tf_op jit(solution)/shard_map/project/ppermute | solution.py:515
  17.8 5.1 %collective-permute-start.4 = (bf16[16,1536]{1,0:T(8,128)(2,1)S(1)}, bf16[16,1536]{1,0:T(8,128)(2,1)S(1)}, u32[]{:S(2)}, u32[]{:S(2)}) collective-permute-start(bf16[16,1536]{1,0:T(8,128)(2,1)S(1)} %project.7.refs_0_), channel_id=1, source_target_pairs={{0,12},{4,8},{8,4},{12,0},{16,28},{20,24},{24,20},{28,16},{1,13},{... | collective-permute-start | bytes 147464 | tf_op jit(solution)/shard_map/project/ppermute | solution.py:515
  19.5 6.1 %collective-permute-start.7 = (bf16[16,1536]{1,0:T(8,128)(2,1)S(1)}, bf16[16,1536]{1,0:T(8,128)(2,1)S(1)}, u32[]{:S(2)}, u32[]{:S(2)}) collective-permute-start(bf16[16,1536]{1,0:T(8,128)(2,1)S(1)} %project.7.refs_0_), channel_id=1, source_target_pairs={{0,8},{4,12},{8,0},{12,4},{16,24},{20,28},{24,16},{28,20},{1,9},{5... | collective-permute-start | bytes 147464 | tf_op jit(solution)/shard_map/project/ppermute | solution.py:515
  19.7 5.9 %collective-permute-start.6 = (bf16[16,1536]{1,0:T(8,128)(2,1)S(1)}, bf16[16,1536]{1,0:T(8,128)(2,1)S(1)}, u32[]{:S(2)}, u32[]{:S(2)}) collective-permute-start(bf16[16,1536]{1,0:T(8,128)(2,1)S(1)} %project.7.refs_0_), channel_id=1, source_target_pairs={{0,4},{4,0},{8,12},{12,8},{16,20},{20,16},{24,28},{28,24},{1,5},{5... | collective-permute-start | bytes 147464 | tf_op jit(solution)/shard_map/project/ppermute | solution.py:515
  24.0 5.8 %collective-permute-start.5 = (bf16[16,1152]{1,0:T(8,128)(2,1)S(1)}, bf16[16,1152]{1,0:T(8,128)(2,1)S(1)}, u32[]{:S(2)}, u32[]{:S(2)}) collective-permute-start(bf16[16,1152]{1,0:T(8,128)(2,1)S(1)} %attend.8), channel_id=1, source_target_pairs={{0,12},{4,8},{8,4},{12,0},{16,28},{20,24},{24,20},{28,16},{1,13},{... | collective-permute-start | bytes 110600 | tf_op jit(solution)/shard_map/attend/ppermute | solution.py:515
  26.8 4.0 %collective-permute-start.8 = (bf16[16,1152]{1,0:T(8,128)(2,1)S(1)}, bf16[16,1152]{1,0:T(8,128)(2,1)S(1)}, u32[]{:S(2)}, u32[]{:S(2)}) collective-permute-start(bf16[16,1152]{1,0:T(8,128)(2,1)S(1)} %get-tuple-element.58), channel_id=1, source_target_pairs={{0,4},{4,0},{8,12},{12,8},{16,20},{20,16},{24,28},{28,24},{1,5},{5... | collective-permute-start | bytes 110600 | tf_op jit(solution)/shard_map/attend/ppermute | solution.py:515
  28.3 4.0 %collective-permute-start.9 = (bf16[16,1152]{1,0:T(8,128)(2,1)S(1)}, bf16[16,1152]{1,0:T(8,128)(2,1)S(1)}, u32[]{:S(2)}, u32[]{:S(2)}) collective-permute-start(bf16[16,1152]{1,0:T(8,128)(2,1)S(1)} %get-tuple-element.59), channel_id=1, source_target_pairs={{0,8},{4,12},{8,0},{12,4},{16,24},{20,28},{24,16},{28,20},{1,9},{5... | collective-permute-start | bytes 110600 | tf_op jit(solution)/shard_map/attend/ppermute | solution.py:515
  32.5 5.4 %collective-permute-start.10 = (bf16[16,1152]{1,0:T(8,128)(2,1)S(1)}, bf16[16,1152]{1,0:T(8,128)(2,1)S(1)}, u32[]{:S(2)}, u32[]{:S(2)}) collective-permute-start(bf16[16,1152]{1,0:T(8,128)(2,1)S(1)} %get-tuple-element.62), channel_id=1, source_target_pairs={{0,16},{4,20},{8,24},{12,28},{16,0},{20,4},{24,8},{28,12},{1,17},{... | collective-permute-start | bytes 110600 | tf_op jit(solution)/shard_map/attend/ppermute | solution.py:515
  38.2 5.8 %collective-permute-start.13 = (bf16[16,1024]{1,0:T(8,128)(2,1)S(1)}, bf16[16,1024]{1,0:T(8,128)(2,1)S(1)}, u32[]{:S(2)}, u32[]{:S(2)}) collective-permute-start(bf16[16,1024]{1,0:T(8,128)(2,1)S(1)} %get-tuple-element.64.a0_ref), channel_id=1, source_target_pairs={{0,12},{4,8},{8,4},{12,0},{16,28},{20,24},{24,20},{28,16},{1,13},{... | collective-permute-start | bytes 98312 | tf_op jit(solution)/shard_map/attend/ppermute | solution.py:515
  38.9 5.1 %collective-permute-start.12 = (bf16[16,1024]{1,0:T(8,128)(2,1)S(1)}, bf16[16,1024]{1,0:T(8,128)(2,1)S(1)}, u32[]{:S(2)}, u32[]{:S(2)}) collective-permute-start(bf16[16,1024]{1,0:T(8,128)(2,1)S(1)} %get-tuple-element.64.a0_ref), channel_id=1, source_target_pairs={{0,8},{4,12},{8,0},{12,4},{16,24},{20,28},{24,16},{28,20},{1,9},{5... | collective-permute-start | bytes 98312 | tf_op jit(solution)/shard_map/attend/ppermute | solution.py:515
  40.2 3.9 %collective-permute-start.11 = (bf16[16,1024]{1,0:T(8,128)(2,1)S(1)}, bf16[16,1024]{1,0:T(8,128)(2,1)S(1)}, u32[]{:S(2)}, u32[]{:S(2)}) collective-permute-start(bf16[16,1024]{1,0:T(8,128)(2,1)S(1)} %get-tuple-element.64.a0_ref), channel_id=1, source_target_pairs={{0,4},{4,0},{8,12},{12,8},{16,20},{20,16},{24,28},{28,24},{1,5},{5... | collective-permute-start | bytes 98312 | tf_op jit(solution)/shard_map/attend/ppermute | solution.py:515
  45.9 4.1 %collective-permute-start.15 = (bf16[32,640]{1,0:T(8,128)(2,1)S(1)}, bf16[32,640]{1,0:T(8,128)(2,1)S(1)}, u32[]{:S(2)}, u32[]{:S(2)}) collective-permute-start(bf16[32,640]{1,0:T(8,128)(2,1)S(1)} %mix.5.mine_ref), channel_id=1, source_target_pairs={{0,2},{1,3},{2,0},{3,1},{4,6},{5,7},{6,4},{7,5},{8,10},{9,11},{10,... | collective-permute-start | bytes 122888 | tf_op jit(solution)/shard_map/mix/ppermute | solution.py:515
  50.3 5.6 %collective-permute-start.16 = (bf16[1,32,768]{2,1,0:T(8,128)(2,1)S(1)}, bf16[1,32,768]{2,1,0:T(8,128)(2,1)S(1)}, u32[]{:S(2)}, u32[]{:S(2)}) collective-permute-start(bf16[1,32,768]{2,1,0:T(8,128)(2,1)S(1)} %get-tuple-element.70.refs_0_), channel_id=1, source_target_pairs={{0,16},{4,20},{8,24},{12,28},{16,0},{20,4},{24,8},{28,12},{1,17},{... | collective-permute-start | bytes 147464 | tf_op jit(solution)/shard_map/mix/ppermute | solution.py:515
  56.0 7.0 %collective-permute-start.22 = (bf16[2,32,768]{2,1,0:T(8,128)(2,1)S(1)}, bf16[2,32,768]{2,1,0:T(8,128)(2,1)S(1)}, u32[]{:S(2)}, u32[]{:S(2)}) collective-permute-start(bf16[2,32,768]{2,1,0:T(8,128)(2,1)S(1)} %mix.7.own_ref), channel_id=1, source_target_pairs={{0,4},{4,0},{8,12},{12,8},{16,20},{20,16},{24,28},{28,24},{1,5},{5... | collective-permute-start | bytes 294920 | tf_op jit(solution)/shard_map/ffn/ppermute | solution.py:515
  57.2 5.6 %collective-permute-start.18 = (bf16[2,32,768]{2,1,0:T(8,128)(2,1)S(1)}, bf16[2,32,768]{2,1,0:T(8,128)(2,1)S(1)}, u32[]{:S(2)}, u32[]{:S(2)}) collective-permute-start(bf16[2,32,768]{2,1,0:T(8,128)(2,1)S(1)} %mix.7.own_ref), channel_id=1, source_target_pairs={{0,8},{4,12},{8,0},{12,4},{16,24},{20,28},{24,16},{28,20},{1,9},{5... | collective-permute-start | bytes 294920 | tf_op jit(solution)/shard_map/ffn/ppermute | solution.py:515
  57.3 8.4 %collective-permute-start.17 = (bf16[2,32,768]{2,1,0:T(8,128)(2,1)S(1)}, bf16[2,32,768]{2,1,0:T(8,128)(2,1)S(1)}, u32[]{:S(2)}, u32[]{:S(2)}) collective-permute-start(bf16[2,32,768]{2,1,0:T(8,128)(2,1)S(1)} %mix.7.own_ref), channel_id=1, source_target_pairs={{0,12},{4,8},{8,4},{12,0},{16,28},{20,24},{24,20},{28,16},{1,13},{... | collective-permute-start | bytes 294920 | tf_op jit(solution)/shard_map/ffn/ppermute | solution.py:515
  71.1 5.7 %collective-permute-start.26 = (bf16[2,32,640]{2,1,0:T(8,128)(2,1)S(1)}, bf16[2,32,640]{2,1,0:T(8,128)(2,1)S(1)}, u32[]{:S(2)}, u32[]{:S(2)}) collective-permute-start(bf16[2,32,640]{2,1,0:T(8,128)(2,1)S(1)} %ffn.24.refs_1_), channel_id=1, source_target_pairs={{0,12},{4,8},{8,4},{12,0},{16,28},{20,24},{24,20},{28,16},{1,13},{... | collective-permute-start | bytes 245768 | tf_op jit(solution)/shard_map/ffn/ppermute | solution.py:515
  73.2 5.4 %collective-permute-start.27 = (bf16[2,32,640]{2,1,0:T(8,128)(2,1)S(1)}, bf16[2,32,640]{2,1,0:T(8,128)(2,1)S(1)}, u32[]{:S(2)}, u32[]{:S(2)}) collective-permute-start(bf16[2,32,640]{2,1,0:T(8,128)(2,1)S(1)} %get-tuple-element.89.refs_2_), channel_id=1, source_target_pairs={{0,4},{4,0},{8,12},{12,8},{16,20},{20,16},{24,28},{28,24},{1,5},{5... | collective-permute-start | bytes 245768 | tf_op jit(solution)/shard_map/ffn/ppermute | solution.py:515
  74.0 4.5 %collective-permute-start.28 = (bf16[2,32,640]{2,1,0:T(8,128)(2,1)S(1)}, bf16[2,32,640]{2,1,0:T(8,128)(2,1)S(1)}, u32[]{:S(2)}, u32[]{:S(2)}) collective-permute-start(bf16[2,32,640]{2,1,0:T(8,128)(2,1)S(1)} %get-tuple-element.90.refs_3_), channel_id=1, source_target_pairs={{0,8},{4,12},{8,0},{12,4},{16,24},{20,28},{24,16},{28,20},{1,9},{5... | collective-permute-start | bytes 245768 | tf_op jit(solution)/shard_map/ffn/ppermute | solution.py:515
  78.6 5.0 %collective-permute-start.30 = (bf16[1,32,640]{2,1,0:T(8,128)(2,1)S(1)}, bf16[1,32,640]{2,1,0:T(8,128)(2,1)S(1)}, u32[]{:S(2)}, u32[]{:S(2)}) collective-permute-start(bf16[1,32,640]{2,1,0:T(8,128)(2,1)S(1)} %get-tuple-element.94), channel_id=1, source_target_pairs={{0,16},{4,20},{8,24},{12,28},{16,0},{20,4},{24,8},{28,12},{1,17},{... | collective-permute-start | bytes 122888 | tf_op jit(solution)/shard_map/ffn/ppermute | solution.py:515
  83.6 4.1 %collective-permute-start.31 = (bf16[1,32,640]{2,1,0:T(8,128)(2,1)S(1)}, bf16[1,32,640]{2,1,0:T(8,128)(2,1)S(1)}, u32[]{:S(2)}, u32[]{:S(2)}) collective-permute-start(bf16[1,32,640]{2,1,0:T(8,128)(2,1)S(1)} %ffn.29.mine_ref), channel_id=1, source_target_pairs={{0,2},{1,3},{2,0},{3,1},{4,6},{5,7},{6,4},{7,5},{8,10},{9,11},{10,... | collective-permute-start | bytes 122888 | tf_op jit(solution)/shard_map/ffn/ppermute | solution.py:515
  (24 other events, 129.7 us)
